TPU v7x, 32 devices: a whole 2x2x4 slice. The times are simulated.
32 devices in a mesh: fsdp: 4 (over y, x), ctx: 8 (over z, core).
Axes of the slice: x: 2, y: 2, z: 4, core: 2. Of those that a mesh axis runs over, the one named last changes fastest.
Arguments:
- tokens: bfloat16 [8, 1024, 2048], P('fsdp', 'ctx'), may hold values from -6 to 6
- cotangent: bfloat16 [8, 1024, 2048], P('fsdp', 'ctx'), may hold values from -6 to 6
- lengths: int32 [8], P('fsdp'), may hold values from 256 to 1024, as said below
- buckets: int32 [2047], replicated, may hold values from 0 to 31, as said below
- norm1_gain: float32 [2048], P(('fsdp', 'ctx')), may hold values from 0.25 to 1.75
- rel_bias: float32 [1024], P(('fsdp', 'ctx')), may hold values from -4 to 4
- w_query: float32 [2048, 2048], P(('fsdp', 'ctx')), may hold values from -0.0625 to 0.0625
- w_key: float32 [2048, 2048], P(('fsdp', 'ctx')), may hold values from -0.0625 to 0.0625
- w_value: float32 [2048, 2048], P(('fsdp', 'ctx')), may hold values from -0.125 to 0.125
- w_attn_out: float32 [2048, 2048], P(('fsdp', 'ctx')), may hold values from -0.5 to 0.5
- norm2_gain: float32 [2048], P(('fsdp', 'ctx')), may hold values from 0.25 to 1.75
- w_gate: float32 [2048, 5120], P(('fsdp', 'ctx')), may hold values from -0.125 to 0.125
- w_up: float32 [2048, 5120], P(('fsdp', 'ctx')), may hold values from -0.125 to 0.125
- w_down: float32 [5120, 2048], P(('fsdp', 'ctx')), may hold values from -0.078125 to 0.078125
Outputs:
- out: bfloat16 [8, 1024, 2048], P('fsdp', 'ctx')
- grad_tokens: bfloat16 [8, 1024, 2048], P('fsdp', 'ctx')
- grad_norm1_gain: float32 [2048], P(('fsdp', 'ctx'))
- grad_rel_bias: float32 [1024], P(('fsdp', 'ctx'))
- grad_w_query: float32 [2048, 2048], P(('fsdp', 'ctx'))
- grad_w_key: float32 [2048, 2048], P(('fsdp', 'ctx'))
- grad_w_value: float32 [2048, 2048], P(('fsdp', 'ctx'))
- grad_w_attn_out: float32 [2048, 2048], P(('fsdp', 'ctx'))
- grad_norm2_gain: float32 [2048], P(('fsdp', 'ctx'))
- grad_w_gate: float32 [2048, 5120], P(('fsdp', 'ctx'))
- grad_w_up: float32 [2048, 5120], P(('fsdp', 'ctx'))
- grad_w_down: float32 [5120, 2048], P(('fsdp', 'ctx'))
Inputs may be any that keep to these rules, and one draw needn't show every extreme that they name: `lengths`: of the 2 sequences of one fsdp index, one has all 1024 slots valid. `buckets`: entry r + 1023 is the bucket of r = key slot minus query slot: 0 for r = 0, -r for -8 < r < 0, 16 + r for 0 < r < 8; for |r| >= 8 it does not fall as |r| grows and lies in 8 to 15 for negative r, 24 to 31 for positive r.
All inputs are finite; a program needn't handle non-finite values.
Results may differ from a plain program's by a relative error of at most 0.018.
The roundings to bfloat16 on the way count: a program that leaves them out, or rounds other values in their place, can miss the bound.
Values may be sent and summed in bfloat16 or wider, within the bound.
A program may use at most 512 MiB of HBM per device.

v0:
```python
import math

import jax
import jax.numpy as jnp
from jax import lax
from jax.sharding import PartitionSpec as P

H = 32
NB = 32


EPSILON = 1e-06
MASKED = -1e30
HIGHEST = lax.Precision.HIGHEST


def rms_scale(values):
    return lax.rsqrt(jnp.mean(values * values, axis=1, keepdims=True) + EPSILON)


def norm_back(grad_normed, values, row_scale, gain_row):
    weighted = grad_normed * gain_row
    inner_mean = jnp.mean(weighted * values, axis=1, keepdims=True)
    return row_scale * (weighted - values * row_scale * row_scale * inner_mean)


def gelu_tanh(values):
    return jax.nn.gelu(values, approximate=True)


def unpack_weights(gathered):
    (
        gain_one,
        bias_flat,
        query_weight,
        key_weight,
        value_weight,
        attn_weight,
        gain_two,
        gate_weight,
        up_weight,
        down_weight,
    ) = gathered
    bias_table = bias_flat.reshape(H, NB)
    return (
        gain_one.astype(jnp.float32),
        bias_table,
        query_weight,
        key_weight,
        value_weight,
        attn_weight,
        gain_two.astype(jnp.float32),
        gate_weight,
        up_weight,
        down_weight,
    )


def block_scores(query_seq, keys_seq, key_start, query_pos, valid_len, offset_bias, span_len):
    total_len = keys_seq.shape[0]
    key_pos = key_start + jnp.arange(span_len, dtype=jnp.int32)
    offset = key_pos[None, :] - query_pos[:, None] + (total_len - 1)
    pair_bias = jnp.take(offset_bias, offset, axis=1)
    scores = (
        jnp.einsum("ihd,jhd->hij", query_seq, keys_seq, preferred_element_type=jnp.float32)
        + pair_bias
    )
    scores = jnp.where((key_pos < valid_len)[None, None, :], scores, MASKED)
    return (scores, offset)


def attend(query_seq, keys_seq, values_seq, query_pos, valid_len, offset_bias, span_len):
    total_len = keys_seq.shape[0]
    row_count, head_count, head_dim = query_seq.shape
    starts = jnp.arange(total_len // span_len, dtype=jnp.int32) * span_len

    def mass_step(running, key_start):
        row_peak, row_mass = running
        scores, unused = block_scores(
            query_seq, keys_seq, key_start, query_pos, valid_len, offset_bias, span_len
        )
        new_peak = jnp.maximum(row_peak, jnp.max(scores, axis=2))
        row_mass = row_mass * jnp.exp(row_peak - new_peak) + jnp.sum(
            jnp.exp(scores - new_peak[:, :, None]), axis=2
        )
        return ((new_peak, row_mass), None)

    start_peak = jnp.full((head_count, row_count), MASKED, jnp.float32)
    start_mass = jnp.zeros((head_count, row_count), jnp.float32)
    (row_peak, row_mass), unused = lax.scan(mass_step, (start_peak, start_mass), starts)
    log_mass = row_peak + jnp.log(row_mass)

    def value_step(running, key_start):
        summed, exact = running
        scores, unused = block_scores(
            query_seq, keys_seq, key_start, query_pos, valid_len, offset_bias, span_len
        )
        weights = jnp.exp(scores - log_mass[:, :, None])
        summed = summed + jnp.einsum(
            "hij,jhd->ihd",
            weights.astype(jnp.bfloat16),
            values_seq,
            preferred_element_type=jnp.float32,
        )
        exact = exact + jnp.einsum(
            "hij,jhd->ihd", weights, values_seq.astype(jnp.float32), precision=HIGHEST
        )
        return ((summed, exact), None)

    start_rows = jnp.zeros((row_count, head_count, head_dim), jnp.float32)
    (summed, exact), unused = lax.scan(value_step, (start_rows, start_rows), starts)
    return (summed.astype(jnp.bfloat16), log_mass, exact)


def attend_back(
    query_seq,
    keys_seq,
    values_seq,
    grad_seq,
    log_mass,
    exact_out,
    query_pos,
    valid_len,
    buckets,
    offset_bias,
    bias_shape,
    span_len,
):
    total_len = keys_seq.shape[0]
    row_count, head_count, head_dim = query_seq.shape
    starts = jnp.arange(total_len // span_len, dtype=jnp.int32) * span_len
    row_delta = jnp.sum(grad_seq.astype(jnp.float32) * exact_out, axis=2).T
    bucket_ids = jnp.arange(bias_shape[1], dtype=jnp.int32)

    def grad_step(running, key_start):
        grad_query, grad_bias = running
        scores, offset = block_scores(
            query_seq, keys_seq, key_start, query_pos, valid_len, offset_bias, span_len
        )
        weights = jnp.exp(scores - log_mass[:, :, None])
        grad_weights = jnp.einsum(
            "ihd,jhd->hij", grad_seq, values_seq, preferred_element_type=jnp.float32
        )
        grad_scores = (weights * (grad_weights - row_delta[:, :, None])).astype(jnp.bfloat16)
        bucket = jnp.take(buckets, offset, axis=0)
        one_hot = (bucket[:, :, None] == bucket_ids[None, None, :]).astype(jnp.bfloat16)
        grad_query = grad_query + jnp.einsum(
            "hij,jhd->ihd", grad_scores, keys_seq, preferred_element_type=jnp.float32
        )
        grad_bias = grad_bias + jnp.einsum(
            "hij,ijn->hn", grad_scores, one_hot, preferred_element_type=jnp.float32
        )
        grad_key = jnp.einsum(
            "hij,ihd->jhd", grad_scores, query_seq, preferred_element_type=jnp.float32
        )
        grad_value = jnp.einsum(
            "hij,ihd->jhd",
            weights.astype(jnp.bfloat16),
            grad_seq,
            preferred_element_type=jnp.float32,
        )
        return ((grad_query, grad_bias), (grad_key, grad_value))

    start_query = jnp.zeros((row_count, head_count, head_dim), jnp.float32)
    start_bias = jnp.zeros(bias_shape, jnp.float32)
    (grad_query, grad_bias), (key_blocks, value_blocks) = lax.scan(
        grad_step, (start_query, start_bias), starts
    )
    return (
        grad_query,
        key_blocks.reshape(total_len, -1),
        value_blocks.reshape(total_len, -1),
        grad_bias,
    )


def shards(
    tokens,
    cotangent,
    lengths,
    buckets,
    norm1_gain,
    rel_bias,
    w_query,
    w_key,
    w_value,
    w_attn_out,
    norm2_gain,
    w_gate,
    w_up,
    w_down,
):
    num_seqs, block_len, model_width = tokens.shape
    row_count = num_seqs * block_len
    total_len = block_len * lax.axis_size("ctx")
    span_len = math.gcd(2048, total_len)
    query_pos = lax.axis_index("ctx") * block_len + jnp.arange(block_len, dtype=jnp.int32)
    valid_rows = (query_pos[None, :] < lengths[:, None]).astype(jnp.float32).reshape(row_count, 1)
    gathered = (
        lax.all_gather(norm1_gain.astype(jnp.bfloat16), ("fsdp", "ctx"), axis=0, tiled=True),
        lax.all_gather(rel_bias.astype(jnp.bfloat16), ("fsdp", "ctx"), axis=0, tiled=True),
        lax.all_gather(w_query.astype(jnp.bfloat16), ("fsdp", "ctx"), axis=0, tiled=True),
        lax.all_gather(w_key.astype(jnp.bfloat16), ("fsdp", "ctx"), axis=0, tiled=True),
        lax.all_gather(w_value.astype(jnp.bfloat16), ("fsdp", "ctx"), axis=0, tiled=True),
        lax.all_gather(w_attn_out.astype(jnp.bfloat16), ("fsdp", "ctx"), axis=0, tiled=True),
        lax.all_gather(norm2_gain.astype(jnp.bfloat16), ("fsdp", "ctx"), axis=0, tiled=True),
        lax.all_gather(w_gate.astype(jnp.bfloat16), ("fsdp", "ctx"), axis=0, tiled=True),
        lax.all_gather(w_up.astype(jnp.bfloat16), ("fsdp", "ctx"), axis=0, tiled=True),
        lax.all_gather(w_down.astype(jnp.bfloat16), ("fsdp", "ctx"), axis=0, tiled=True),
    )
    (
        gain_one,
        bias_table,
        query_weight,
        key_weight,
        value_weight,
        attn_weight,
        gain_two,
        gate_weight,
        up_weight,
        down_weight,
    ) = unpack_weights(gathered)
    head_dim = query_weight.shape[1] // H
    offset_bias = jnp.take(bias_table.astype(jnp.float32), buckets, axis=1)
    inputs = tokens.reshape(row_count, model_width).astype(jnp.float32)
    scale_one = rms_scale(inputs)
    normed = (inputs * scale_one * gain_one).astype(jnp.bfloat16)
    query_rows = jnp.dot(normed, query_weight, preferred_element_type=jnp.float32).astype(
        jnp.bfloat16
    )
    key_rows = jnp.dot(normed, key_weight, preferred_element_type=jnp.float32).astype(jnp.bfloat16)
    value_rows = jnp.dot(normed, value_weight, preferred_element_type=jnp.float32).astype(
        jnp.bfloat16
    )
    keys_all, values_all = (
        lax.all_gather(key_rows.reshape(num_seqs, block_len, -1), "ctx", axis=1, tiled=True),
        lax.all_gather(value_rows.reshape(num_seqs, block_len, -1), "ctx", axis=1, tiled=True),
    )
    query_heads = query_rows.reshape(num_seqs, block_len, H, head_dim)
    attended_list = []
    log_masses = []
    exact_list = []
    for seq_index in range(num_seqs):
        attended_seq, log_mass, exact_out = attend(
            query_heads[seq_index],
            keys_all[seq_index].reshape(total_len, H, head_dim),
            values_all[seq_index].reshape(total_len, H, head_dim),
            query_pos,
            lengths[seq_index],
            offset_bias,
            span_len,
        )
        attended_list.append(attended_seq)
        log_masses.append(log_mass)
        exact_list.append(exact_out)
    attended = jnp.stack(attended_list).reshape(row_count, -1)
    hidden_one = inputs + jnp.dot(attended, attn_weight, preferred_element_type=jnp.float32)
    scale_two = rms_scale(hidden_one)
    normed_two = (hidden_one * scale_two * gain_two).astype(jnp.bfloat16)
    gate_act = jnp.dot(normed_two, gate_weight, preferred_element_type=jnp.float32)
    upward = jnp.dot(normed_two, up_weight, preferred_element_type=jnp.float32)
    activated, gelu_pull = jax.vjp(gelu_tanh, gate_act)
    hidden_ff = (activated * upward).astype(jnp.bfloat16)
    result = hidden_one + jnp.dot(hidden_ff, down_weight, preferred_element_type=jnp.float32)
    output = (result * valid_rows).astype(jnp.bfloat16).reshape(num_seqs, block_len, model_width)
    gathered = (
        lax.all_gather(norm1_gain.astype(jnp.bfloat16), ("fsdp", "ctx"), axis=0, tiled=True),
        lax.all_gather(rel_bias.astype(jnp.bfloat16), ("fsdp", "ctx"), axis=0, tiled=True),
        lax.all_gather(w_query.astype(jnp.bfloat16), ("fsdp", "ctx"), axis=0, tiled=True),
        lax.all_gather(w_key.astype(jnp.bfloat16), ("fsdp", "ctx"), axis=0, tiled=True),
        lax.all_gather(w_value.astype(jnp.bfloat16), ("fsdp", "ctx"), axis=0, tiled=True),
        lax.all_gather(w_attn_out.astype(jnp.bfloat16), ("fsdp", "ctx"), axis=0, tiled=True),
        lax.all_gather(norm2_gain.astype(jnp.bfloat16), ("fsdp", "ctx"), axis=0, tiled=True),
        lax.all_gather(w_gate.astype(jnp.bfloat16), ("fsdp", "ctx"), axis=0, tiled=True),
        lax.all_gather(w_up.astype(jnp.bfloat16), ("fsdp", "ctx"), axis=0, tiled=True),
        lax.all_gather(w_down.astype(jnp.bfloat16), ("fsdp", "ctx"), axis=0, tiled=True),
    )
    (
        gain_one,
        bias_table,
        query_weight,
        key_weight,
        value_weight,
        attn_weight,
        gain_two,
        gate_weight,
        up_weight,
        down_weight,
    ) = unpack_weights(gathered)
    offset_bias = jnp.take(bias_table.astype(jnp.float32), buckets, axis=1)
    keys_all, values_all = (
        lax.all_gather(key_rows.reshape(num_seqs, block_len, -1), "ctx", axis=1, tiled=True),
        lax.all_gather(value_rows.reshape(num_seqs, block_len, -1), "ctx", axis=1, tiled=True),
    )
    grad_rows = cotangent.reshape(row_count, model_width).astype(jnp.float32) * valid_rows
    grad_branch = grad_rows.astype(jnp.bfloat16)
    grad_down = jnp.einsum("rf,rd->fd", hidden_ff, grad_branch, preferred_element_type=jnp.float32)
    grad_hidden = jnp.einsum(
        "rd,fd->rf", grad_branch, down_weight, preferred_element_type=jnp.float32
    )
    grad_gate = gelu_pull(grad_hidden * upward)[0].astype(jnp.bfloat16)
    grad_upward = (grad_hidden * activated).astype(jnp.bfloat16)
    grad_gate_weight = jnp.einsum(
        "rd,rf->df", normed_two, grad_gate, preferred_element_type=jnp.float32
    )
    grad_up_weight = jnp.einsum(
        "rd,rf->df", normed_two, grad_upward, preferred_element_type=jnp.float32
    )
    grad_normed_two = jnp.einsum(
        "rf,df->rd", grad_gate, gate_weight, preferred_element_type=jnp.float32
    ) + jnp.einsum("rf,df->rd", grad_upward, up_weight, preferred_element_type=jnp.float32)
    grad_gain_two = jnp.sum(grad_normed_two * hidden_one * scale_two, axis=0)
    grad_hidden_one = grad_rows + norm_back(grad_normed_two, hidden_one, scale_two, gain_two)
    ffn_part = (
        lax.psum_scatter(grad_gain_two, ("fsdp", "ctx"), scatter_dimension=0, tiled=True),
        lax.psum_scatter(grad_gate_weight, ("fsdp", "ctx"), scatter_dimension=0, tiled=True),
        lax.psum_scatter(grad_up_weight, ("fsdp", "ctx"), scatter_dimension=0, tiled=True),
        lax.psum_scatter(grad_down, ("fsdp", "ctx"), scatter_dimension=0, tiled=True),
    )
    grad_attn_branch = grad_hidden_one.astype(jnp.bfloat16)
    grad_attn_weight = jnp.einsum(
        "rk,rd->kd", attended, grad_attn_branch, preferred_element_type=jnp.float32
    )
    grad_attended = jnp.einsum(
        "rd,kd->rk", grad_attn_branch, attn_weight, preferred_element_type=jnp.float32
    ).astype(jnp.bfloat16)
    grad_heads = grad_attended.reshape(num_seqs, block_len, H, head_dim)
    grad_query_list = []
    grad_key_list = []
    grad_value_list = []
    grad_bias_total = jnp.zeros(bias_table.shape, jnp.float32)
    for seq_index in range(num_seqs):
        grad_query_seq, grad_key_seq, grad_value_seq, grad_bias_seq = attend_back(
            query_heads[seq_index],
            keys_all[seq_index].reshape(total_len, H, head_dim),
            values_all[seq_index].reshape(total_len, H, head_dim),
            grad_heads[seq_index],
            log_masses[seq_index],
            exact_list[seq_index],
            query_pos,
            lengths[seq_index],
            buckets,
            offset_bias,
            bias_table.shape,
            span_len,
        )
        grad_query_list.append(grad_query_seq)
        grad_key_list.append(grad_key_seq)
        grad_value_list.append(grad_value_seq)
        grad_bias_total = grad_bias_total + grad_bias_seq
    grad_query_rows = jnp.stack(grad_query_list).reshape(row_count, -1).astype(jnp.bfloat16)
    key_sums, value_sums = (
        lax.psum_scatter(
            jnp.stack(grad_key_list).astype(jnp.bfloat16), "ctx", scatter_dimension=1, tiled=True
        ).astype(jnp.float32),
        lax.psum_scatter(
            jnp.stack(grad_value_list).astype(jnp.bfloat16), "ctx", scatter_dimension=1, tiled=True
        ).astype(jnp.float32),
    )
    grad_key_rows = key_sums.reshape(row_count, -1).astype(jnp.bfloat16)
    grad_value_rows = value_sums.reshape(row_count, -1).astype(jnp.bfloat16)
    grad_query_weight = jnp.einsum(
        "rd,rk->dk", normed, grad_query_rows, preferred_element_type=jnp.float32
    )
    grad_key_weight = jnp.einsum(
        "rd,rk->dk", normed, grad_key_rows, preferred_element_type=jnp.float32
    )
    grad_value_weight = jnp.einsum(
        "rd,rk->dk", normed, grad_value_rows, preferred_element_type=jnp.float32
    )
    grad_normed = jnp.einsum(
        "rk,dk->rd", grad_query_rows, query_weight, preferred_element_type=jnp.float32
    )
    grad_normed = grad_normed + jnp.einsum(
        "rk,dk->rd", grad_key_rows, key_weight, preferred_element_type=jnp.float32
    )
    grad_normed = grad_normed + jnp.einsum(
        "rk,dk->rd", grad_value_rows, value_weight, preferred_element_type=jnp.float32
    )
    grad_gain_one = jnp.sum(grad_normed * inputs * scale_one, axis=0)
    grad_inputs = grad_hidden_one + norm_back(grad_normed, inputs, scale_one, gain_one)
    attn_part = (
        lax.psum_scatter(grad_gain_one, ("fsdp", "ctx"), scatter_dimension=0, tiled=True),
        lax.psum_scatter(
            grad_bias_total.reshape(-1), ("fsdp", "ctx"), scatter_dimension=0, tiled=True
        ),
        lax.psum_scatter(grad_query_weight, ("fsdp", "ctx"), scatter_dimension=0, tiled=True),
        lax.psum_scatter(grad_key_weight, ("fsdp", "ctx"), scatter_dimension=0, tiled=True),
        lax.psum_scatter(grad_value_weight, ("fsdp", "ctx"), scatter_dimension=0, tiled=True),
        lax.psum_scatter(grad_attn_weight, ("fsdp", "ctx"), scatter_dimension=0, tiled=True),
    )
    grad_tokens = grad_inputs.astype(jnp.bfloat16).reshape(num_seqs, block_len, model_width)
    return (
        output,
        grad_tokens,
        attn_part[0],
        attn_part[1],
        attn_part[2],
        attn_part[3],
        attn_part[4],
        attn_part[5],
        ffn_part[0],
        ffn_part[1],
        ffn_part[2],
        ffn_part[3],
    )


def solution(mesh):
    in_specs = (
        P("fsdp", "ctx", None),
        P("fsdp", "ctx", None),
        P("fsdp"),
        P(),
        P(("fsdp", "ctx")),
        P(("fsdp", "ctx")),
        P(("fsdp", "ctx"), None),
        P(("fsdp", "ctx"), None),
        P(("fsdp", "ctx"), None),
        P(("fsdp", "ctx"), None),
        P(("fsdp", "ctx")),
        P(("fsdp", "ctx"), None),
        P(("fsdp", "ctx"), None),
        P(("fsdp", "ctx"), None),
    )
    out_specs = (
        P("fsdp", "ctx", None),
        P("fsdp", "ctx", None),
        P(("fsdp", "ctx")),
        P(("fsdp", "ctx")),
        P(("fsdp", "ctx"), None),
        P(("fsdp", "ctx"), None),
        P(("fsdp", "ctx"), None),
        P(("fsdp", "ctx"), None),
        P(("fsdp", "ctx")),
        P(("fsdp", "ctx"), None),
        P(("fsdp", "ctx"), None),
        P(("fsdp", "ctx"), None),
    )
    return jax.shard_map(shards, mesh=mesh, in_specs=in_specs, out_specs=out_specs, check_vma=False)
```

profile of v0, /device:TPU:22, one launch (start us, length us, event | category | flops | bytes accessed | tf_op | source)
XLA Modules:
  0.0 3330.1 jit_solution(7980746905534743047)
XLA Ops:
  15.3 40.4 %all-reduce.7 = (bf16[2048]{0:T(1024)(128)(2,1)S(1)}, bf16[1024]{0:T(1024)(128)(2,1)S(1)}, bf16[2048]{0:T(1024)(128)(2,1)S(1)}) all-reduce(bf16[2048]{0:T(1024)(128)(2,1)S(1)} %dynamic-update-slice, bf16[1024]{0:T(1024)(128)(2,1)S(1)} %dynamic-update-slice.1, ...), channel_id=1, replica_groups=mesh['fsdp'=4,'ctx'=8] {'fsdp','ctx'}, use_global_device_ids=true, to_apply=%add | all-reduce | flops 5120 | bytes 20480
  60.0 28.6 all-gather.10.cloned.1.call-done
  88.6 6.7 convolution_convert_fusion.7
  95.5 72.8 %all-gather.16.cloned.1.call-done = bf16[2048,2048]{1,0:T(8,128)(2,1)} async-done(((bf16[64,2048]{1,0:T(8,128)(2,1)}), bf16[2048,2048]{1,0:T(8,128)(2,1)}) %all-gather.16.cloned.1.call-update) | async-done | bytes 8388624 | tf_op jit(solution)/shard_map/all_gather | solution.py:203
  168.2 6.7 convolution_convert_fusion.5
  180.8 5.5 gather_fusion
  186.7 433.3 %gather_fusion.1 = f32[131072,32]{1,0:T(8,128)} fusion(f32[32,2047]{0,1:T(8,128)S(1)} %select_bitcast_fusion, s32[131072]{0:T(1024)S(1)} %broadcast_clamp_fusion), kind=kCustom, calls=%fused_computation.1.clone | custom fusion | bytes 34078720 | tf_op jit(solution)/shard_map/while/body/eval_jaxpr/jit(_take)/gather | solution.py:63
  620.0 43.5 %copy.91 = f32[128,1024,32]{1,0,2:T(8,128)} copy(f32[128,1024,32]{2,1,0:T(8,128)} %bitcast.9) | data formatting | bytes 33554432 | tf_op jit(solution)/shard_map/while/body/eval_jaxpr/jit(_take)/gather | solution.py:63
  667.0 5.7 convolution_convert_fusion.6
  673.5 6.3 fusion.92
  679.7 6.4 copy.74
  686.2 6.1 fusion.91
  692.3 6.4 copy.76
  698.7 6.5 copy.69
  705.2 6.4 copy.71
  711.6 17.1 fusion.96
  728.7 11.8 fusion.97
  740.5 8.1 exponential_reduce_fusion
  751.8 3.8 exponential_reduce_fusion.1
  755.7 8.7 fusion.55
  764.4 7.6 fusion.58
  773.3 6.7 multiply_reduce_fusion.2
  781.6 12.7 fusion.98
  794.3 12.9 fusion.99
  807.2 92.2 %all-gather.26.cloned.1.call-done = bf16[5120,2048]{1,0:T(8,128)(2,1)} async-done(((bf16[160,2048]{1,0:T(8,128)(2,1)}), bf16[5120,2048]{1,0:T(8,128)(2,1)}) %all-gather.26.cloned.1.call-update) | async-done | bytes 20971536 | tf_op jit(solution)/shard_map/all_gather | solution.py:209
  899.5 23.7 multiply_convert_fusion.2
  923.2 12.3 fusion.100
  935.5 12.4 multiply_reduce_fusion
  950.5 6.5 convolution_convert_fusion.4
  958.2 18.4 fusion.61
  976.6 11.3 multiply_convert_fusion
  989.2 18.2 fusion.62
  1007.5 11.7 multiply_convert_fusion.1
  1019.2 6.6 convolution_convert_fusion.2
  1025.8 6.5 copy.82
  1032.3 6.8 convolution_convert_fusion.3
  1039.1 6.5 copy.81
  1045.6 7.5 pad_maximum_fusion
  1053.2 8.9 convolution_convert_fusion
  1062.1 6.5 copy.84
  1068.6 8.9 convolution_convert_fusion.1
  1077.5 6.5 copy.83
  1084.0 7.6 pad_maximum_fusion.1
  1093.2 8.3 convolution_bitcast_fusion.2
  1106.9 8.2 fusion.72
  1116.4 8.2 fusion.76
  1124.8 15.5 reduce-scatter.10.cloned.1.call-done
  1140.3 9.7 convolution_bitcast_fusion.1
  1150.1 80.5 %reduce-scatter.12.cloned.1.call-done = bf16[2,128,2048]{2,1,0:T(8,128)(2,1)} async-done(((bf16[2,1024,2048]{2,1,0:T(8,128)(2,1)}), bf16[2,128,2048]{2,1,0:T(8,128)(2,1)}) %reduce-scatter.12.cloned.1.call-update) | async-done | bytes 1048592 | tf_op jit(solution)/shard_map/reduce_scatter | solution.py:356
  1230.6 9.5 convolution_bitcast_fusion
  1241.4 18.4 fusion.101
  1259.9 18.5 fusion.102
  1280.2 17.9 fusion.103
  1299.2 725.3 %gather_fusion.2 = s32[131072]{0:T(1024)S(1)} fusion(s32[2047]{0:T(1024)S(1)} %copy-done.1, s32[131072]{0:T(1024)S(1)} %copy-done.25), kind=kCustom, calls=%fused_computation.2.clone | custom fusion | bytes 1572864 | tf_op jit(solution)/shard_map/while/body/eval_jaxpr/jit(_take)/gather | solution.py:145
  2025.0 13.7 fusion.63
  2038.7 10.3 fusion.69
  2049.1 6.0 fusion.74
  2055.1 11.7 fusion.22
  2066.8 5.9 convolution_add_fusion.3
  2072.8 4.3 fusion.44
  2077.1 43.0 %all-reduce.6 = (f32[2048]{0:T(1024)S(1)}, f32[1024]{0:T(1024)S(1)}, f32[2048]{0:T(1024)S(1)}) all-reduce(f32[2048]{0:T(1024)S(1)} %get-tuple-element.157, f32[1024]{0:T(1024)S(1)} %reshape.233, f32[2048]{0:T(1024)S(1)} %copy-done.52), channel_id=4, replica_groups=mesh['fsdp'=4,'ctx'=8] {'fsdp','ctx'}, use_global_device_ids=true, to_apply=%region_13.16.clone | all-reduce | flops 5120 | bytes 40960
  2125.2 302.6 %reduce-scatter.22.cloned.1.call-done = f32[64,5120]{1,0:T(8,128)} async-done(((f32[2048,5120]{1,0:T(8,128)}), f32[64,5120]{1,0:T(8,128)}) %reduce-scatter.22.cloned.1.call-update) | async-done | bytes 1310736 | tf_op jit(solution)/shard_map/reduce_scatter | solution.py:316
  2427.8 447.6 %reduce-scatter.24.cloned.1.call-done = f32[64,5120]{1,0:T(8,128)} async-done(((f32[2048,5120]{1,0:T(8,128)}), f32[64,5120]{1,0:T(8,128)}) %reduce-scatter.24.cloned.1.call-update) | async-done | bytes 1310736 | tf_op jit(solution)/shard_map/reduce_scatter | solution.py:317
  2875.4 447.6 %reduce-scatter.26.cloned.1.call-done = f32[160,2048]{1,0:T(8,128)} async-done(((f32[5120,2048]{1,0:T(8,128)}), f32[160,2048]{1,0:T(8,128)}) %reduce-scatter.26.cloned.1.call-update) | async-done | bytes 1310736 | tf_op jit(solution)/shard_map/reduce_scatter | solution.py:318
  (236 shorter events, 51.8 us)
Async XLA Ops:
  7.2 81.5 %all-gather.10.cloned.1.call-start = ((), (), s32[]{:S(2)}) async-start(), calls=%async_computation.9 | async-start | bytes 8650752 | tf_op jit(solution)/shard_map/all_gather | solution.py:204
  9.0 159.2 %all-gather.16.cloned.1.call-start = ((), (), s32[]{:S(2)}) async-start(), calls=%async_computation.12 | async-start | bytes 8650752 | tf_op jit(solution)/shard_map/all_gather | solution.py:203
  10.9 656.1 %all-gather.14.cloned.1.call-start = ((), (), s32[]{:S(2)}) async-start(), calls=%async_computation.11 | async-start | bytes 8650752 | tf_op jit(solution)/shard_map/all_gather | solution.py:202
  12.7 660.7 %all-gather.12.cloned.1.call-start = ((), (), s32[]{:S(2)}) async-start(), calls=%async_computation.10 | async-start | bytes 9437184 | tf_op jit(solution)/shard_map/all_gather | solution.py:237
  60.0 108.2 %copy-start.39 = (bf16[256,2048]{1,0:T(8,128)(2,1)}, bf16[256,2048]{1,0:T(8,128)(2,1)S(1)}, u32[]{:S(2)}) copy-start(bf16[256,2048]{1,0:T(8,128)(2,1)S(1)} %fusion.33) | copy-start | bytes 3145732
  95.4 79.7 %copy-start.41 = (f32[64,2048]{1,0:T(8,128)S(1)}, f32[64,2048]{1,0:T(8,128)}, u32[]{:S(2)}) copy-start(f32[64,2048]{1,0:T(8,128)} %param.29) | copy-start | bytes 1572868
  95.4 80.5 %copy-start.35 = (f32[64,5120]{1,0:T(8,128)S(1)}, f32[64,5120]{1,0:T(8,128)}, u32[]{:S(2)}) copy-start(f32[64,5120]{1,0:T(8,128)} %param.31) | copy-start | bytes 3932164
  95.4 590.8 %all-gather.18.cloned.1.call-start = ((), (), s32[]{:S(2)}) async-start(), calls=%async_computation.13 | async-start | bytes 9437184 | tf_op jit(solution)/shard_map/all_gather | solution.py:236
  175.0 5.8 copy-start
  175.0 598.3 %all-gather.20.cloned.1.call-start = ((), (), s32[]{:S(2)}) async-start(), calls=%async_computation.14 | async-start | bytes 8650752 | tf_op jit(solution)/shard_map/all_gather | solution.py:205
  175.8 605.8 %all-gather.22.cloned.1.call-start = ((), (), s32[]{:S(2)}) async-start(), calls=%async_computation.15 | async-start | bytes 21626880 | tf_op jit(solution)/shard_map/all_gather | solution.py:207
  176.8 617.6 %all-gather.24.cloned.1.call-start = ((), (), s32[]{:S(2)}) async-start(), calls=%async_computation.16 | async-start | bytes 21626880 | tf_op jit(solution)/shard_map/all_gather | solution.py:208
  177.8 721.7 %all-gather.26.cloned.1.call-start = ((), (), s32[]{:S(2)}) async-start(), calls=%async_computation.17 | async-start | bytes 21626880 | tf_op jit(solution)/shard_map/all_gather | solution.py:209
  180.1 960.2 %reduce-scatter.10.cloned.1.call-start = ((), (), s32[]{:S(2)}) async-start(), calls=%async_computation.18 | async-start | bytes 9437184 | tf_op jit(solution)/shard_map/reduce_scatter | solution.py:353
  180.5 485.0 %copy-start.50 = (s32[128]{0:T(128)}, s32[128]{0:T(128)S(1)}, u32[]{:S(2)}) copy-start(s32[128]{0:T(128)S(1)} %iota_add_fusion) | copy-start | bytes 1540
  186.7 433.3 %copy-start.24 = (s32[131072]{0:T(1024)}, s32[131072]{0:T(1024)S(1)}, u32[]{:S(2)}) copy-start(s32[131072]{0:T(1024)S(1)} %broadcast_clamp_fusion) | copy-start | bytes 1572868
  620.0 43.6 %copy-start.53 = (s32[2]{0:T(128)S(1)}, s32[2]{0:T(128)}, u32[]{:S(2)}) copy-start(s32[2]{0:T(128)} %param.22) | copy-start | bytes 28
  620.0 45.8 %copy-start.31 = (bf16[2,128,2048]{2,1,0:T(8,128)(2,1)S(1)}, bf16[2,128,2048]{2,1,0:T(8,128)(2,1)}, u32[]{:S(2)}) copy-start(bf16[2,128,2048]{2,1,0:T(8,128)(2,1)} %param.21) | copy-start | bytes 3145732
  620.0 47.0 %copy-start.40 = (bf16[256,2048]{1,0:T(8,128)(2,1)S(1)}, bf16[256,2048]{1,0:T(8,128)(2,1)}, u32[]{:S(2)}) copy-start(bf16[256,2048]{1,0:T(8,128)(2,1)} %copy-done.39) | copy-start | bytes 3145732
  665.5 7.3 copy-start.47
  673.1 38.5 %copy-start.22 = (bf16[128,2048]{0,1:T(8,128)(2,1)}, bf16[128,2048]{0,1:T(8,128)(2,1)S(1)}, u32[]{:S(2)}) copy-start(bf16[128,2048]{0,1:T(8,128)(2,1)S(1)} %copy.75) | copy-start | bytes 1572868
  673.4 55.3 %copy-start.21 = (bf16[128,2048]{0,1:T(8,128)(2,1)}, bf16[128,2048]{0,1:T(8,128)(2,1)S(1)}, u32[]{:S(2)}) copy-start(bf16[128,2048]{0,1:T(8,128)(2,1)S(1)} %copy.70) | copy-start | bytes 1572868
  711.6 17.1 copy-start.5
  740.5 11.3 copy-start.2
  755.6 8.7 copy-start.4
  764.4 7.7 copy-start.34
  764.4 8.9 copy-start.7
  773.2 6.8 copy-start.17
  781.6 12.7 copy-start.19
  794.3 105.2 %copy-start.28 = (bf16[256,2048]{1,0:T(8,128)(2,1)S(1)}, bf16[256,2048]{1,0:T(8,128)(2,1)}, u32[]{:S(2)}) copy-start(bf16[256,2048]{1,0:T(8,128)(2,1)} %fusion.30) | copy-start | bytes 3145732
  923.2 12.3 copy-start.33
  923.2 12.3 copy-start.13
  923.2 12.3 copy-start.32
  935.4 12.4 copy-start.48
  950.5 164.7 %copy-start.10 = (f32[256,2048]{1,0:T(8,128)}, f32[256,2048]{1,0:T(8,128)S(1)}, u32[]{:S(2)}) copy-start(f32[256,2048]{1,0:T(8,128)S(1)} %fusion.29) | copy-start | bytes 6291460
  1007.5 11.7 copy-start.23
  1053.1 177.4 %reduce-scatter.12.cloned.1.call-start = ((), (), s32[]{:S(2)}) async-start(), calls=%async_computation.19 | async-start | bytes 9437184 | tf_op jit(solution)/shard_map/reduce_scatter | solution.py:356
  1091.6 1033.5 %reduce-scatter.14.cloned.1.call-start = ((), (), s32[]{:S(2)}) async-start(), calls=%async_computation.20 | async-start | bytes 17301504 | tf_op jit(solution)/shard_map/reduce_scatter | solution.py:387
  1092.8 8.7 slice-start.2
  1093.2 12.8 copy-start.15
  1093.2 8.3 slice-start.3
  1093.2 8.6 copy-start.6
  1115.2 1010.0 %reduce-scatter.20.cloned.1.call-start = ((), (), s32[]{:S(2)}) async-start(), calls=%async_computation.23 | async-start | bytes 17301504 | tf_op jit(solution)/shard_map/reduce_scatter | solution.py:390
  1124.5 15.8 copy-start.16
  1124.5 1000.6 %reduce-scatter.16.cloned.1.call-start = ((), (), s32[]{:S(2)}) async-start(), calls=%async_computation.21 | async-start | bytes 17301504 | tf_op jit(solution)/shard_map/reduce_scatter | solution.py:388
  1150.1 975.1 %reduce-scatter.18.cloned.1.call-start = ((), (), s32[]{:S(2)}) async-start(), calls=%async_computation.22 | async-start | bytes 17301504 | tf_op jit(solution)/shard_map/reduce_scatter | solution.py:389
  1240.1 1187.7 %reduce-scatter.22.cloned.1.call-start = ((), (), s32[]{:S(2)}) async-start(), calls=%async_computation.24 | async-start | bytes 43253760 | tf_op jit(solution)/shard_map/reduce_scatter | solution.py:316
  1259.9 1615.5 %reduce-scatter.24.cloned.1.call-start = ((), (), s32[]{:S(2)}) async-start(), calls=%async_computation.25 | async-start | bytes 43253760 | tf_op jit(solution)/shard_map/reduce_scatter | solution.py:317
  1278.5 2044.5 %reduce-scatter.26.cloned.1.call-start = ((), (), s32[]{:S(2)}) async-start(), calls=%async_computation.26 | async-start | bytes 43253760 | tf_op jit(solution)/shard_map/reduce_scatter | solution.py:318
  1299.2 725.5 %copy-start.51 = (s32[128]{0:T(128)S(1)}, s32[128]{0:T(128)}, u32[]{:S(2)}) copy-start(s32[128]{0:T(128)} %copy-done.50) | copy-start | bytes 1540
  2024.7 13.9 slice-start
  2024.9 13.7 slice-start.1
  2038.7 10.4 copy-start.30
  2049.0 6.0 copy-start.14
  2049.0 6.0 copy-start.27
  2049.0 6.0 copy-start.49
  2049.1 23.7 slice-start.4
  2055.1 11.7 copy-start.37
  2055.1 17.7 slice-start.5
  2066.8 6.0 copy-start.9
  2066.8 6.0 copy-start.38
  2066.8 6.0 copy-start.44
  2066.8 6.0 copy-start.46
  2072.8 49.1 %copy-start.11 = (f32[256,2048]{1,0:T(8,128)S(1)}, f32[256,2048]{1,0:T(8,128)}, u32[]{:S(2)}) copy-start(f32[256,2048]{1,0:T(8,128)} %copy-done.10) | copy-start | bytes 6291460
  (15 other events, 24.8 us)
Sparse Core Ops, SparseCore 0:
  11.6 77.0 all-gather.9
  92.2 75.9 all-gather.15
  171.8 76.0 all-gather.13
  249.9 80.5 all-gather.11
  332.6 80.5 all-gather.17
  416.6 75.9 all-gather.19
  495.5 132.7 all-gather.21
  631.1 132.7 all-gather.23
  766.7 132.7 all-gather.25
  1053.3 87.0 reduce-scatter.9
  1142.6 87.9 reduce-scatter.11
  1233.3 182.3 reduce-scatter.13
  1418.6 184.4 reduce-scatter.19
  1605.8 184.3 reduce-scatter.15
  1792.9 184.3 reduce-scatter.17
  1980.0 447.7 reduce-scatter.21
  2430.5 444.8 reduce-scatter.23
  2878.2 444.8 reduce-scatter.25
where the time goes:
time: 3340 us; the launch traced here: 3330 us
  waiting for transfers between devices  1490 us (45%)
  local copies, waits for them, and re-layouts  1290 us (39%)
  matrix products  396 us (12%)
  blocking collectives  83.4 us (2%)
  other arithmetic  53.1 us (2%)
    gather x2, local copies, waits for them, and re-layouts, grad_step(): bucket = jnp.take(buckets, offset, axis=0)  725 us
    gather x2, local copies, waits for them, and re-layouts, block_scores(): pair_bias = jnp.take(offset_bias, offset, axis=1)  477 us
    reduce_scatter x1, waiting for transfers between devices, shards(): lax.psum_scatter(grad_up_weight, ('fsdp', 'ctx'), scatter_dimension=0, ti...  448 us
    reduce_scatter x1, waiting for transfers between devices, shards(): lax.psum_scatter(grad_down, ('fsdp', 'ctx'), scatter_dimension=0, tiled=T...  448 us
    reduce_scatter x1, waiting for transfers between devices, shards(): lax.psum_scatter(grad_gate_weight, ('fsdp', 'ctx'), scatter_dimension=0,...  303 us
    all_gather x1, waiting for transfers between devices, shards(): lax.all_gather(w_down.astype(jnp.bfloat16), ('fsdp', 'ctx'), axis=0, tile...  92.2 us
    unnamed x2, blocking collectives  83.4 us
    reduce_scatter x1, waiting for transfers between devices, shards(): lax.psum_scatter(jnp.stack(grad_value_list).astype(jnp.bfloat16), 'ctx',...  80.5 us
  transfers between devices with their start and end apart: 18, of which 8 were waited for; matrix products, arithmetic and copies ran while one was open for 47% of the time, Pallas kernels for 0%

commit v1 on v0

v1 whole, which is shorter than its diff:
```python
import functools, math
import jax, jax.numpy as jnp
from jax import lax
from jax.experimental import pallas as pl
from jax.experimental.pallas import tpu as pltpu

MASKED = -1e30
NT = (((1,), (1,)), ((), ()))
NN = (((1,), (0,)), ((), ()))


def dotf(a, b, dims=NN):
    return lax.dot_general(a, b, dims, preferred_element_type=jnp.float32)


def head_mask(width, head_dim, h):
    lane = lax.broadcasted_iota(jnp.int32, (1, width), 1)
    return (lane // head_dim == h).astype(jnp.float32).astype(jnp.bfloat16)


def fill_skew(bias_ref, skew_ref, heads, block, length):
    for h in range(heads):
        rows = jnp.broadcast_to(bias_ref[h : h + 1, :], (block, 2 * length))
        rolled = pltpu.roll(rows, 2 * length - (block - 1), 1, stride=1, stride_axis=0)
        skew_ref[h] = rolled[:, : 2 * length - block]


def attn_fwd_kernel(
    heads, head_dim, block, length, lens_ref, q_ref, k_ref, v_ref, bias_ref, out_ref, lse_ref,
    skew_ref, kt_ref,
):
    seq, blk = pl.program_id(0), pl.program_id(1)
    width = heads * head_dim

    @pl.when((seq == 0) & (blk == 0))
    def _():
        fill_skew(bias_ref, skew_ref, heads, block, length)

    @pl.when(blk == 0)
    def _():
        kt_ref[...] = k_ref[...].T

    valid_len = lens_ref[seq]
    key_pos = lax.broadcasted_iota(jnp.int32, (1, length), 1)
    key_mask = jnp.where(key_pos < valid_len, 0.0, MASKED)
    start = pl.multiple_of(length - block - blk * block, block)
    lane = lax.broadcasted_iota(jnp.int32, (block, 128), 1)
    out = jnp.zeros((block, width), jnp.float32)
    lse_all = jnp.zeros((block, 128), jnp.float32)
    for h in range(heads):
        mask = head_mask(width, head_dim, h)
        scores = dotf(q_ref[...] * mask, kt_ref[...])
        scores = scores + skew_ref[h, :, pl.ds(start, length)] + key_mask
        peak = jnp.max(scores, axis=1, keepdims=True)
        probs = jnp.exp(scores - peak)
        mass = jnp.sum(probs, axis=1, keepdims=True)
        probs = (probs * (1.0 / mass)).astype(jnp.bfloat16)
        out = out + dotf(probs, v_ref[...] * mask)
        lse_all = jnp.where(lane == h, peak + jnp.log(mass), lse_all)
    out_ref[...] = out.astype(jnp.bfloat16)
    lse_ref[...] = lse_all


def attn_fwd(qkv, offset_bias, lens, heads, head_dim, seqs, block=256):
    rows, width3 = qkv.shape
    width = width3 // 3
    length = rows // seqs
    block = min(block, length)
    blocks = length // block
    return pl.pallas_call(
        functools.partial(attn_fwd_kernel, heads, head_dim, block, length),
        grid_spec=pltpu.PrefetchScalarGridSpec(
            num_scalar_prefetch=1,
            grid=(seqs, blocks),
            in_specs=[
                pl.BlockSpec((block, width), lambda s, i, lens: (s * blocks + i, 0)),
                pl.BlockSpec((length, width), lambda s, i, lens: (s, 1)),
                pl.BlockSpec((length, width), lambda s, i, lens: (s, 2)),
                pl.BlockSpec((heads, 2 * length), lambda s, i, lens: (0, 0)),
            ],
            out_specs=[
                pl.BlockSpec((block, width), lambda s, i, lens: (s * blocks + i, 0)),
                pl.BlockSpec((block, 128), lambda s, i, lens: (s * blocks + i, 0)),
            ],
            scratch_shapes=[
                pltpu.VMEM((heads, block, 2 * length - block), jnp.float32),
                pltpu.VMEM((width, length), jnp.bfloat16),
            ],
        ),
        out_shape=[
            jax.ShapeDtypeStruct((rows, width), jnp.bfloat16),
            jax.ShapeDtypeStruct((rows, 128), jnp.float32),
        ],
        compiler_params=pltpu.CompilerParams(
            dimension_semantics=("arbitrary", "arbitrary"), vmem_limit_bytes=56 * 1024 * 1024
        ),
        name="attn_fwd",
    )(lens, qkv, qkv, qkv, offset_bias)


def attn_bwd_kernel(
    heads, head_dim, block, length, lens_ref, q_ref, k_ref, v_ref, g_ref, lse_ref, bias_ref,
    dq_ref, dk_ref, dv_ref, dbias_ref, skew_ref, kt_ref, vt_ref, acc_ref, dkt_ref, dvt_ref,
):
    seq, blk = pl.program_id(0), pl.program_id(1)
    last_seq, last_blk = pl.num_programs(0) - 1, pl.num_programs(1) - 1
    width = heads * head_dim

    @pl.when((seq == 0) & (blk == 0))
    def _():
        fill_skew(bias_ref, skew_ref, heads, block, length)
        acc_ref[...] = jnp.zeros_like(acc_ref)

    @pl.when(blk == 0)
    def _():
        kt_ref[...] = k_ref[...].T
        vt_ref[...] = v_ref[...].T
        dkt_ref[...] = jnp.zeros_like(dkt_ref)
        dvt_ref[...] = jnp.zeros_like(dvt_ref)

    valid_len = lens_ref[seq]
    key_pos = lax.broadcasted_iota(jnp.int32, (1, length), 1)
    key_mask = jnp.where(key_pos < valid_len, 0.0, MASKED)
    start = pl.multiple_of(length - block - blk * block, block)
    q_t = q_ref[...].T
    g_t = g_ref[...].T
    dq = jnp.zeros((block, width), jnp.float32)
    row = lax.broadcasted_iota(jnp.int32, (width, 1), 0)
    for h in range(heads):
        mask = head_mask(width, head_dim, h)
        rmask = (row // head_dim == h).astype(jnp.float32).astype(jnp.bfloat16)
        scores = dotf(q_ref[...] * mask, kt_ref[...])
        scores = scores + skew_ref[h, :, pl.ds(start, length)] + key_mask
        probs = jnp.exp(scores - lse_ref[:, h : h + 1])
        grad_probs = dotf(g_ref[...] * mask, vt_ref[...])
        delta = jnp.sum(probs * grad_probs, axis=1, keepdims=True)
        ds = (probs * (grad_probs - delta)).astype(jnp.bfloat16)
        dq = dq + dotf(ds, k_ref[...] * mask)
        acc_ref[h, :, pl.ds(start, length)] += ds.astype(jnp.float32)
        dkt_ref[...] += dotf(q_t * rmask, ds)
        dvt_ref[...] += dotf(g_t * rmask, probs.astype(jnp.bfloat16))
    dq_ref[...] = dq.astype(jnp.bfloat16)

    @pl.when(blk == last_blk)
    def _():
        dk_ref[...] = dkt_ref[...].astype(jnp.bfloat16).T
        dv_ref[...] = dvt_ref[...].astype(jnp.bfloat16).T

    @pl.when((seq == last_seq) & (blk == last_blk))
    def _():
        for h in range(heads):
            part = jnp.concatenate(
                [acc_ref[h], jnp.zeros((block, block), jnp.float32)], axis=1
            )
            n = block
            while n > 8:
                n //= 2
                part = pltpu.roll(part[:n], n, 1) + part[n:]
            total = jnp.zeros((1, 2 * length), jnp.float32)
            for i in range(n):
                total = total + (pltpu.roll(part, n - 1 - i, 1) if i < n - 1 else part)[i : i + 1]
            dbias_ref[h : h + 1, :] = total


def attn_bwd(qkv, grad, lse, offset_bias, lens, heads, head_dim, seqs, block=256):
    rows, width3 = qkv.shape
    width = width3 // 3
    length = rows // seqs
    block = min(block, length)
    blocks = length // block
    return pl.pallas_call(
        functools.partial(attn_bwd_kernel, heads, head_dim, block, length),
        grid_spec=pltpu.PrefetchScalarGridSpec(
            num_scalar_prefetch=1,
            grid=(seqs, blocks),
            in_specs=[
                pl.BlockSpec((block, width), lambda s, i, lens: (s * blocks + i, 0)),
                pl.BlockSpec((length, width), lambda s, i, lens: (s, 1)),
                pl.BlockSpec((length, width), lambda s, i, lens: (s, 2)),
                pl.BlockSpec((block, width), lambda s, i, lens: (s * blocks + i, 0)),
                pl.BlockSpec((block, 128), lambda s, i, lens: (s * blocks + i, 0)),
                pl.BlockSpec((heads, 2 * length), lambda s, i, lens: (0, 0)),
            ],
            out_specs=[
                pl.BlockSpec((block, width), lambda s, i, lens: (s * blocks + i, 0)),
                pl.BlockSpec((length, width), lambda s, i, lens: (s, 0)),
                pl.BlockSpec((length, width), lambda s, i, lens: (s, 0)),
                pl.BlockSpec((heads, 2 * length), lambda s, i, lens: (0, 0)),
            ],
            scratch_shapes=[
                pltpu.VMEM((heads, block, 2 * length - block), jnp.float32),
                pltpu.VMEM((width, length), jnp.bfloat16),
                pltpu.VMEM((width, length), jnp.bfloat16),
                pltpu.VMEM((heads, block, 2 * length - block), jnp.float32),
                pltpu.VMEM((width, length), jnp.float32),
                pltpu.VMEM((width, length), jnp.float32),
            ],
        ),
        out_shape=[
            jax.ShapeDtypeStruct((rows, width), jnp.bfloat16),
            jax.ShapeDtypeStruct((rows, width), jnp.bfloat16),
            jax.ShapeDtypeStruct((rows, width), jnp.bfloat16),
            jax.ShapeDtypeStruct((heads, 2 * length), jnp.float32),
        ],
        compiler_params=pltpu.CompilerParams(
            dimension_semantics=("arbitrary", "arbitrary"), vmem_limit_bytes=60 * 1024 * 1024
        ),
        name="attn_bwd",
    )(lens, qkv, qkv, qkv, grad, lse, offset_bias)


from jax.sharding import Mesh
from jax.sharding import PartitionSpec as P

H = 32
EPSILON = 1e-06
HIGHEST = lax.Precision.HIGHEST
BF = jnp.bfloat16
F32 = jnp.float32
TP = ("fsdp", "core")
ALL = ("fsdp", "z", "core")


def rms_scale(values):
    return lax.rsqrt(jnp.mean(values * values, axis=1, keepdims=True) + EPSILON)


def norm_back(grad_normed, values, row_scale, gain_row):
    weighted = grad_normed * gain_row
    inner_mean = jnp.mean(weighted * values, axis=1, keepdims=True)
    return row_scale * (weighted - values * row_scale * row_scale * inner_mean)


def gelu_tanh(values):
    return jax.nn.gelu(values, approximate=True)


def swap_planes(x):
    f, z = lax.axis_size("fsdp"), lax.axis_size("z")
    pairs = [(i * z + j, j * f + i) for i in range(f) for j in range(z)]
    return lax.ppermute(x, ("fsdp", "z"), pairs)


def gather_rows(x, seqs):
    b = x.shape[0] // seqs
    full = lax.all_gather(x.reshape(seqs, b, -1), TP, axis=1, tiled=True)
    return full.reshape(-1, x.shape[1])


def scatter_rows(x, seqs):
    part = lax.psum_scatter(
        x.reshape(seqs, x.shape[0] // seqs, -1), TP, scatter_dimension=1, tiled=True
    )
    return part.reshape(-1, x.shape[1])


class Layout:
    def __init__(self, per_device, head_dim):
        self.f, self.z, self.c = (lax.axis_size(a) for a in ALL)
        self.natural = per_device % head_dim == 0
        self.per_device = per_device

    def split(self, w):
        rows, cols = w.shape
        if self.natural:
            w = w.reshape(rows, self.f, self.z, self.c, self.per_device)
            w = w.transpose(1, 3, 0, 2, 4)
        else:
            w = w.reshape(rows, self.f, self.c, -1).transpose(1, 2, 0, 3)
        return w.reshape(self.f * self.c, rows, -1)

    def join(self, w):
        devices, rows, cols = w.shape
        if self.natural:
            w = w.reshape(self.f, self.c, rows, self.z, self.per_device)
            w = w.transpose(2, 0, 3, 1, 4)
        else:
            w = w.reshape(self.f, self.c, rows, cols).transpose(2, 0, 1, 3)
        return w.reshape(rows, -1)

    def gather(self, w):
        if self.natural:
            return lax.all_gather(w, "z", axis=0, tiled=True)
        both = lax.all_gather(w, ("z", "core"), axis=0, tiled=True)
        size = both.shape[0] // self.c
        return lax.dynamic_slice_in_dim(both, lax.axis_index("core") * size, size, 0)

    def scatter(self, g):
        if self.natural:
            return lax.psum_scatter(g, "z", scatter_dimension=0, tiled=True)
        size = g.shape[0]
        both = jnp.zeros((size * self.c, g.shape[1]), g.dtype)
        both = lax.dynamic_update_slice_in_dim(both, g, lax.axis_index("core") * size, 0)
        return lax.psum_scatter(both, ("z", "core"), scatter_dimension=0, tiled=True)


def spread(pieces):
    f, z, c = (lax.axis_size(a) for a in ALL)
    devices, rows, cols = pieces.shape
    got = lax.all_to_all(pieces, TP, split_axis=0, concat_axis=0, tiled=True)
    return got.reshape(f, c * rows, cols)


def over_z(got):
    f, cr, cols = got.shape
    full = lax.all_gather(got, "z", axis=1, tiled=True)
    return full.reshape(-1, cols)


def reduce_z(grad):
    f, z = lax.axis_size("fsdp"), lax.axis_size("z")
    return lax.psum_scatter(
        grad.reshape(f, grad.shape[0] // f, -1), "z", scatter_dimension=1, tiled=True
    )


def unspread(part):
    f, cr, cols = part.shape
    c = lax.axis_size("core")
    return lax.all_to_all(
        part.reshape(f * c, cr // c, cols), TP, split_axis=0, concat_axis=0, tiled=True
    )


def shards(
    tokens, cotangent, lengths, buckets, norm1_gain, rel_bias,
    w_query, w_key, w_value, w_attn_out, norm2_gain, w_gate, w_up, w_down,
):
    fs, zs, cs = (lax.axis_size(a) for a in ALL)
    seqs, block_len, width = tokens.shape
    rows = seqs * block_len
    length = block_len * fs * cs
    head_dim = w_query.shape[1] // H
    heads = H // (fs * cs)
    buckets_n = rel_bias.shape[0] * fs * zs * cs // H
    head_cols = Layout(w_attn_out.shape[0], head_dim)
    ff_cols = Layout(w_down.shape[0], w_down.shape[0])

    small = lax.all_gather(
        jnp.concatenate([norm1_gain, norm2_gain, rel_bias]).astype(BF), ALL, axis=0
    )
    g = norm1_gain.shape[0]
    gain_one = small[:, :g].reshape(1, -1).astype(F32)
    gain_two = small[:, g : 2 * g].reshape(1, -1).astype(F32)
    table = small[:, 2 * g :].reshape(1, -1).astype(F32).reshape(H, buckets_n)
    plane_index = lax.axis_index("fsdp") * cs + lax.axis_index("core")
    table = head_cols.split(jnp.repeat(table.T, head_dim, axis=1))[:, :, ::head_dim]
    table = lax.dynamic_index_in_dim(table, plane_index, 0, keepdims=False).T
    one_hot = (buckets[:, None] == jnp.arange(buckets_n, dtype=jnp.int32)[None, :]).astype(F32)
    one_hot = jnp.pad(one_hot, ((0, 1), (0, 0)))
    offset_bias = jnp.dot(table, one_hot.T, precision=HIGHEST)

    lens = swap_planes(lengths)
    x_in = swap_planes(tokens)
    cot = swap_planes(cotangent)

    qkv_pieces = jnp.concatenate(
        [head_cols.split(w.astype(BF)) for w in (w_query, w_key, w_value)], axis=2
    )
    ff_pieces = jnp.concatenate([ff_cols.split(w.astype(BF)) for w in (w_gate, w_up)], axis=2)
    w_qkv = over_z(spread(qkv_pieces))
    w_o = head_cols.gather(w_attn_out.astype(BF))
    w_gu = over_z(spread(ff_pieces))
    w_d = ff_cols.gather(w_down.astype(BF))
    ff = w_d.shape[0]

    positions = plane_index * block_len + jnp.arange(block_len, dtype=jnp.int32)
    valid = (positions[None, :] < lens[:, None]).astype(F32).reshape(rows, 1)

    x = x_in.reshape(rows, width).astype(F32)
    scale_one = rms_scale(x)
    normed = gather_rows((x * scale_one * gain_one).astype(BF), seqs)
    grad_rows = cot.reshape(rows, width).astype(F32) * valid
    grad_branch = gather_rows(grad_rows.astype(BF), seqs)

    qkv = jnp.dot(normed, w_qkv, preferred_element_type=F32).astype(BF)
    attended, lse = attn_fwd(qkv, offset_bias, lens, heads, head_dim, seqs)
    attn_sum = scatter_rows(jnp.dot(attended, w_o, preferred_element_type=F32).astype(BF), seqs)
    hidden_one = x + attn_sum.astype(F32)
    scale_two = rms_scale(hidden_one)
    normed_two = gather_rows((hidden_one * scale_two * gain_two).astype(BF), seqs)

    gate = jnp.dot(normed_two, w_gu[:, :ff], preferred_element_type=F32)
    upward = jnp.dot(normed_two, w_gu[:, ff:], preferred_element_type=F32)
    activated, gelu_pull = jax.vjp(gelu_tanh, gate)
    hidden_ff = (activated * upward).astype(BF)
    out_part = jnp.dot(hidden_ff, w_d, preferred_element_type=F32).astype(BF)
    grad_hidden = jnp.einsum("rd,fd->rf", grad_branch, w_d, preferred_element_type=F32)
    grad_gate = gelu_pull(grad_hidden * upward)[0].astype(BF)
    grad_up = (grad_hidden * activated).astype(BF)
    grad_gu = jnp.concatenate([grad_gate, grad_up], axis=1)
    grad_n2_part = jnp.einsum("rf,df->rd", grad_gu, w_gu, preferred_element_type=F32).astype(BF)
    grad_normed_two = scatter_rows(grad_n2_part, seqs).astype(F32)
    gain_two_part = jnp.sum(grad_normed_two * hidden_one * scale_two, axis=0)
    grad_hidden_one = grad_rows + norm_back(grad_normed_two, hidden_one, scale_two, gain_two)
    grad_attn = gather_rows(grad_hidden_one.astype(BF), seqs)

    result = hidden_one + scatter_rows(out_part, seqs).astype(F32)
    output = swap_planes((result * valid).astype(BF).reshape(seqs, block_len, width))

    grad_w_down = jnp.einsum("rf,rd->fd", hidden_ff, grad_branch, preferred_element_type=F32)
    grad_w_gu = jnp.einsum("rd,rf->df", normed_two, grad_gu, preferred_element_type=F32)
    sum_down = ff_cols.scatter(grad_w_down.astype(BF))
    sum_gu = reduce_z(grad_w_gu.astype(BF))

    grad_attended = jnp.einsum("rd,kd->rk", grad_attn, w_o, preferred_element_type=F32).astype(BF)
    grad_w_o = jnp.einsum("rk,rd->kd", attended, grad_attn, preferred_element_type=F32)
    sum_o = head_cols.scatter(grad_w_o.astype(BF))
    dq, dk, dv, grad_offset = attn_bwd(
        qkv, grad_attended, lse, offset_bias, lens, heads, head_dim, seqs
    )
    dqkv = jnp.concatenate([dq, dk, dv], axis=1)
    grad_w_qkv = jnp.einsum("rd,rk->dk", normed, dqkv, preferred_element_type=F32)
    sum_qkv = reduce_z(grad_w_qkv.astype(BF))
    grad_n_part = jnp.einsum("rk,dk->rd", dqkv, w_qkv, preferred_element_type=F32).astype(BF)
    grad_normed = scatter_rows(grad_n_part, seqs).astype(F32)
    gain_one_part = jnp.sum(grad_normed * x * scale_one, axis=0)
    grad_x = grad_hidden_one + norm_back(grad_normed, x, scale_one, gain_one)
    grad_tokens = swap_planes(grad_x.astype(BF).reshape(seqs, block_len, width))

    grad_table = jnp.dot(grad_offset, one_hot, precision=HIGHEST)
    bias_all = jnp.zeros((fs * cs, heads, buckets_n), F32)
    bias_all = lax.dynamic_update_index_in_dim(bias_all, grad_table, plane_index, 0)
    bias_all = jnp.repeat(bias_all.transpose(0, 2, 1), head_dim, axis=2)
    bias_all = head_cols.join(bias_all)[:, ::head_dim].T.reshape(fs * zs * cs, -1)
    small_grad = jnp.concatenate(
        [
            gain_one_part.reshape(fs * zs * cs, -1),
            gain_two_part.reshape(fs * zs * cs, -1),
            bias_all,
        ],
        axis=1,
    )
    small_grad = lax.psum_scatter(small_grad, ALL, scatter_dimension=0, tiled=True)[0]

    got_gu = unspread(sum_gu)
    got_qkv = unspread(sum_qkv)
    hw = heads * head_dim
    grads_qkv = [
        head_cols.join(got_qkv[:, :, i * hw : (i + 1) * hw]).astype(F32) for i in range(3)
    ]
    grads_gu = [ff_cols.join(got_gu[:, :, i * ff : (i + 1) * ff]).astype(F32) for i in range(2)]
    return (
        output,
        grad_tokens,
        small_grad[:g],
        small_grad[2 * g :],
        grads_qkv[0],
        grads_qkv[1],
        grads_qkv[2],
        sum_o.astype(F32),
        small_grad[g : 2 * g],
        grads_gu[0],
        grads_gu[1],
        sum_down.astype(F32),
    )


def solution(mesh):
    fs, ctx = mesh.shape["fsdp"], mesh.shape["ctx"]
    mesh3 = Mesh(mesh.devices.reshape(fs, ctx // 2, 2), ALL)
    act = P("fsdp", ("z", "core"), None)
    vec, mat = P(ALL), P(ALL, None)
    in_specs = (act, act, P("fsdp"), P(), vec, vec, mat, mat, mat, mat, vec, mat, mat, mat)
    out_specs = (act, act, vec, vec, mat, mat, mat, mat, vec, mat, mat, mat)
    return jax.shard_map(shards, mesh=mesh3, in_specs=in_specs, out_specs=out_specs, check_vma=False)
```

time: 3340 us -> 1390 us (0.42)
  local copies, waits for them, and re-layouts: 1290 us -> 61.9 us
  waiting for transfers between devices: 1490 us -> 796 us
  matrix products: 396 us -> 146 us
  blocking collectives: 83.4 us -> 232 us
  Pallas kernels: 0 us -> 70.1 us
    gather x5 -> x0, local copies, waits for them, and re-layouts: 1210 us -> none  [the longest x2 725 us: grad_step(): bucket = jnp.take(buckets, offset, axis=0)]
    reduce_scatter x9 -> x8, waiting for transfers between devices: 1290 us -> 415 us  [the longest x4 212 us: scatter_rows(): lax.psum_scatter(x.reshape(seqs, x.shape[0] // seqs, -1), TP, scatter_dim...]
    dot_general x37 -> x15, matrix products: 396 us -> 146 us  [the longest x1 16.6 us: shards(): jnp.einsum('rd,rf->df', normed_two, grad_gu, preferred_element_type=F32)]
    all_gather x0 -> x1, blocking collectives: none -> 142 us  [shards(): lax.all_gather(jnp.concatenate([norm1_gain, norm2_gain, rel_bias]).astype...]
    all_gather x9 -> x8, waiting for transfers between devices: 194 us -> 312 us  [the longest x4 191 us: gather_rows(): full = lax.all_gather(x.reshape(seqs, b, -1), TP, axis=1, tiled=True)]
    pallas_call x0 -> x2, Pallas kernels: none -> 70.1 us  [the longest x1 44.5 us: attn_bwd(): pl.pallas_call(functools.partial(attn_bwd_kernel, heads, head_dim, block,...]
    ppermute x0 -> x5, waiting for transfers between devices: none -> 68.1 us  [swap_planes(): return lax.ppermute(x, ('fsdp', 'z'), pairs)]
    slice x13 -> x4, local copies, waits for them, and re-layouts: 41.8 us -> 1.27 us  [the longest x1 0.59 us: shards(): small_grad[2 * g:]]
  transfers between devices with their start and end apart: 18 -> 23, of which waited for: 8 -> 14; matrix products, arithmetic and copies ran while one was open for 47% -> 13% of each run, Pallas kernels for 0% -> 5%
where the time goes in v1:
time: 1390 us; the launch traced here: 1380 us
  waiting for transfers between devices  796 us (57%)
  blocking collectives  232 us (17%)
  matrix products  146 us (11%)
  Pallas kernels  70.1 us (5%)
  local copies, waits for them, and re-layouts  61.9 us (4%)
  other arithmetic  32.7 us (2%)
  starting transfers between devices  28.1 us (2%)
  between operations  14.9 us (1%)
    reduce_scatter x4, waiting for transfers between devices, scatter_rows(): lax.psum_scatter(x.reshape(seqs, x.shape[0] // seqs, -1), TP, scatter_dim...  212 us
    all_gather x4, waiting for transfers between devices, gather_rows(): full = lax.all_gather(x.reshape(seqs, b, -1), TP, axis=1, tiled=True)  191 us
    all_gather x1, blocking collectives, shards(): lax.all_gather(jnp.concatenate([norm1_gain, norm2_gain, rel_bias]).astype...  142 us
    reduce_scatter x2, waiting for transfers between devices, scatter(): return lax.psum_scatter(g, 'z', scatter_dimension=0, tiled=True)  131 us
    all_gather x2, waiting for transfers between devices, over_z(): full = lax.all_gather(got, 'z', axis=1, tiled=True)  87.8 us
    reduce_scatter x2, waiting for transfers between devices, reduce_z(): lax.psum_scatter(grad.reshape(f, grad.shape[0] // f, -1), 'z', scatter_di...  71.9 us
    ppermute x5, waiting for transfers between devices, swap_planes(): return lax.ppermute(x, ('fsdp', 'z'), pairs)  68.1 us
    unnamed x1, blocking collectives  55.8 us
  transfers between devices with their start and end apart: 23, of which 14 were waited for; matrix products, arithmetic and copies ran while one was open for 13% of the time, Pallas kernels for 5%

profile of v1, /device:TPU:22, one launch (start us, length us, event | category | flops | bytes accessed | tf_op | source)
XLA Modules:
  0.0 1381.7 jit_solution(17431289987565526280)
XLA Ops:
  11.6 14.3 %all_to_all.20 = bf16[8,64,768]{2,1,0:T(8,128)(2,1)} all-to-all(bf16[8,64,768]{2,1,0:T(8,128)(2,1)S(1)} %pad_maximum_fusion.4), channel_id=1, replica_groups=mesh['fsdp'=4,'z'=4,'core'=2] {'fsdp','core'}, dimensions={0} | all-to-all | bytes 1572864 | tf_op jit(solution)/shard_map/all_to_all | solution.py:300
  26.0 4.5 collective-permute-start
  30.6 141.9 %all-gather = bf16[32,1,160]{2,1,0:T(2,128)(2,1)S(1)} all-gather(bf16[1,1,160]{2,1,0:T(2,128)(2,1)S(1)} %maximum_bitcast_fusion), channel_id=1, replica_groups=mesh['fsdp'=4,'z'=4,'core'=2] {'fsdp','z','core'}, dimensions={0}, use_global_device_ids=true | all-gather | bytes 10560 | tf_op jit(solution)/shard_map/all_gather | solution.py:339
  174.3 1.9 collective-permute-start.1
  179.0 52.2 %all-gather.10.cloned.1.call-done = bf16[2,1024,2048]{2,1,0:T(8,128)(2,1)} async-done(((bf16[2,128,2048]{2,1,0:T(8,128)(2,1)}), bf16[2,1024,2048]{2,1,0:T(8,128)(2,1)}) %all-gather.10.cloned.1.call-update) | async-done | bytes 8388624 | tf_op jit(solution)/shard_map/all_gather | solution.py:246
  231.3 11.2 convolution_convert_fusion.5.q_ref.k_ref.v_ref
  243.0 25.6 %attn_fwd.1 = (bf16[2048,256]{1,0:T(8,128)(2,1)}, f32[2048,128]{1,0:T(8,128)}) custom-call(s32[2]{0:T(128)} %copy-done.18, bf16[2048,768]{1,0:T(8,128)(2,1)} %convolution_convert_fusion.5.q_ref.k_ref.v_ref, bf16[2048,768]{1,0:T(8,128)(2,1)} %convolution_convert_fusion.5.q_ref.k_ref.v_ref, bf16[2048,768]{1,0:T(8,128)(2,1)} %convolution_convert_fusion.5.q_ref.k_ref.v_ref, ...), custom_call_target="tpu_custom_call" | custom-call | tf_op jit(solution)/shard_map/attn_fwd/pallas_call | solution.py:70
  268.5 7.1 convolution_convert_fusion.3
  278.0 4.1 collective-permute-start.3
  282.2 68.1 %collective-permute-done.3 = bf16[2,128,2048]{2,1,0:T(8,128)(2,1)S(1)} collective-permute-done((bf16[2,128,2048]{2,1,0:T(8,128)(2,1)}, bf16[2,128,2048]{2,1,0:T(8,128)(2,1)S(1)}, u32[]{:S(2)}, u32[]{:S(2)}) %collective-permute-start.3) | collective-permute-done | bytes 1048608 | tf_op jit(solution)/shard_map/ppermute | solution.py:241
  352.7 4.4 reshape.434
  358.5 2.9 reshape.435
  361.4 2.2 convert_element_type.256
  363.6 4.4 reshape.436
  369.4 2.2 reshape.437
  372.8 19.9 %all_to_all.21 = bf16[8,64,1280]{2,1,0:T(8,128)(2,1)} all-to-all(bf16[8,64,1280]{2,1,0:T(8,128)(2,1)S(1)} %pad_maximum_fusion.3), channel_id=1, replica_groups=mesh['fsdp'=4,'z'=4,'core'=2] {'fsdp','core'}, dimensions={0} | all-to-all | bytes 2621440 | tf_op jit(solution)/shard_map/all_to_all | solution.py:300
  392.9 1.7 multiply_reduce_fusion
  396.6 33.1 %all-gather.20.cloned.1.call-done = bf16[640,2048]{1,0:T(8,128)(2,1)} async-done(((bf16[160,2048]{1,0:T(8,128)(2,1)}), bf16[640,2048]{1,0:T(8,128)(2,1)}) %all-gather.20.cloned.1.call-update) | async-done | bytes 2621456 | tf_op jit(solution)/shard_map/all_gather | solution.py:283
  429.7 56.0 %all-gather.22.cloned.1.call-done = bf16[2,1024,2048]{2,1,0:T(8,128)(2,1)} async-done(((bf16[2,128,2048]{2,1,0:T(8,128)(2,1)}), bf16[2,1024,2048]{2,1,0:T(8,128)(2,1)}) %all-gather.22.cloned.1.call-update) | async-done | bytes 8388624 | tf_op jit(solution)/shard_map/all_gather | solution.py:246
  485.7 11.2 fusion.43
  496.9 87.8 %all-gather.18.cloned.1.call-done = bf16[4,512,1280]{2,1,0:T(8,128)(2,1)} async-done(((bf16[4,128,1280]{2,1,0:T(8,128)(2,1)}), bf16[4,512,1280]{2,1,0:T(8,128)(2,1)}) %all-gather.18.cloned.1.call-update) | async-done | bytes 5242896 | tf_op jit(solution)/shard_map/all_gather | solution.py:306
  584.7 56.1 %all-gather.16.cloned.1.call-done = bf16[2,1024,2048]{2,1,0:T(8,128)(2,1)} async-done(((bf16[2,128,2048]{2,1,0:T(8,128)(2,1)}), bf16[2,1024,2048]{2,1,0:T(8,128)(2,1)}) %all-gather.16.cloned.1.call-update) | async-done | bytes 8388624 | tf_op jit(solution)/shard_map/all_gather | solution.py:246
  640.8 10.5 fusion.7
  651.4 15.3 %fusion.6 = (bf16[2048,640]{0,1:T(8,128)(2,1)S(1)}, bf16[2048,640]{0,1:T(8,128)(2,1)}, bf16[2048,640]{0,1:T(8,128)(2,1)}) fusion(f32[2048,640]{0,1:T(8,128)} %fusion.43, f32[2048,640]{0,1:T(8,128)} %fusion.7, bf16[2048,2048]{1,0:T(8,128)(2,1)} %bitcast.130, bf16[2048,1280]{1,0:T(8,128)(2,1)S(1)} %bitcast.133), kind=kOutput, calls=%fused_computation.13 | convolution fusion | flops 5402787840 | bytes 29360128 | tf_op jit(solution)/shard_map/dot_general | solution.py:383
  666.7 16.0 %convolution_convert_fusion.1 = bf16[2048,2048]{1,0:T(8,128)(2,1)} fusion(bf16[2048,1280]{1,0:T(8,128)(2,1)S(1)} %bitcast.134, bf16[2048,640]{0,1:T(8,128)(2,1)} %get-tuple-element.29, bf16[2048,640]{0,1:T(8,128)(2,1)S(1)} %get-tuple-element.28), kind=kOutput, calls=%fused_computation.1 | convolution fusion | flops 10752098304 | bytes 18874368 | tf_op jit(solution)/shard_map/rf,df->rd/dot_general | solution.py:392
  682.8 71.4 %reduce-scatter.13.cloned.1.call-done = bf16[2,128,2048]{2,1,0:T(8,128)(2,1)} async-done(((bf16[2,1024,2048]{2,1,0:T(8,128)(2,1)}), bf16[2,128,2048]{2,1,0:T(8,128)(2,1)}) %reduce-scatter.13.cloned.1.call-update) | async-done | bytes 1048592 | tf_op jit(solution)/shard_map/reduce_scatter | solution.py:251
  754.2 2.0 fusion.25
  756.3 2.0 fusion.35
  758.3 16.6 %convolution_convert_fusion.4 = bf16[2048,1280]{1,0:T(8,128)(2,1)} fusion(bf16[2048,2048]{1,0:T(8,128)(2,1)} %bitcast.131, bf16[2048,640]{0,1:T(8,128)(2,1)} %get-tuple-element.29, bf16[2048,640]{0,1:T(8,128)(2,1)} %copy-done.27), kind=kOutput, calls=%fused_computation.4 | convolution fusion | flops 10750525440 | bytes 18874368 | tf_op jit(solution)/shard_map/rd,rf->df/dot_general | solution.py:402
  775.0 10.7 convolution_convert_fusion.7
  785.7 27.1 %all-gather.24.cloned.1.call-done = bf16[2,1024,2048]{2,1,0:T(8,128)(2,1)} async-done(((bf16[2,128,2048]{2,1,0:T(8,128)(2,1)}), bf16[2,1024,2048]{2,1,0:T(8,128)(2,1)}) %all-gather.24.cloned.1.call-update) | async-done | bytes 8388624 | tf_op jit(solution)/shard_map/all_gather | solution.py:246
  812.8 7.0 convolution_convert_fusion.9.g_ref
  819.8 44.5 %attn_bwd.1 = (bf16[2048,256]{1,0:T(8,128)(2,1)}, bf16[2048,256]{1,0:T(8,128)(2,1)}, bf16[2048,256]{1,0:T(8,128)(2,1)}, f32[4,2048]{1,0:T(4,128)}) custom-call(s32[2]{0:T(128)} %copy-done.18, bf16[2048,768]{1,0:T(8,128)(2,1)} %convolution_convert_fusion.5.q_ref.k_ref.v_ref, bf16[2048,768]{1,0:T(8,128)(2,1)} %convolution_convert_fusion.5.q_ref.k_ref.v_ref, ...), custom_call_target="tpu_custom_call" | custom-call | tf_op jit(solution)/shard_map/attn_bwd/pallas_call | solution.py:171
  867.8 9.1 convolution_convert_fusion
  877.0 11.6 convolution_convert_fusion.6
  888.7 11.3 convolution_convert_fusion.2
  900.0 10.3 reduce-scatter.21.cloned.1.call-done
  910.3 4.7 all-to-all-start.3
  915.1 7.0 convolution_convert_fusion.8
  922.2 42.2 %reduce-scatter.23.cloned.1.call-done = bf16[160,2048]{1,0:T(8,128)(2,1)} async-done(((bf16[640,2048]{1,0:T(8,128)(2,1)}), bf16[160,2048]{1,0:T(8,128)(2,1)}) %reduce-scatter.23.cloned.1.call-update) | async-done | bytes 655376 | tf_op jit(solution)/shard_map/reduce_scatter | solution.py:290
  964.3 2.3 convert_element_type.299
  966.6 71.5 %reduce-scatter.15.cloned.1.call-done = bf16[2,128,2048]{2,1,0:T(8,128)(2,1)} async-done(((bf16[2,1024,2048]{2,1,0:T(8,128)(2,1)}), bf16[2,128,2048]{2,1,0:T(8,128)(2,1)}) %reduce-scatter.15.cloned.1.call-update) | async-done | bytes 1048592 | tf_op jit(solution)/shard_map/reduce_scatter | solution.py:251
  1038.2 1.9 fusion.29
  1040.0 61.6 %reduce-scatter.17.cloned.1.call-done = bf16[4,128,768]{2,1,0:T(8,128)(2,1)} async-done(((bf16[4,512,768]{2,1,0:T(8,128)(2,1)}), bf16[4,128,768]{2,1,0:T(8,128)(2,1)}) %reduce-scatter.17.cloned.1.call-update) | async-done | bytes 786448 | tf_op jit(solution)/shard_map/reduce_scatter | solution.py:312
  1101.6 4.7 all-to-all-start.2
  1106.3 69.4 %reduce-scatter.11.cloned.1.call-done = bf16[2,128,2048]{2,1,0:T(8,128)(2,1)} async-done(((bf16[2,1024,2048]{2,1,0:T(8,128)(2,1)}), bf16[2,128,2048]{2,1,0:T(8,128)(2,1)}) %reduce-scatter.11.cloned.1.call-update) | async-done | bytes 1048592 | tf_op jit(solution)/shard_map/reduce_scatter | solution.py:251
  1175.7 4.5 fusion.20
  1180.2 4.2 collective-permute-start.2
  1184.4 2.6 collective-permute-start.4
  1187.0 3.0 slice_convert_fusion
  1190.0 3.0 reshape.463
  1193.1 3.0 copy.58
  1196.0 4.7 reshape.458
  1200.7 2.9 reshape.464
  1203.6 3.0 copy.59
  1206.5 4.7 reshape.459
  1212.2 88.8 %reduce-scatter.19.cloned.1.call-done = bf16[64,2048]{1,0:T(8,128)(2,1)} async-done(((bf16[256,2048]{1,0:T(8,128)(2,1)}), bf16[64,2048]{1,0:T(8,128)(2,1)}) %reduce-scatter.19.cloned.1.call-update) | async-done | bytes 262160 | tf_op jit(solution)/shard_map/reduce_scatter | solution.py:290
  1301.0 1.8 convert_element_type.288
  1305.4 1.8 reshape.455
  1308.4 1.8 reshape.456
  1311.4 1.8 reshape.457
  1313.3 55.8 %all-reduce.1 = f32[32,160]{1,0:T(8,128)S(1)} all-reduce(f32[32,160]{1,0:T(8,128)S(1)} %pad_maximum_fusion.5), channel_id=6, replica_groups=mesh['fsdp'=4,'z'=4,'core'=2] {'fsdp','z','core'}, use_global_device_ids=true, to_apply=%region_10.11.clone | all-reduce | flops 5120 | bytes 40960
  1370.3 2.3 copy.78
  1372.6 2.3 copy.79
  (160 shorter events, 31.3 us)
Async XLA Ops:
  7.2 2.2 copy-start.8
  7.2 171.8 %all-gather.12.cloned.1.call-start = ((), (), s32[]{:S(2)}) async-start(), calls=%async_computation.13 | async-start | bytes 3932160 | tf_op jit(solution)/shard_map/all_gather | solution.py:306
  8.9 1.6 copy-start.9
  11.1 14.8 %copy-start.24 = (bf16[2,128,2048]{2,1,0:T(8,128)(2,1)S(1)}, bf16[2,128,2048]{2,1,0:T(8,128)(2,1)}, u32[]{:S(2)}) copy-start(bf16[2,128,2048]{2,1,0:T(8,128)(2,1)} %param.14) | copy-start | bytes 3145732
  11.2 19.3 %copy-start.25 = (f32[32]{0:T(128)S(1)}, f32[32]{0:T(128)}, u32[]{:S(2)}) copy-start(f32[32]{0:T(128)} %param.19) | copy-start | bytes 388
  11.2 19.4 %copy-start.20 = (f32[64]{0:T(128)S(1)}, f32[64]{0:T(128)}, u32[]{:S(2)}) copy-start(f32[64]{0:T(128)} %param.24) | copy-start | bytes 772
  11.2 19.4 %copy-start.21 = (f32[64]{0:T(128)S(1)}, f32[64]{0:T(128)}, u32[]{:S(2)}) copy-start(f32[64]{0:T(128)} %param.18) | copy-start | bytes 772
  25.9 148.4 %copy-start.26 = (s32[2]{0:T(128)S(1)}, s32[2]{0:T(128)}, u32[]{:S(2)}) copy-start(s32[2]{0:T(128)} %param.16) | copy-start | bytes 28
  25.9 150.4 %copy-start.10 = (f32[64,2048]{1,0:T(8,128)S(1)}, f32[64,2048]{1,0:T(8,128)}, u32[]{:S(2)}) copy-start(f32[64,2048]{1,0:T(8,128)} %param.23) | copy-start | bytes 1572868
  25.9 205.3 %all-gather.10.cloned.1.call-start = ((), (), s32[]{:S(2)}) async-start(), calls=%async_computation.12 | async-start | bytes 9437184 | tf_op jit(solution)/shard_map/all_gather | solution.py:246
  26.0 146.7 %collective-permute-start = (bf16[2,128,2048]{2,1,0:T(8,128)(2,1)S(1)}, bf16[2,128,2048]{2,1,0:T(8,128)(2,1)S(1)}, u32[]{:S(2)}, u32[]{:S(2)}) collective-permute-start(bf16[2,128,2048]{2,1,0:T(8,128)(2,1)S(1)} %copy-done.24), channel_id=1, source_target_pairs={{0,0},{2,8},{4,16},{6,24},{8,2},{10,10},{12,18},{14,26},{16,4},{18... | collective-permute-start | bytes 3145736 | tf_op jit(solution)/shard_map/ppermute | solution.py:241
  172.7 4.4 copy-start.12
  173.0 4.3 copy-start.15
  173.0 4.5 copy-start.17
  174.3 94.2 %all-gather.14.cloned.1.call-start = ((), (), s32[]{:S(2)}) async-start(), calls=%async_computation.14 | async-start | bytes 1310720 | tf_op jit(solution)/shard_map/all_gather | solution.py:283
  174.3 68.1 %collective-permute-start.1 = (s32[2]{0:T(128)S(1)}, s32[2]{0:T(128)S(1)}, u32[]{:S(2)}, u32[]{:S(2)}) collective-permute-start(s32[2]{0:T(128)S(1)} %copy-done.26), channel_id=1, source_target_pairs={{0,0},{2,8},{4,16},{6,24},{8,2},{10,10},{12,18},{14,26},{16,4},{18... | collective-permute-start | bytes 32 | tf_op jit(solution)/shard_map/ppermute | solution.py:241
  177.0 215.8 %reduce-scatter.9.cloned.1.call-start = ((), (), s32[]{:S(2)}) async-start(), calls=%async_computation.15 | async-start | bytes 9437184 | tf_op jit(solution)/shard_map/reduce_scatter | solution.py:251
  177.8 64.6 %copy-start.2 = (pred[2047,32]{1,0:T(8,128)(4,1)}, pred[2047,32]{1,0:T(8,128)(4,1)S(1)}, u32[]{:S(2)}) copy-start(pred[2047,32]{1,0:T(8,128)(4,1)S(1)} %iota_compare_fusion) | copy-start | bytes 196516
  242.4 0.5 copy-start.18
  275.7 1.3 copy-start.4
  275.7 6.4 copy-start.19
  275.7 154.0 %all-gather.20.cloned.1.call-start = ((), (), s32[]{:S(2)}) async-start(), calls=%async_computation.18 | async-start | bytes 3276800 | tf_op jit(solution)/shard_map/all_gather | solution.py:283
  277.9 73.8 %copy-start.5 = (f32[64,5120]{1,0:T(8,128)S(1)}, f32[64,5120]{1,0:T(8,128)}, u32[]{:S(2)}) copy-start(f32[64,5120]{1,0:T(8,128)} %param.25) | copy-start | bytes 3932164
  278.0 207.7 %all-gather.22.cloned.1.call-start = ((), (), s32[]{:S(2)}) async-start(), calls=%async_computation.20 | async-start | bytes 9437184 | tf_op jit(solution)/shard_map/all_gather | solution.py:246
  278.0 72.3 %collective-permute-start.3 = (bf16[2,128,2048]{2,1,0:T(8,128)(2,1)}, bf16[2,128,2048]{2,1,0:T(8,128)(2,1)S(1)}, u32[]{:S(2)}, u32[]{:S(2)}) collective-permute-start(bf16[2,128,2048]{2,1,0:T(8,128)(2,1)} %param.15), channel_id=1, source_target_pairs={{0,0},{2,8},{4,16},{6,24},{8,2},{10,10},{12,18},{14,26},{16,4},{18... | collective-permute-start | bytes 3145736 | tf_op jit(solution)/shard_map/ppermute | solution.py:241
  351.5 233.2 %all-gather.18.cloned.1.call-start = ((), (), s32[]{:S(2)}) async-start(), calls=%async_computation.17 | async-start | bytes 6553600 | tf_op jit(solution)/shard_map/all_gather | solution.py:306
  392.8 248.0 %all-gather.16.cloned.1.call-start = ((), (), s32[]{:S(2)}) async-start(), calls=%async_computation.16 | async-start | bytes 9437184 | tf_op jit(solution)/shard_map/all_gather | solution.py:246
  392.9 1.7 copy-start
  396.1 358.0 %reduce-scatter.13.cloned.1.call-start = ((), (), s32[]{:S(2)}) async-start(), calls=%async_computation.21 | async-start | bytes 9437184 | tf_op jit(solution)/shard_map/reduce_scatter | solution.py:251
  640.8 10.5 copy-start.22
  666.7 16.0 %copy-start.27 = (bf16[2048,640]{0,1:T(8,128)(2,1)}, bf16[2048,640]{0,1:T(8,128)(2,1)S(1)}, u32[]{:S(2)}) copy-start(bf16[2048,640]{0,1:T(8,128)(2,1)S(1)} %get-tuple-element.28) | copy-start | bytes 7864324
  682.7 130.0 %all-gather.24.cloned.1.call-start = ((), (), s32[]{:S(2)}) async-start(), calls=%async_computation.22 | async-start | bytes 9437184 | tf_op jit(solution)/shard_map/all_gather | solution.py:246
  754.2 2.1 copy-start.1
  758.2 152.1 %reduce-scatter.21.cloned.1.call-start = ((), (), s32[]{:S(2)}) async-start(), calls=%async_computation.26 | async-start | bytes 6553600 | tf_op jit(solution)/shard_map/reduce_scatter | solution.py:312
  774.9 189.4 %reduce-scatter.23.cloned.1.call-start = ((), (), s32[]{:S(2)}) async-start(), calls=%async_computation.27 | async-start | bytes 3276800 | tf_op jit(solution)/shard_map/reduce_scatter | solution.py:290
  785.7 252.5 %reduce-scatter.15.cloned.1.call-start = ((), (), s32[]{:S(2)}) async-start(), calls=%async_computation.23 | async-start | bytes 9437184 | tf_op jit(solution)/shard_map/reduce_scatter | solution.py:251
  864.3 1.6 copy-start.7
  864.3 2.0 copy-start.6
  865.8 2.0 copy-start.23
  867.8 9.1 copy-start.11
  876.9 224.7 %reduce-scatter.17.cloned.1.call-start = ((), (), s32[]{:S(2)}) async-start(), calls=%async_computation.24 | async-start | bytes 3932160 | tf_op jit(solution)/shard_map/reduce_scatter | solution.py:312
  888.7 287.1 %reduce-scatter.11.cloned.1.call-start = ((), (), s32[]{:S(2)}) async-start(), calls=%async_computation.19 | async-start | bytes 9437184 | tf_op jit(solution)/shard_map/reduce_scatter | solution.py:251
  910.3 129.7 %all-to-all-start.3 = ((bf16[8,64,1280]{2,1,0:T(8,128)(2,1)}), bf16[8,64,1280]{2,1,0:T(8,128)(2,1)}, u32[]{:S(2)}, u32[]{:S(2)}) async-start(bf16[8,64,1280]{2,1,0:T(8,128)(2,1)} %bitcast.115), calls=%async_computation.10 | async-start | bytes 2621440 | tf_op jit(solution)/shard_map/all_to_all | solution.py:320
  915.1 386.0 %reduce-scatter.19.cloned.1.call-start = ((), (), s32[]{:S(2)}) async-start(), calls=%async_computation.25 | async-start | bytes 1310720 | tf_op jit(solution)/shard_map/reduce_scatter | solution.py:290
  922.1 116.0 %copy-start.13 = (f32[2048]{0:T(1024)S(1)}, f32[2048]{0:T(1024)}, u32[]{:S(2)}) copy-start(f32[2048]{0:T(1024)} %copy-done.12) | copy-start | bytes 24580
  922.1 116.0 %copy-start.16 = (f32[2,128]{1,0:T(2,128)S(1)}, f32[2,128]{1,0:T(2,128)}, u32[]{:S(2)}) copy-start(f32[2,128]{1,0:T(2,128)} %copy-done.15) | copy-start | bytes 3076
  1101.6 201.2 %all-to-all-start.2 = ((bf16[8,64,768]{2,1,0:T(8,128)(2,1)}), bf16[8,64,768]{2,1,0:T(8,128)(2,1)}, u32[]{:S(2)}, u32[]{:S(2)}) async-start(bf16[8,64,768]{2,1,0:T(8,128)(2,1)} %bitcast.118), calls=%async_computation.7 | async-start | bytes 1572864 | tf_op jit(solution)/shard_map/all_to_all | solution.py:320
  1180.2 190.1 %collective-permute-start.2 = (bf16[2,128,2048]{2,1,0:T(8,128)(2,1)}, bf16[2,128,2048]{2,1,0:T(8,128)(2,1)}, u32[]{:S(2)}, u32[]{:S(2)}) collective-permute-start(bf16[2,128,2048]{2,1,0:T(8,128)(2,1)} %get-tuple-element.32), channel_id=1, source_target_pairs={{0,0},{2,8},{4,16},{6,24},{8,2},{10,10},{12,18},{14,26},{16,4},{18... | collective-permute-start | bytes 3145736 | tf_op jit(solution)/shard_map/ppermute | solution.py:241
  1184.4 185.9 %collective-permute-start.4 = (bf16[2,128,2048]{2,1,0:T(8,128)(2,1)}, bf16[2,128,2048]{2,1,0:T(8,128)(2,1)}, u32[]{:S(2)}, u32[]{:S(2)}) collective-permute-start(bf16[2,128,2048]{2,1,0:T(8,128)(2,1)} %get-tuple-element.31), channel_id=1, source_target_pairs={{0,0},{2,8},{4,16},{6,24},{8,2},{10,10},{12,18},{14,26},{16,4},{18... | collective-permute-start | bytes 3145736 | tf_op jit(solution)/shard_map/ppermute | solution.py:241
  1206.5 4.8 copy-start.3
  1206.5 4.8 copy-start.14
Sparse Core Ops, SparseCore 0:
  26.0 121.9 all-gather.11
  174.4 56.8 all-gather.9
  233.4 28.3 all-gather.13
  275.8 97.7 reduce-scatter.8
  375.1 54.4 all-gather.19
  432.2 53.4 all-gather.21
  487.3 97.3 all-gather.17
  587.3 53.4 all-gather.15
  682.9 71.2 reduce-scatter.12
  758.4 54.3 all-gather.23
  815.1 95.1 reduce-scatter.20
  912.5 51.7 reduce-scatter.22
  967.8 70.3 reduce-scatter.14
  1040.4 61.1 reduce-scatter.16
  1105.3 70.3 reduce-scatter.10
  1177.9 123.1 reduce-scatter.18

commit v2 on v1

--- a/solution.py
+++ b/solution.py
@@ -94,16 +94,43 @@
         compiler_params=pltpu.CompilerParams(
             dimension_semantics=("arbitrary", "arbitrary"), vmem_limit_bytes=56 * 1024 * 1024
         ),
+        cost_estimate=estimate(26),
         name="attn_fwd",
     )(lens, qkv, qkv, qkv, offset_bias)
 
 
 def attn_bwd_kernel(
-    heads, head_dim, block, length, lens_ref, q_ref, k_ref, v_ref, g_ref, lse_ref, bias_ref,
-    dq_ref, dk_ref, dv_ref, dbias_ref, skew_ref, kt_ref, vt_ref, acc_ref, dkt_ref, dvt_ref,
+    heads, head_dim, block, length, seqs, fs, lens_ref, q_ref, k_ref, v_ref, g_ref, lse_ref, bias_ref,
+    *refs,
 ):
     seq, blk = pl.program_id(0), pl.program_id(1)
-    last_seq, last_blk = pl.num_programs(0) - 1, pl.num_programs(1) - 1
+    blocks = length // block
+    last_seq, last_blk = seqs - 1, blocks - 1
+    if fs:
+        a_ref, w_ref, dq_ref, dk_ref, dv_ref, dbias_ref, sum_ref = refs[:7]
+        refs = refs[7:]
+        plane = Plane(fs)
+
+        def partial(slot, cols):
+            return dotf(a_ref[:, slot].reshape(-1, a_ref.shape[3]), w_ref[:, cols])
+
+        actions = [plane.barrier] + scatter_actions(
+            plane, partial, 256, sum_ref.shape[2], sum_ref, refs[6:]
+        )
+        grid_step = seq * blocks + blk
+        steps = seqs * blocks
+        for step in range(steps):
+            todo = actions[len(actions) * step // steps : len(actions) * (step + 1) // steps]
+
+            @pl.when(grid_step == step)
+            def _(todo=todo):
+                for action in todo:
+                    action()
+
+    else:
+        dq_ref, dk_ref, dv_ref, dbias_ref = refs[:4]
+        refs = refs[4:]
+    skew_ref, kt_ref, vt_ref, acc_ref, dkt_ref, dvt_ref = refs[:6]
     width = heads * head_dim
 
     @pl.when((seq == 0) & (blk == 0))
@@ -162,52 +189,823 @@
             dbias_ref[h : h + 1, :] = total
 
 
-def attn_bwd(qkv, grad, lse, offset_bias, lens, heads, head_dim, seqs, block=256):
+def attn_bwd(
+    qkv, grad, lse, offset_bias, lens, heads, head_dim, seqs, block=256, product=None,
+    collective_id=None,
+):
     rows, width3 = qkv.shape
     width = width3 // 3
     length = rows // seqs
     block = min(block, length)
     blocks = length // block
+    in_specs = [
+        pl.BlockSpec(memory_space=pltpu.SMEM),
+        pl.BlockSpec((block, width), lambda s, i: (s * blocks + i, 0)),
+        pl.BlockSpec((length, width), lambda s, i: (s, 1)),
+        pl.BlockSpec((length, width), lambda s, i: (s, 2)),
+        pl.BlockSpec((block, width), lambda s, i: (s * blocks + i, 0)),
+        pl.BlockSpec((block, 128), lambda s, i: (s * blocks + i, 0)),
+        pl.BlockSpec((heads, 2 * length), lambda s, i: (0, 0)),
+    ]
+    out_specs = [
+        pl.BlockSpec((block, width), lambda s, i: (s * blocks + i, 0)),
+        pl.BlockSpec((length, width), lambda s, i: (s, 0)),
+        pl.BlockSpec((length, width), lambda s, i: (s, 0)),
+        pl.BlockSpec((heads, 2 * length), lambda s, i: (0, 0)),
+    ]
+    out_shape = [
+        jax.ShapeDtypeStruct((rows, width), jnp.bfloat16),
+        jax.ShapeDtypeStruct((rows, width), jnp.bfloat16),
+        jax.ShapeDtypeStruct((rows, width), jnp.bfloat16),
+        jax.ShapeDtypeStruct((heads, 2 * length), jnp.float32),
+    ]
+    scratch = [
+        pltpu.VMEM((heads, block, 2 * length - block), jnp.float32),
+        pltpu.VMEM((width, length), jnp.bfloat16),
+        pltpu.VMEM((width, length), jnp.bfloat16),
+        pltpu.VMEM((heads, block, 2 * length - block), jnp.float32),
+        pltpu.VMEM((width, length), jnp.float32),
+        pltpu.VMEM((width, length), jnp.float32),
+    ]
+    args = [lens, qkv, qkv, qkv, grad, lse, offset_bias]
+    fs = 0
+    if product is not None:
+        fs = lax.axis_size("fsdp")
+        a, w = product
+        a = a.reshape(seqs, 2 * fs, -1, a.shape[1])
+        args += [a, w]
+        in_specs += [vmem(), vmem()]
+        out_specs.append(vmem())
+        out_shape.append(jax.ShapeDtypeStruct((seqs, a.shape[2], w.shape[1]), jnp.float32))
+        scratch += scatter_scratch(fs, a.shape[2], w.shape[1])
+    out = pl.pallas_call(
+        functools.partial(attn_bwd_kernel, heads, head_dim, block, length, seqs, fs),
+        grid=(seqs, blocks),
+        in_specs=in_specs,
+        out_specs=out_specs,
+        out_shape=out_shape,
+        scratch_shapes=scratch,
+        compiler_params=pltpu.CompilerParams(
+            dimension_semantics=("arbitrary", "arbitrary"), vmem_limit_bytes=62 * 1024 * 1024,
+            collective_id=collective_id, has_side_effects=fs > 0,
+        ),
+        cost_estimate=estimate(50),
+        name="attn_bwd",
+    )(*args)
+    if product is not None:
+        out = list(out[:4]) + [out[4].reshape(-1, w.shape[1])]
+    return out
+
+MESH_ID = pl.DeviceIdType.MESH
+MIB = 1024 * 1024
+
+
+def remote_copy(src, dst, send_sem, recv_sem, device):
+    return pltpu.make_async_remote_copy(
+        src_ref=src, dst_ref=dst, send_sem=send_sem, recv_sem=recv_sem, device_id=device,
+        device_id_type=MESH_ID,
+    )
+
+
+def landed(ref, sem):
+    pltpu.make_async_copy(ref, ref, sem).wait()
+
+
+def estimate(us):
+    return pl.CostEstimate(flops=int(us * 1.1e9), bytes_accessed=int(us * 1e6), transcendentals=0)
+
+
+def flip(f, bits):
+    k = 1
+    while k <= bits:
+        if bits & k:
+            f = f + (1 - 2 * (lax.rem(lax.div(f, k), 2))) * k
+        k *= 2
+    return f
+
+
+class Plane:
+    def __init__(self, fs):
+        self.fs = fs
+        self.f, self.z, self.c = (lax.axis_index(a) for a in ("fsdp", "z", "core"))
+        self.bits = [1 << i for i in range(fs.bit_length() - 1)]
+        self.orders = [self.bits, self.bits[::-1]]
+        self.steps = len(self.bits)
+
+    def peer(self, bit):
+        return (flip(self.f, bit), self.z, self.c)
+
+    def mate(self):
+        return (self.f, self.z, 1 - self.c)
+
+    def slot(self, rel, other=False):
+        c = 1 - self.c if other else self.c
+        return flip(self.f, rel) * 2 + c
+
+    def barrier(self):
+        bar = pltpu.get_barrier_semaphore()
+        for dev in [self.mate()] + [self.peer(b) for b in self.bits]:
+            pl.semaphore_signal(bar, inc=1, device_id=dev, device_id_type=MESH_ID)
+        pl.semaphore_wait(bar, 1 + self.steps)
+
+
+def gather_sems(fs):
+    steps = fs.bit_length() - 1
+    return [
+        pltpu.SemaphoreType.DMA((2, steps, fs)),
+        pltpu.SemaphoreType.DMA((2, fs)),
+        pltpu.SemaphoreType.DMA((2, fs)),
+        pltpu.SemaphoreType.DMA((2, fs)),
+    ]
+
+
+def run_gather(plane, x_ref, buf_ref, sems, consume):
+    send, recv, mate_send, mate_recv = sems
+    started = []
+
+    def remote(*args):
+        started.append(remote_copy(*args))
+        started[-1].start()
+
+    def source(p, rel):
+        return x_ref.at[p] if rel == 0 else buf_ref.at[p, plane.slot(rel)]
+
+    def to_mate(p, rel):
+        remote(
+            source(p, rel), buf_ref.at[p, plane.slot(rel)], mate_send.at[p, rel],
+            mate_recv.at[p, rel], plane.mate(),
+        )
+
+    def to_peer(p, step, rel):
+        bit = plane.orders[p][step]
+        remote(
+            source(p, rel), buf_ref.at[p, plane.slot(rel)], send.at[p, step, rel],
+            recv.at[p, rel ^ bit], plane.peer(bit),
+        )
+
+    for step in range(plane.steps):
+        for p in range(2):
+            to_peer(p, step, 0)
+        if step == 0:
+            for p in range(2):
+                to_mate(p, 0)
+    for p in range(2):
+        consume(p, plane.slot(0), x_ref.at[p])
+
+    def arrived(p, rel):
+        landed(buf_ref.at[p, plane.slot(rel)], recv.at[p, rel])
+
+    def mate_arrived(p, rel):
+        ref = buf_ref.at[p, plane.slot(rel, True)]
+        landed(ref, mate_recv.at[p, rel])
+        consume(p, plane.slot(rel, True), ref)
+
+    have = [[0], [0]]
+    pending = [(0, 0), (1, 0)]
+    for step in range(plane.steps):
+        fresh = []
+        for i in range(len(have[0])):
+            for p in range(2):
+                rel = have[p][i] ^ plane.orders[p][step]
+                fresh.append((p, rel))
+        for p, rel in pending:
+            mate_arrived(p, rel)
+        for p, rel in fresh:
+            arrived(p, rel)
+            to_mate(p, rel)
+            for later in range(step + 1, plane.steps):
+                to_peer(p, later, rel)
+            consume(p, plane.slot(rel), buf_ref.at[p, plane.slot(rel)])
+        for p in range(2):
+            have[p] = have[p] + [rel for q, rel in fresh if q == p]
+        pending = fresh
+    for p, rel in pending:
+        mate_arrived(p, rel)
+    for cp in started:
+        cp.wait_send()
+
+
+def scatter_scratch(fs, b, width):
+    return [
+        pltpu.VMEM((2, fs, b, width), jnp.bfloat16),
+        pltpu.VMEM((2, fs, b, width), jnp.bfloat16),
+        pltpu.VMEM((2, fs // 2, b, width), jnp.float32),
+        pltpu.VMEM((2, fs, b, width), jnp.bfloat16),
+        pltpu.VMEM((2, fs - 1, b, width), jnp.bfloat16),
+        pltpu.SemaphoreType.DMA((fs,)),
+        pltpu.SemaphoreType.DMA((fs,)),
+        pltpu.SemaphoreType.DMA((2, fs)),
+        pltpu.SemaphoreType.DMA((2, fs - 1)),
+    ]
+
+
+def scatter_actions(plane, partial, tile, width, out_ref, scratch):
+    give, got, total, outbox, inbox, give_sem, got_sem, send, recv = scratch
+    b = out_ref.shape[1]
+    rels = sorted(range(plane.fs), key=lambda r: (-bin(r).count("1"), r))
+    tiles = width // tile
+
+    def each_tile(body):
+        def one(j, carry):
+            body(pl.ds(pl.multiple_of(j * tile, tile), tile))
+            return carry
+
+        lax.fori_loop(0, tiles, one, 0)
+
+    def leaves(p, rel):
+        for step, bit in enumerate(plane.orders[p]):
+            if rel & bit:
+                return step
+        return plane.steps
+
+    def place(p, step, rel):
+        kept = [r for r in range(plane.fs) if leaves(p, r) > step]
+        return plane.fs - 2 * len(kept) + kept.index(rel)
+
+    def held(p, rel):
+        return [r for r in range(plane.fs) if leaves(p, r) > 0].index(rel)
+
+    def to_peer(p, rel):
+        step = leaves(p, rel)
+        bit = plane.orders[p][step]
+        at = place(p, step, rel ^ bit)
+        return remote_copy(
+            outbox.at[p, rel], inbox.at[p, at], send.at[p, rel], recv.at[p, at], plane.peer(bit)
+        )
+
+    def to_mate(rel):
+        return remote_copy(
+            give.at[:, rel], got.at[:, rel], give_sem.at[rel], got_sem.at[rel], plane.mate()
+        )
+
+    def give_part(rel):
+        theirs = plane.slot(rel, True)
+
+        def body(cols):
+            part = partial(theirs, cols).astype(jnp.bfloat16)
+            give[0, rel, :, cols] = part[:b]
+            give[1, rel, :, cols] = part[b:]
+
+        each_tile(body)
+        to_mate(rel).start()
+
+    def own_part(rel):
+        mine = plane.slot(rel)
+        landed(got.at[:, rel], got_sem.at[rel])
+
+        def body(cols):
+            part = partial(mine, cols)
+            for p in range(2):
+                here = part[p * b : (p + 1) * b] + got[p, rel, :, cols].astype(jnp.float32)
+                if leaves(p, rel) == 0:
+                    outbox[p, rel, :, cols] = here.astype(jnp.bfloat16)
+                else:
+                    total[p, held(p, rel), :, cols] = here
+
+        each_tile(body)
+        for p in range(2):
+            if leaves(p, rel) == 0:
+                to_peer(p, rel).start()
+
+    def add_part(step, rel, p):
+        at = place(p, step, rel)
+        landed(inbox.at[p, at], recv.at[p, at])
+        sends = leaves(p, rel) == step + 1
+
+        def body(cols):
+            here = total[p, held(p, rel), :, cols] + inbox[p, at, :, cols].astype(jnp.float32)
+            if step + 1 == plane.steps:
+                out_ref[p, :, cols] = here
+            elif sends:
+                outbox[p, rel, :, cols] = here.astype(jnp.bfloat16)
+            else:
+                total[p, held(p, rel), :, cols] = here
+
+        each_tile(body)
+        if sends and step + 1 < plane.steps:
+            to_peer(p, rel).start()
+
+    def close():
+        for rel in rels:
+            to_mate(rel).wait_send()
+            for p in range(2):
+                if leaves(p, rel) < plane.steps:
+                    to_peer(p, rel).wait_send()
+
+    actions = [functools.partial(give_part, rels[0])]
+    for i, rel in enumerate(rels):
+        if i + 1 < len(rels):
+            actions.append(functools.partial(give_part, rels[i + 1]))
+        actions.append(functools.partial(own_part, rel))
+    for step in range(plane.steps):
+        for rel in rels:
+            for p in range(2):
+                if leaves(p, rel) > step:
+                    actions.append(functools.partial(add_part, step, rel, p))
+    return actions + [close]
+
+
+def vmem():
+    return pl.BlockSpec(memory_space=pltpu.VMEM)
+
+
+def anywhere():
+    return pl.BlockSpec(memory_space=pl.ANY)
+
+
+def plane_params(collective_id, limit=58):
+    return pltpu.CompilerParams(
+        collective_id=collective_id, has_side_effects=True, vmem_limit_bytes=limit * MIB
+    )
+
+
+def gather_kernel(fs, x_ref, out_ref, *sems):
+    plane = Plane(fs)
+    plane.barrier()
+    own_sem = sems[4]
+    own = pltpu.make_async_copy(x_ref, out_ref.at[:, plane.slot(0)], own_sem)
+    own.start()
+    run_gather(plane, x_ref, out_ref, sems[:4], lambda p, slot, ref: None)
+    own.wait()
+
+
+def plane_gather(x, seqs, collective_id):
+    fs = lax.axis_size("fsdp")
+    x = x.reshape(seqs, -1, x.shape[1])
+    _, b, width = x.shape
+    full = pl.pallas_call(
+        functools.partial(gather_kernel, fs),
+        out_shape=jax.ShapeDtypeStruct((seqs, 2 * fs, b, width), x.dtype),
+        in_specs=[vmem()],
+        out_specs=anywhere(),
+        scratch_shapes=gather_sems(fs) + [pltpu.SemaphoreType.DMA],
+        compiler_params=plane_params(collective_id),
+        cost_estimate=estimate(45),
+        name="plane_gather",
+    )(x)
+    return full.reshape(-1, width)
+
+
+def gather_dot_kernel(fs, dims, tile, x_ref, w_ref, full_ref, y_ref, buf_ref, *sems):
+    plane = Plane(fs)
+    plane.barrier()
+    keep_sem = sems[4]
+    columns = y_ref.shape[3]
+    kept = []
+
+    def consume(p, slot, ref):
+        cp = pltpu.make_async_copy(ref, full_ref.at[p, slot], keep_sem.at[len(kept)])
+        cp.start()
+        kept.append(cp)
+
+        def one(j, carry):
+            cols = pl.ds(pl.multiple_of(j * tile, tile), tile)
+            w = w_ref[:, cols] if dims == NN else w_ref[cols, :]
+            y_ref[p, slot, :, cols] = dotf(ref[...], w, dims).astype(y_ref.dtype)
+            return carry
+
+        lax.fori_loop(0, columns // tile, one, 0)
+
+    run_gather(plane, x_ref, buf_ref, sems[:4], consume)
+    for cp in kept:
+        cp.wait()
+
+
+def plane_gather_dot(x, w, dims, seqs, collective_id):
+    fs = lax.axis_size("fsdp")
+    x = x.reshape(seqs, -1, x.shape[1])
+    _, b, width = x.shape
+    columns = w.shape[1] if dims == NN else w.shape[0]
+    tile = math.gcd(columns, 256)
+    full, y = pl.pallas_call(
+        functools.partial(gather_dot_kernel, fs, dims, tile),
+        out_shape=[
+            jax.ShapeDtypeStruct((seqs, 2 * fs, b, width), x.dtype),
+            jax.ShapeDtypeStruct((seqs, 2 * fs, b, columns), jnp.bfloat16),
+        ],
+        in_specs=[vmem(), vmem()],
+        out_specs=[anywhere(), vmem()],
+        scratch_shapes=[pltpu.VMEM((seqs, 2 * fs, b, width), x.dtype)]
+        + gather_sems(fs)
+        + [pltpu.SemaphoreType.DMA((seqs * 2 * fs,))],
+        compiler_params=plane_params(collective_id),
+        cost_estimate=estimate(45),
+        name="plane_gather_dot",
+    )(x, w)
+    return full.reshape(-1, width), y.reshape(-1, columns)
+
+
+class Swap:
+    def __init__(self, x_ref, out_ref, scratch):
+        self.x_ref, self.out_ref = x_ref, out_ref
+        self.relay, self.d_sem, self.in_send, self.in_recv, self.on_send, self.on_recv = scratch
+        self.f, self.z, self.c = (lax.axis_index(a) for a in ("fsdp", "z", "core"))
+        self.zs = self.relay.shape[0]
+
+    @staticmethod
+    def scratch(zs, b, width):
+        dma = pltpu.SemaphoreType.DMA
+        return [
+            pltpu.VMEM((zs, b, width), jnp.bfloat16), dma((2,)), dma, dma((zs,)), dma((zs,)), dma
+        ]
+
+    def straight(self):
+        return remote_copy(
+            self.x_ref.at[0], self.out_ref.at[0], self.d_sem.at[0], self.d_sem.at[1],
+            (self.z, self.f, self.c),
+        )
+
+    def inward(self):
+        return remote_copy(
+            self.x_ref.at[1], self.relay.at[self.f], self.in_send, self.in_recv.at[self.f],
+            (self.z, self.z, self.c),
+        )
+
+    def onward(self, source):
+        return remote_copy(
+            self.relay.at[source], self.out_ref.at[1], self.on_send.at[source], self.on_recv,
+            (self.f, source, self.c),
+        )
+
+    def own(self):
+        return pltpu.make_async_copy(self.x_ref, self.out_ref, self.d_sem.at[0])
+
+    def start(self):
+        @pl.when(self.f != self.z)
+        def _():
+            self.inward().start()
+            self.straight().start()
+
+        @pl.when(self.f == self.z)
+        def _():
+            self.own().start()
+
+    def hand_on(self):
+        @pl.when(self.f == self.z)
+        def _():
+            for source in range(self.zs):
+
+                @pl.when(source != self.z)
+                def _(source=source):
+                    landed(self.relay.at[source], self.in_recv.at[source])
+                    self.onward(source).start()
+
+    def close(self):
+        @pl.when(self.f == self.z)
+        def _():
+            for source in range(self.zs):
+
+                @pl.when(source != self.z)
+                def _(source=source):
+                    self.onward(source).wait_send()
+
+            self.own().wait()
+
+        @pl.when(self.f != self.z)
+        def _():
+            self.inward().wait_send()
+            self.straight().wait_send()
+            landed(self.out_ref.at[0], self.d_sem.at[1])
+            landed(self.out_ref.at[1], self.on_recv)
+
+
+class Everyone:
+    def __init__(self, sizes):
+        self.fs, self.zs, self.cs = sizes
+        self.n = math.prod(sizes)
+        f, z, c = (lax.axis_index(a) for a in ("fsdp", "z", "core"))
+        self.me = (f * self.zs + z) * self.cs + c
+
+    def place(self, index):
+        zs, cs = self.zs, self.cs
+        return (lax.div(index, zs * cs), lax.rem(lax.div(index, cs), zs), lax.rem(index, cs))
+
+    def other(self, d):
+        return lax.rem(self.me + d, self.n)
+
+    def barrier(self):
+        bar = pltpu.get_barrier_semaphore()
+
+        def greet(d, carry):
+            pl.semaphore_signal(
+                bar, inc=1, device_id=self.place(self.other(d)), device_id_type=MESH_ID
+            )
+            return carry
+
+        lax.fori_loop(1, self.n, greet, 0)
+        pl.semaphore_wait(bar, self.n - 1)
+
+    def copy(self, d, x_ref, spread_out, slots, send, recv):
+        src = x_ref.at[self.other(d)] if spread_out else x_ref.at[0]
+        return remote_copy(
+            src, slots.at[self.me], send.at[d], recv.at[d], self.place(self.other(d))
+        )
+
+    def begin(self, x_ref, spread_out, slots, send, recv, own_sem):
+        def one(d, carry):
+            self.copy(d, x_ref, spread_out, slots, send, recv).start()
+            return carry
+
+        lax.fori_loop(1, self.n, one, 0)
+        src = x_ref.at[self.me] if spread_out else x_ref.at[0]
+        own = pltpu.make_async_copy(src, slots.at[self.me], own_sem)
+        own.start()
+        own.wait()
+
+    def finish(self, x_ref, spread_out, slots, send, recv):
+        def one(d, carry):
+            landed(slots.at[lax.rem(self.me + self.n - d, self.n)], recv.at[d])
+            self.copy(d, x_ref, spread_out, slots, send, recv).wait_send()
+            return carry
+
+        lax.fori_loop(1, self.n, one, 0)
+
+
+def dot_scatter_kernel(fs, zs, dims, tile, swaps, a_ref, w_ref, *refs):
+    plane = Plane(fs)
+    if swaps:
+        Everyone((fs, zs, 2)).barrier()
+        swap = Swap(refs[0], refs[2], refs[3:9])
+        out_ref, scratch = refs[1], refs[9:]
+    else:
+        plane.barrier()
+        out_ref, scratch = refs[0], refs[1:]
+
+    def partial(slot, cols):
+        a = a_ref[:, slot].reshape(-1, a_ref.shape[3])
+        return dotf(a, w_ref[:, cols] if dims == NN else w_ref[cols, :], dims)
+
+    actions = scatter_actions(plane, partial, tile, out_ref.shape[2], out_ref, scratch)
+    if swaps:
+        swap.start()
+    for i, action in enumerate(actions):
+        action()
+        if swaps and i == 2 * fs:
+            swap.hand_on()
+    if swaps:
+        swap.close()
+
+
+def plane_dot_scatter(a, w, dims, seqs, collective_id, swapped=None):
+    fs, zs = lax.axis_size("fsdp"), lax.axis_size("z")
+    a = a.reshape(seqs, 2 * fs, -1, a.shape[1])
+    b = a.shape[2]
+    width = w.shape[1] if dims == NN else w.shape[0]
+    out_shape = [jax.ShapeDtypeStruct((seqs, b, width), jnp.float32)]
+    args, scratch = [a, w], scatter_scratch(fs, b, width)
+    if swapped is not None:
+        out_shape.append(jax.ShapeDtypeStruct(swapped.shape, swapped.dtype))
+        args.append(swapped)
+        scratch = Swap.scratch(zs, b, width) + scratch
+    out = pl.pallas_call(
+        functools.partial(dot_scatter_kernel, fs, zs, dims, 256, swapped is not None),
+        out_shape=out_shape,
+        in_specs=[vmem()] * len(args),
+        out_specs=[vmem()] + [anywhere()] * (len(args) - 2),
+        scratch_shapes=scratch,
+        compiler_params=plane_params(collective_id),
+        cost_estimate=estimate(45),
+        name="plane_dot_scatter",
+    )(*args)
+    rows = out[0].reshape(-1, width)
+    return rows if swapped is None else (rows, out[1])
+
+
+GELU_C = math.sqrt(2.0 / math.pi)
+
+
+def gather_ffn_kernel(fs, x_ref, g_ref, wgu_ref, wd_ref, full_ref, h_ref, ggu_ref, buf_ref, *sems):
+    plane = Plane(fs)
+    plane.barrier()
+    keep_sem = sems[4]
+    ff = wd_ref.shape[0]
+    kept = []
+
+    def consume(p, slot, ref):
+        cp = pltpu.make_async_copy(ref, full_ref.at[p, slot], keep_sem.at[len(kept)])
+        cp.start()
+        kept.append(cp)
+        gate = dotf(ref[...], wgu_ref[:, :ff])
+        up = dotf(ref[...], wgu_ref[:, ff:])
+        grad_hidden = dotf(g_ref[p, slot], wd_ref[...], NT)
+        square = gate * gate
+        tanh = jnp.tanh(GELU_C * gate * (1.0 + 0.044715 * square))
+        half = 0.5 * (1.0 + tanh)
+        act = gate * half
+        slope = half + (0.5 * GELU_C) * gate * (1.0 - tanh * tanh) * (1.0 + 0.134145 * square)
+        h_ref[p, slot] = (act * up).astype(jnp.bfloat16)
+        ggu_ref[p, slot, :, :ff] = (grad_hidden * up * slope).astype(jnp.bfloat16)
+        ggu_ref[p, slot, :, ff:] = (grad_hidden * act).astype(jnp.bfloat16)
+
+    run_gather(plane, x_ref, buf_ref, sems[:4], consume)
+    for cp in kept:
+        cp.wait()
+
+
+def plane_gather_ffn(x, grad, w_gu, w_d, seqs, collective_id):
+    fs = lax.axis_size("fsdp")
+    x = x.reshape(seqs, -1, x.shape[1])
+    _, b, width = x.shape
+    ff = w_d.shape[0]
+    lead = (seqs, 2 * fs, b)
+    full, h, ggu = pl.pallas_call(
+        functools.partial(gather_ffn_kernel, fs),
+        out_shape=[
+            jax.ShapeDtypeStruct(lead + (width,), x.dtype),
+            jax.ShapeDtypeStruct(lead + (ff,), jnp.bfloat16),
+            jax.ShapeDtypeStruct(lead + (2 * ff,), jnp.bfloat16),
+        ],
+        in_specs=[vmem()] * 4,
+        out_specs=[anywhere(), vmem(), vmem()],
+        scratch_shapes=[pltpu.VMEM(lead + (width,), x.dtype)]
+        + gather_sems(fs)
+        + [pltpu.SemaphoreType.DMA((seqs * 2 * fs,))],
+        compiler_params=plane_params(collective_id),
+        cost_estimate=estimate(45),
+        name="plane_gather_ffn",
+    )(x, grad.reshape(lead + (width,)), w_gu, w_d)
+    return full.reshape(-1, width), h.reshape(-1, ff), ggu.reshape(-1, 2 * ff)
+
+def start_kernel(
+    sizes, small_ref, qkv_ref, gu_ref, tok_ref, cot_ref, o_ref, d_ref,
+    small_out, wqkv_ref, ggu_ref, x_ref, g_ref, o_out, d_out,
+    slots, s_send, s_recv, own_sem, q_send, q_recv, g_send, g_recv, line_send, line_recv,
+    *swap_scratch,
+):
+    fs, zs, cs = sizes
+    f, z, c = (lax.axis_index(a) for a in ("fsdp", "z", "core"))
+    me = f * cs + c
+    devices = fs * cs
+    rows = qkv_ref.shape[1]
+    everyone = Everyone(sizes)
+    everyone.barrier()
+    everyone.begin(small_ref, False, slots, s_send, s_recv, own_sem.at[0])
+    half = len(swap_scratch) // 2
+    swaps = [
+        Swap(tok_ref, x_ref, swap_scratch[:half]), Swap(cot_ref, g_ref, swap_scratch[half:])
+    ]
+
+    def block(out_ref, index, lead):
+        at = pl.ds(pl.multiple_of(lax.rem(index, cs) * rows, rows), rows)
+        if lead is None:
+            return out_ref.at[lax.div(index, cs), at]
+        return out_ref.at[lax.div(index, cs), lead, at]
+
+    def spread_copy(d, src_ref, out_ref, lead, send, recv):
+        to = lax.rem(me + d, devices)
+        return remote_copy(
+            src_ref.at[to], block(out_ref, me, lead), send.at[d], recv.at[d],
+            (lax.div(to, cs), z, lax.rem(to, cs)),
+        )
+
+    own_qkv = pltpu.make_async_copy(qkv_ref.at[me], block(wqkv_ref, me, z), own_sem.at[1])
+    own_gu = pltpu.make_async_copy(gu_ref.at[me], block(ggu_ref, me, None), own_sem.at[2])
+    later = [
+        pltpu.make_async_copy(o_ref, o_out, own_sem.at[3]),
+        pltpu.make_async_copy(d_ref, d_out, own_sem.at[4]),
+    ]
+    for copy in later:
+        copy.start()
+    own_qkv.start()
+    for d in range(1, devices):
+        spread_copy(d, qkv_ref, wqkv_ref, z, q_send, q_recv).start()
+    own_gu.start()
+
+    swaps[0].start()
+    own_qkv.wait()
+    for d in range(1, devices):
+        landed(block(wqkv_ref, lax.rem(me + devices - d, devices), z), q_recv.at[d])
+
+    def line(step, way):
+        source = lax.rem(z - way * step + zs, zs)
+        to = lax.rem(z + way + zs, zs)
+        k = 0 if way > 0 else 1
+        ref = wqkv_ref.at[:, source]
+        return remote_copy(ref, ref, line_send.at[k, step], line_recv.at[k, step], (f, to, c))
+
+    def sends(step, way):
+        if way > 0:
+            return (z >= step) & (z < zs - 1)
+        return (z < zs - step) & (z > 0)
+
+    def arrives(step, way):
+        return (z > step) if way > 0 else (z < zs - 1 - step)
+
+    def arrive(step, way):
+        k = 0 if way > 0 else 1
+        source = lax.rem(z - way * (step + 1) + zs, zs)
+        landed(wqkv_ref.at[:, source], line_recv.at[k, step])
+
+    for step in range(zs - 1):
+        for way in (1, -1):
+
+            @pl.when(sends(step, way))
+            def _(step=step, way=way):
+                line(step, way).start()
+
+        if step == 1:
+            swaps[1].start()
+        if step == 0:
+            for d in range(1, devices):
+                spread_copy(d, gu_ref, ggu_ref, None, g_send, g_recv).start()
+        for way in (1, -1):
+
+            @pl.when(arrives(step, way))
+            def _(step=step, way=way):
+                arrive(step, way)
+
+        if step < 2:
+            swaps[step].hand_on()
+
+    everyone.finish(small_ref, False, slots, s_send, s_recv)
+    small_out[...] = slots[...]
+    own_gu.wait()
+    for copy in later:
+        copy.wait()
+    for d in range(1, devices):
+        landed(block(ggu_ref, lax.rem(me + devices - d, devices), None), g_recv.at[d])
+    for d in range(1, devices):
+        spread_copy(d, qkv_ref, wqkv_ref, z, q_send, q_recv).wait_send()
+        spread_copy(d, gu_ref, ggu_ref, None, g_send, g_recv).wait_send()
+    for step in range(zs - 1):
+        for way in (1, -1):
+
+            @pl.when(sends(step, way))
+            def _(step=step, way=way):
+                line(step, way).wait_send()
+
+    for swap in swaps:
+        swap.close()
+
+
+def start(small, qkv_pieces, gu_pieces, tokens, cotangent, own_o, own_d, collective_id):
+    sizes = tuple(lax.axis_size(a) for a in ("fsdp", "z", "core"))
+    fs, zs, cs = sizes
+    n = math.prod(sizes)
+    devices, rows, qkv_cols = qkv_pieces.shape
+    dma = pltpu.SemaphoreType.DMA
     return pl.pallas_call(
-        functools.partial(attn_bwd_kernel, heads, head_dim, block, length),
-        grid_spec=pltpu.PrefetchScalarGridSpec(
-            num_scalar_prefetch=1,
-            grid=(seqs, blocks),
-            in_specs=[
-                pl.BlockSpec((block, width), lambda s, i, lens: (s * blocks + i, 0)),
-                pl.BlockSpec((length, width), lambda s, i, lens: (s, 1)),
-                pl.BlockSpec((length, width), lambda s, i, lens: (s, 2)),
-                pl.BlockSpec((block, width), lambda s, i, lens: (s * blocks + i, 0)),
-                pl.BlockSpec((block, 128), lambda s, i, lens: (s * blocks + i, 0)),
-                pl.BlockSpec((heads, 2 * length), lambda s, i, lens: (0, 0)),
-            ],
-            out_specs=[
-                pl.BlockSpec((block, width), lambda s, i, lens: (s * blocks + i, 0)),
-                pl.BlockSpec((length, width), lambda s, i, lens: (s, 0)),
-                pl.BlockSpec((length, width), lambda s, i, lens: (s, 0)),
-                pl.BlockSpec((heads, 2 * length), lambda s, i, lens: (0, 0)),
-            ],
-            scratch_shapes=[
-                pltpu.VMEM((heads, block, 2 * length - block), jnp.float32),
-                pltpu.VMEM((width, length), jnp.bfloat16),
-                pltpu.VMEM((width, length), jnp.bfloat16),
-                pltpu.VMEM((heads, block, 2 * length - block), jnp.float32),
-                pltpu.VMEM((width, length), jnp.float32),
-                pltpu.VMEM((width, length), jnp.float32),
-            ],
-        ),
+        functools.partial(start_kernel, sizes),
         out_shape=[
-            jax.ShapeDtypeStruct((rows, width), jnp.bfloat16),
-            jax.ShapeDtypeStruct((rows, width), jnp.bfloat16),
-            jax.ShapeDtypeStruct((rows, width), jnp.bfloat16),
-            jax.ShapeDtypeStruct((heads, 2 * length), jnp.float32),
+            jax.ShapeDtypeStruct((n, 8, 128), jnp.float32),
+            jax.ShapeDtypeStruct((fs, zs, cs * rows, qkv_cols), jnp.bfloat16),
+            jax.ShapeDtypeStruct((fs, cs * rows, gu_pieces.shape[2]), jnp.bfloat16),
+            jax.ShapeDtypeStruct(tokens.shape, tokens.dtype),
+            jax.ShapeDtypeStruct(cotangent.shape, cotangent.dtype),
+            jax.ShapeDtypeStruct(own_o.shape, own_o.dtype),
+            jax.ShapeDtypeStruct(own_d.shape, own_d.dtype),
         ],
-        compiler_params=pltpu.CompilerParams(
-            dimension_semantics=("arbitrary", "arbitrary"), vmem_limit_bytes=60 * 1024 * 1024
-        ),
-        name="attn_bwd",
-    )(lens, qkv, qkv, qkv, grad, lse, offset_bias)
-
+        in_specs=[vmem()] * 7,
+        out_specs=[vmem()] + [anywhere()] * 6,
+        scratch_shapes=[
+            pltpu.VMEM((n, 8, 128), jnp.float32),
+            dma((n,)), dma((n,)), dma((5,)),
+            dma((devices,)), dma((devices,)), dma((devices,)), dma((devices,)),
+            dma((2, zs)), dma((2, zs)),
+        ]
+        + Swap.scratch(zs, *tokens.shape[1:]) * 2,
+        compiler_params=plane_params(collective_id),
+        cost_estimate=estimate(120),
+        name="start",
+    )(small, qkv_pieces, gu_pieces, tokens, cotangent, own_o, own_d)
+
+
+def finish_kernel(
+    sizes, small_ref, g_ref, small_out, out_ref, slots, send, recv, own_sem, *swap_scratch
+):
+    everyone = Everyone(sizes)
+    everyone.barrier()
+    everyone.begin(small_ref, True, slots, send, recv, own_sem)
+    swap = Swap(g_ref, out_ref, swap_scratch)
+    swap.start()
+    swap.hand_on()
+    everyone.finish(small_ref, True, slots, send, recv)
+    small_out[...] = jnp.sum(slots[...], axis=0)
+    swap.close()
+
+
+def finish(small, grad, collective_id):
+    sizes = tuple(lax.axis_size(a) for a in ("fsdp", "z", "core"))
+    n = math.prod(sizes)
+    dma = pltpu.SemaphoreType.DMA
+    return pl.pallas_call(
+        functools.partial(finish_kernel, sizes),
+        out_shape=[
+            jax.ShapeDtypeStruct((8, 128), small.dtype),
+            jax.ShapeDtypeStruct(grad.shape, grad.dtype),
+        ],
+        in_specs=[vmem(), vmem()],
+        out_specs=[vmem(), anywhere()],
+        scratch_shapes=[pltpu.VMEM((n, 8, 128), small.dtype), dma((n,)), dma((n,)), dma]
+        + Swap.scratch(sizes[1], *grad.shape[1:]),
+        compiler_params=plane_params(collective_id),
+        cost_estimate=estimate(45),
+        name="finish",
+    )(small, grad)
+
+
+def to_tiles(x):
+    return jnp.pad(x, ((0, 0), (0, 1024 - x.shape[1]))).reshape(-1, 8, 128)
 
 from jax.sharding import Mesh
 from jax.sharding import PartitionSpec as P
@@ -229,29 +1027,6 @@
     weighted = grad_normed * gain_row
     inner_mean = jnp.mean(weighted * values, axis=1, keepdims=True)
     return row_scale * (weighted - values * row_scale * row_scale * inner_mean)
-
-
-def gelu_tanh(values):
-    return jax.nn.gelu(values, approximate=True)
-
-
-def swap_planes(x):
-    f, z = lax.axis_size("fsdp"), lax.axis_size("z")
-    pairs = [(i * z + j, j * f + i) for i in range(f) for j in range(z)]
-    return lax.ppermute(x, ("fsdp", "z"), pairs)
-
-
-def gather_rows(x, seqs):
-    b = x.shape[0] // seqs
-    full = lax.all_gather(x.reshape(seqs, b, -1), TP, axis=1, tiled=True)
-    return full.reshape(-1, x.shape[1])
-
-
-def scatter_rows(x, seqs):
-    part = lax.psum_scatter(
-        x.reshape(seqs, x.shape[0] // seqs, -1), TP, scatter_dimension=1, tiled=True
-    )
-    return part.reshape(-1, x.shape[1])
 
 
 class Layout:
@@ -292,13 +1067,6 @@
         both = jnp.zeros((size * self.c, g.shape[1]), g.dtype)
         both = lax.dynamic_update_slice_in_dim(both, g, lax.axis_index("core") * size, 0)
         return lax.psum_scatter(both, ("z", "core"), scatter_dimension=0, tiled=True)
-
-
-def spread(pieces):
-    f, z, c = (lax.axis_size(a) for a in ALL)
-    devices, rows, cols = pieces.shape
-    got = lax.all_to_all(pieces, TP, split_axis=0, concat_axis=0, tiled=True)
-    return got.reshape(f, c * rows, cols)
 
 
 def over_z(got):
@@ -336,13 +1104,28 @@
     head_cols = Layout(w_attn_out.shape[0], head_dim)
     ff_cols = Layout(w_down.shape[0], w_down.shape[0])
 
-    small = lax.all_gather(
-        jnp.concatenate([norm1_gain, norm2_gain, rel_bias]).astype(BF), ALL, axis=0
+    own_small = jnp.concatenate([norm1_gain, norm2_gain, rel_bias]).astype(BF).astype(F32)
+    own_small = jnp.concatenate([own_small, lengths.astype(F32)])
+    qkv_pieces = jnp.concatenate(
+        [head_cols.split(w.astype(BF)) for w in (w_query, w_key, w_value)], axis=2
     )
+    ff_pieces = jnp.concatenate([ff_cols.split(w.astype(BF)) for w in (w_gate, w_up)], axis=2)
+    small, w_qkv, got_gu, x_in, cot, own_o, own_d = start(
+        to_tiles(own_small[None]), qkv_pieces, ff_pieces, tokens, cotangent,
+        w_attn_out.astype(BF), w_down.astype(BF), 9,
+    )
+    w_qkv = w_qkv.reshape(width, -1)
+    w_o = head_cols.gather(own_o)
+    w_gu = over_z(got_gu)
+    w_d = ff_cols.gather(own_d)
+    small = small.reshape(-1, 1024)[:, : own_small.shape[0]]
+    lens = lax.dynamic_index_in_dim(
+        small[:, -seqs:], lax.axis_index("z") * zs * cs, 0, keepdims=False
+    ).astype(jnp.int32)
     g = norm1_gain.shape[0]
     gain_one = small[:, :g].reshape(1, -1).astype(F32)
     gain_two = small[:, g : 2 * g].reshape(1, -1).astype(F32)
-    table = small[:, 2 * g :].reshape(1, -1).astype(F32).reshape(H, buckets_n)
+    table = small[:, 2 * g : -seqs].reshape(1, -1).astype(F32).reshape(H, buckets_n)
     plane_index = lax.axis_index("fsdp") * cs + lax.axis_index("core")
     table = head_cols.split(jnp.repeat(table.T, head_dim, axis=1))[:, :, ::head_dim]
     table = lax.dynamic_index_in_dim(table, plane_index, 0, keepdims=False).T
@@ -350,18 +1133,6 @@
     one_hot = jnp.pad(one_hot, ((0, 1), (0, 0)))
     offset_bias = jnp.dot(table, one_hot.T, precision=HIGHEST)
 
-    lens = swap_planes(lengths)
-    x_in = swap_planes(tokens)
-    cot = swap_planes(cotangent)
-
-    qkv_pieces = jnp.concatenate(
-        [head_cols.split(w.astype(BF)) for w in (w_query, w_key, w_value)], axis=2
-    )
-    ff_pieces = jnp.concatenate([ff_cols.split(w.astype(BF)) for w in (w_gate, w_up)], axis=2)
-    w_qkv = over_z(spread(qkv_pieces))
-    w_o = head_cols.gather(w_attn_out.astype(BF))
-    w_gu = over_z(spread(ff_pieces))
-    w_d = ff_cols.gather(w_down.astype(BF))
     ff = w_d.shape[0]
 
     positions = plane_index * block_len + jnp.arange(block_len, dtype=jnp.int32)
@@ -369,54 +1140,53 @@
 
     x = x_in.reshape(rows, width).astype(F32)
     scale_one = rms_scale(x)
-    normed = gather_rows((x * scale_one * gain_one).astype(BF), seqs)
     grad_rows = cot.reshape(rows, width).astype(F32) * valid
-    grad_branch = gather_rows(grad_rows.astype(BF), seqs)
-
-    qkv = jnp.dot(normed, w_qkv, preferred_element_type=F32).astype(BF)
+    grad_branch = plane_gather(grad_rows.astype(BF), seqs, 1)
+
+    normed, qkv = plane_gather_dot((x * scale_one * gain_one).astype(BF), w_qkv, NN, seqs, 2)
     attended, lse = attn_fwd(qkv, offset_bias, lens, heads, head_dim, seqs)
-    attn_sum = scatter_rows(jnp.dot(attended, w_o, preferred_element_type=F32).astype(BF), seqs)
-    hidden_one = x + attn_sum.astype(F32)
+    hidden_one = x + plane_dot_scatter(attended, w_o, NN, seqs, 3)
     scale_two = rms_scale(hidden_one)
-    normed_two = gather_rows((hidden_one * scale_two * gain_two).astype(BF), seqs)
-
-    gate = jnp.dot(normed_two, w_gu[:, :ff], preferred_element_type=F32)
-    upward = jnp.dot(normed_two, w_gu[:, ff:], preferred_element_type=F32)
-    activated, gelu_pull = jax.vjp(gelu_tanh, gate)
-    hidden_ff = (activated * upward).astype(BF)
-    out_part = jnp.dot(hidden_ff, w_d, preferred_element_type=F32).astype(BF)
-    grad_hidden = jnp.einsum("rd,fd->rf", grad_branch, w_d, preferred_element_type=F32)
-    grad_gate = gelu_pull(grad_hidden * upward)[0].astype(BF)
-    grad_up = (grad_hidden * activated).astype(BF)
-    grad_gu = jnp.concatenate([grad_gate, grad_up], axis=1)
-    grad_n2_part = jnp.einsum("rf,df->rd", grad_gu, w_gu, preferred_element_type=F32).astype(BF)
-    grad_normed_two = scatter_rows(grad_n2_part, seqs).astype(F32)
+    normed_two, hidden_ff, grad_gu = plane_gather_ffn(
+        (hidden_one * scale_two * gain_two).astype(BF), grad_branch, w_gu, w_d, seqs, 4
+    )
+    grad_w_down = jnp.einsum("rf,rd->fd", hidden_ff, grad_branch, preferred_element_type=F32)
+    grad_w_gu = jnp.einsum("rd,rf->df", normed_two, grad_gu, preferred_element_type=F32)
+    grad_w_down, grad_gu = lax.optimization_barrier((grad_w_down.astype(BF), grad_gu))
+    sum_down = ff_cols.scatter(grad_w_down)
+    grad_w_gu, grad_gu = lax.optimization_barrier((grad_w_gu.astype(BF), grad_gu))
+    grad_normed_two = plane_dot_scatter(grad_gu, w_gu, NT, seqs, 5)
+    grad_w_gu, grad_normed_two, sum_down = lax.optimization_barrier(
+        (grad_w_gu, grad_normed_two, sum_down)
+    )
+    sum_gu = reduce_z(grad_w_gu)
     gain_two_part = jnp.sum(grad_normed_two * hidden_one * scale_two, axis=0)
     grad_hidden_one = grad_rows + norm_back(grad_normed_two, hidden_one, scale_two, gain_two)
-    grad_attn = gather_rows(grad_hidden_one.astype(BF), seqs)
-
-    result = hidden_one + scatter_rows(out_part, seqs).astype(F32)
-    output = swap_planes((result * valid).astype(BF).reshape(seqs, block_len, width))
-
-    grad_w_down = jnp.einsum("rf,rd->fd", hidden_ff, grad_branch, preferred_element_type=F32)
-    grad_w_gu = jnp.einsum("rd,rf->df", normed_two, grad_gu, preferred_element_type=F32)
-    sum_down = ff_cols.scatter(grad_w_down.astype(BF))
-    sum_gu = reduce_z(grad_w_gu.astype(BF))
-
-    grad_attended = jnp.einsum("rd,kd->rk", grad_attn, w_o, preferred_element_type=F32).astype(BF)
+    grad_attn, grad_attended = plane_gather_dot(grad_hidden_one.astype(BF), w_o, NT, seqs, 6)
+
+
     grad_w_o = jnp.einsum("rk,rd->kd", attended, grad_attn, preferred_element_type=F32)
-    sum_o = head_cols.scatter(grad_w_o.astype(BF))
-    dq, dk, dv, grad_offset = attn_bwd(
-        qkv, grad_attended, lse, offset_bias, lens, heads, head_dim, seqs
-    )
+    grad_w_o, grad_attended = lax.optimization_barrier((grad_w_o.astype(BF), grad_attended))
+    if fs <= 4:
+        dq, dk, dv, grad_offset, ff_sum = attn_bwd(
+            qkv, grad_attended, lse, offset_bias, lens, heads, head_dim, seqs,
+            product=(hidden_ff, w_d), collective_id=7,
+        )
+    else:
+        ff_sum = plane_dot_scatter(hidden_ff, w_d, NN, seqs, 7)
+        dq, dk, dv, grad_offset = attn_bwd(
+            qkv, grad_attended, lse, offset_bias, lens, heads, head_dim, seqs
+        )
+    result = ((hidden_one + ff_sum) * valid).astype(BF).reshape(seqs, block_len, width)
     dqkv = jnp.concatenate([dq, dk, dv], axis=1)
     grad_w_qkv = jnp.einsum("rd,rk->dk", normed, dqkv, preferred_element_type=F32)
-    sum_qkv = reduce_z(grad_w_qkv.astype(BF))
-    grad_n_part = jnp.einsum("rk,dk->rd", dqkv, w_qkv, preferred_element_type=F32).astype(BF)
-    grad_normed = scatter_rows(grad_n_part, seqs).astype(F32)
+    grad_w_qkv, dqkv = lax.optimization_barrier((grad_w_qkv.astype(BF), dqkv))
+    grad_w_qkv, grad_w_o, sum_gu = lax.optimization_barrier((grad_w_qkv, grad_w_o, sum_gu))
+    sum_qkv = reduce_z(grad_w_qkv)
+    sum_o = head_cols.scatter(grad_w_o)
+    grad_normed, output = plane_dot_scatter(dqkv, w_qkv, NT, seqs, 8, swapped=result)
     gain_one_part = jnp.sum(grad_normed * x * scale_one, axis=0)
     grad_x = grad_hidden_one + norm_back(grad_normed, x, scale_one, gain_one)
-    grad_tokens = swap_planes(grad_x.astype(BF).reshape(seqs, block_len, width))
 
     grad_table = jnp.dot(grad_offset, one_hot, precision=HIGHEST)
     bias_all = jnp.zeros((fs * cs, heads, buckets_n), F32)
@@ -431,7 +1201,10 @@
         ],
         axis=1,
     )
-    small_grad = lax.psum_scatter(small_grad, ALL, scatter_dimension=0, tiled=True)[0]
+    small_sum, grad_tokens = finish(
+        to_tiles(small_grad), grad_x.astype(BF).reshape(seqs, block_len, width), 10
+    )
+    small_grad = small_sum.reshape(-1)[: small_grad.shape[1]]
 
     got_gu = unspread(sum_gu)
     got_qkv = unspread(sum_qkv)

time: 1390 us -> 883 us (0.64)
  waiting for transfers between devices: 796 us -> 22.1 us
  Pallas kernels: 70.1 us -> 690 us
  blocking collectives: 232 us -> 0 us
  matrix products: 146 us -> 45.8 us
  starting transfers between devices: 28.1 us -> 11.7 us
    pallas_call x0 -> x9, Pallas kernels: none -> 589 us  [the longest x3 201 us: plane_dot_scatter(): pl.pallas_call(functools.partial(dot_scatter_kernel, fs, zs, dims, 256, s...]
    reduce_scatter x4 -> x0, waiting for transfers between devices: 212 us -> none  [scatter_rows(): lax.psum_scatter(x.reshape(seqs, x.shape[0] // seqs, -1), TP, scatter_dim...]
    all_gather x4 -> x0, waiting for transfers between devices: 191 us -> none  [gather_rows(): full = lax.all_gather(x.reshape(seqs, b, -1), TP, axis=1, tiled=True)]
    all_gather x1 -> x0, blocking collectives: 142 us -> none  [shards(): lax.all_gather(jnp.concatenate([norm1_gain, norm2_gain, rel_bias]).astype...]
    reduce_scatter x2, waiting for transfers between devices: 131 us -> 0.04 us  [scatter(): return lax.psum_scatter(g, 'z', scatter_dimension=0, tiled=True)]
    dot_general x9 -> x0, matrix products: 98.8 us -> none  [the longest x1 16 us: shards(): jnp.einsum('rf,df->rd', grad_gu, w_gu, preferred_element_type=F32)]
    all_gather x2 -> x1, waiting for transfers between devices: 87.8 us -> 12.1 us  [over_z(): full = lax.all_gather(got, 'z', axis=1, tiled=True)]
    reduce_scatter x2, waiting for transfers between devices: 71.9 us -> 0.01 us  [reduce_z(): lax.psum_scatter(grad.reshape(f, grad.shape[0] // f, -1), 'z', scatter_di...]
  transfers between devices with their start and end apart: 23 -> 9, of which waited for: 14 -> 2; matrix products, arithmetic and copies ran while one was open for 13% -> 10% of each run, Pallas kernels for 5% -> 56%
where the time goes in v2:
time: 883 us; the launch traced here: 876 us
  Pallas kernels  690 us (78%)
  local copies, waits for them, and re-layouts  51 us (6%)
  matrix products  45.8 us (5%)
  other arithmetic  40.1 us (5%)
  waiting for transfers between devices  22.1 us (3%)
  between operations  15.3 us (2%)
  starting transfers between devices  11.7 us (1%)
    pallas_call x3, Pallas kernels, plane_dot_scatter(): pl.pallas_call(functools.partial(dot_scatter_kernel, fs, zs, dims, 256, s...  201 us
    pallas_call x1, Pallas kernels, start(): pl.pallas_call(functools.partial(start_kernel, sizes), out_shape=[jax.Sha...  141 us
    pallas_call x2, Pallas kernels, plane_gather_dot(): pl.pallas_call(functools.partial(gather_dot_kernel, fs, dims, tile), out_...  91.7 us
    pallas_call x1, Pallas kernels, attn_bwd(): pl.pallas_call(functools.partial(attn_bwd_kernel, heads, head_dim, block,...  74.8 us
    pallas_call x1, Pallas kernels, finish(): pl.pallas_call(functools.partial(finish_kernel, sizes), out_shape=[jax.Sh...  60.1 us
    pallas_call x1, Pallas kernels, plane_gather_ffn(): pl.pallas_call(functools.partial(gather_ffn_kernel, fs), out_shape=[jax.S...  56.6 us
    pallas_call x1, Pallas kernels, plane_gather(): pl.pallas_call(functools.partial(gather_kernel, fs), out_shape=jax.ShapeD...  39 us
    pallas_call x1, Pallas kernels, attn_fwd(): pl.pallas_call(functools.partial(attn_fwd_kernel, heads, head_dim, block,...  25.7 us
  transfers between devices with their start and end apart: 9, of which 2 were waited for; matrix products, arithmetic and copies ran while one was open for 10% of the time, Pallas kernels for 56%

profile of v2, /device:TPU:22, one launch (start us, length us, event | category | flops | bytes accessed | tf_op | source)
XLA Modules:
  0.0 875.7 jit_solution(10950298676442662799)
XLA Ops:
  7.2 1.4 convert_element_type.182
  8.6 1.2 reshape.309
  10.9 1.4 convert_element_type.183
  12.3 1.2 reshape.311
  16.7 1.1 convert_element_type.181
  18.9 2.2 convert_element_type.185.d_ref
  21.1 0.7 convert_element_type.184.o_ref
  21.9 1.2 pad_maximum_fusion.gu_ref
  23.8 0.9 pad_maximum_fusion.1.qkv_ref
  24.8 141.2 %start.1 = (f32[32,8,128]{2,1,0:T(8,128)}, bf16[4,4,128,768]{3,2,1,0:T(8,128)(2,1)}, bf16[4,128,1280]{2,1,0:T(8,128)(2,1)}, bf16[2,128,2048]{2,1,0:T(8,128)(2,1)...) custom-call(f32[1,8,128]{2,1,0:T(8,128)} %bitcast.165, ...), custom_call_target="tpu_custom_call" | custom-call | flops 131999997952 | bytes 120000000 | tf_op jit(solution)/shard_map/start/pallas_call | solution.py:947
  166.1 0.7 all-gather.8.cloned.1.call-update
  168.6 1.3 fusion
  171.8 39.0 %plane_gather.1.g_ref = bf16[2,8,128,2048]{3,2,1,0:T(8,128)(2,1)} custom-call(bf16[2,128,2048]{2,1,0:T(8,128)(2,1)} %get-tuple-element.112.x_ref), custom_call_target="tpu_custom_call" | custom-call | flops 49500000256 | bytes 45000000 | tf_op jit(solution)/shard_map/plane_gather/pallas_call | solution.py:536
  210.9 1.3 fusion.2.x_ref
  212.1 47.8 %plane_gather_dot.2 = (bf16[2,8,128,2048]{3,2,1,0:T(8,128)(2,1)}, bf16[2,8,128,768]{3,2,1,0:T(8,128)(2,1)}) custom-call(bf16[2,128,2048]{2,1,0:T(8,128)(2,1)} %fusion.2.x_ref, bf16[2048,768]{1,0:T(8,128)(2,1)} %bitcast.172), custom_call_target="tpu_custom_call" | custom-call | flops 49500000256 | bytes 45000000 | tf_op jit(solution)/shard_map/plane_gather_dot/pallas_call | solution.py:580
  259.9 1.2 fusion.13.bias_ref
  261.1 25.7 %attn_fwd.1 = (bf16[2048,256]{1,0:T(8,128)(2,1)}, f32[2048,128]{1,0:T(8,128)}) custom-call(s32[2]{0:T(128)} %copy-done.29, bf16[2048,768]{1,0:T(8,128)(2,1)} %bitcast.174, bf16[2048,768]{1,0:T(8,128)(2,1)} %bitcast.175, bf16[2048,768]{1,0:T(8,128)(2,1)} %bitcast.176, f32[4,2048]{1,0:T(4,128)} %fusion.13.bias_ref), custom_call_target="tpu_custom_call" | custom-call | flops 28600000512 | bytes 26000000 | tf_op jit(solution)/shard_map/attn_fwd/pallas_call | solution.py:70
  286.8 46.0 %plane_dot_scatter.3 = f32[2,128,2048]{2,1,0:T(8,128)} custom-call(bf16[2,8,128,256]{3,2,1,0:T(8,128)(2,1)} %bitcast.145, bf16[256,2048]{1,0:T(8,128)(2,1)} %all-gather.4.cloned.1.call-done.w_ref), custom_call_target="tpu_custom_call" | custom-call | flops 49500000256 | bytes 45000000 | tf_op jit(solution)/shard_map/plane_dot_scatter/pallas_call | solution.py:760
  332.9 2.1 multiply_reduce_fusion.2
  335.1 1.3 multiply_convert_fusion.2.x_ref
  336.4 12.1 %all-gather.6.cloned.1.call-done = bf16[4,512,1280]{2,1,0:T(8,128)(2,1)} async-done(((bf16[4,128,1280]{2,1,0:T(8,128)(2,1)}), bf16[4,512,1280]{2,1,0:T(8,128)(2,1)}) %all-gather.6.cloned.1.call-update) | async-done | bytes 5242896 | tf_op jit(solution)/shard_map/all_gather | solution.py:1074
  348.6 56.6 %plane_gather_ffn.1 = (bf16[2,8,128,2048]{3,2,1,0:T(8,128)(2,1)}, bf16[2,8,128,640]{3,2,1,0:T(8,128)(2,1)}, bf16[2,8,128,1280]{3,2,1,0:T(8,128)(2,1)}) custom-call(bf16[2,128,2048]{2,1,0:T(8,128)(2,1)} %multiply_convert_fusion.2.x_ref, bf16[2,8,128,2048]{3,2,1,0:T(8,128)(2,1)} %plane_gather.1.g_ref, bf16[2048,1280]{1,0:T(8,128)(2,1)} %bitcast.169, ...), custom_call_target="tpu_custom_call" | custom-call | flops 49500000256 | bytes 45000000 | tf_op jit(solution)/shard_map/plane_gather_ffn/pallas_call | solution.py:811
  405.2 9.9 %bitcast_convert_fusion.1 = bf16[640,2048]{1,0:T(8,128)(2,1)} fusion(bf16[2,8,128,640]{3,2,1,0:T(8,128)(2,1)} %get-tuple-element.63.refs_0_, bf16[2,8,128,2048]{3,2,1,0:T(8,128)(2,1)} %plane_gather.1.g_ref), kind=kOutput, calls=%fused_computation.1 | convolution fusion | flops 5370019840 | bytes 13631488 | tf_op jit(solution)/shard_map/rf,rd->fd/dot_general | solution.py:1153
  415.2 16.8 %bitcast_convert_fusion = bf16[2048,1280]{1,0:T(8,128)(2,1)} fusion(bf16[2,8,128,2048]{3,2,1,0:T(8,128)(2,1)} %get-tuple-element.61, bf16[2,8,128,1280]{3,2,1,0:T(8,128)(2,1)} %get-tuple-element.62), kind=kOutput, calls=%fused_computation | convolution fusion | flops 10740039680 | bytes 18874368 | tf_op jit(solution)/shard_map/rd,rf->df/dot_general | solution.py:1154
  432.0 51.8 %plane_dot_scatter.4 = f32[2,128,2048]{2,1,0:T(8,128)} custom-call(bf16[2,8,128,1280]{3,2,1,0:T(8,128)(2,1)} %get-tuple-element.62, bf16[2048,1280]{1,0:T(8,128)(2,1)} %bitcast.170), custom_call_target="tpu_custom_call" | custom-call | flops 49500000256 | bytes 45000000 | tf_op jit(solution)/shard_map/plane_dot_scatter/pallas_call | solution.py:760
  483.9 3.4 multiply_reduce_fusion
  487.6 0.9 copy-done.3
  488.5 4.8 fusion.26
  493.3 44.0 %plane_gather_dot.3 = (bf16[2,8,128,2048]{3,2,1,0:T(8,128)(2,1)}, bf16[2,8,128,256]{3,2,1,0:T(8,128)(2,1)}) custom-call(bf16[2,128,2048]{2,1,0:T(8,128)(2,1)} %bitcast.152, bf16[256,2048]{1,0:T(8,128)(2,1)} %all-gather.4.cloned.1.call-done.w_ref), custom_call_target="tpu_custom_call" | custom-call | flops 49500000256 | bytes 45000000 | tf_op jit(solution)/shard_map/plane_gather_dot/pallas_call | solution.py:580
  537.2 6.7 convolution_convert_fusion.1
  544.0 74.8 %attn_bwd.1 = (bf16[2048,256]{1,0:T(8,128)(2,1)}, bf16[2048,256]{1,0:T(8,128)(2,1)}, bf16[2048,256]{1,0:T(8,128)(2,1)}, f32[4,2048]{1,0:T(4,128)}, f32[2,128,2048]{2,1,0:T(8,128)}) custom-call(s32[2]{0:T(128)} %copy-done.29, bf16[2048,768]{1,0:T(8,128)(2,1)} %bitcast.177, bf16[2048,768]{1,0:T(8,128)(2,1)} %bitcast.178, bf16[2048,768]{1,0:T(8,128)(2,1)} %bitcast.179, ...), custom_call_target="tpu_custom_call" | custom-call | flops 54999998464 | bytes 50000000 | tf_op jit(solution)/shard_map/attn_bwd/pallas_call | solution.py:241
  618.8 1.4 constant_dynamic-update-slice_fusion.2
  620.7 1.7 copy-done.15
  622.4 10.7 %convolution_convert_fusion = bf16[2048,768]{1,0:T(8,128)(2,1)} fusion(bf16[2048,2048]{1,0:T(8,128)(2,1)} %bitcast.171, bf16[2048,768]{1,0:T(8,128)(2,1)S(1)} %constant_dynamic-update-slice_fusion), kind=kOutput, calls=%fused_computation.2 | convolution fusion | flops 6444023808 | bytes 14680064 | tf_op jit(solution)/shard_map/rd,rk->dk/dot_general | solution.py:1182
  633.7 3.5 multiply_convert_fusion.refs_0_
  637.2 102.8 %plane_dot_scatter.5 = (f32[2,128,2048]{2,1,0:T(8,128)}, bf16[2,128,2048]{2,1,0:T(8,128)(2,1)}) custom-call(bf16[2,8,128,768]{3,2,1,0:T(8,128)(2,1)} %bitcast.155, bf16[2048,768]{1,0:T(8,128)(2,1)} %bitcast.173, bf16[2,128,2048]{2,1,0:T(8,128)(2,1)} %multiply_convert_fusion.refs_0_), custom_call_target="tpu_custom_call" | custom-call | flops 49500000256 | bytes 45000000 | tf_op jit(solution)/shard_map/plane_dot_scatter/pallas_call | solution.py:760
  740.1 2.1 fusion.5
  742.3 4.3 all-to-all-start.1
  747.1 1.0 broadcast_in_dim.34
  748.2 1.2 slice.56
  750.3 3.8 fusion.9
  754.1 8.4 all-to-all-done.1
  762.5 6.7 all-to-all-start
  769.3 60.1 %finish.1 = (f32[8,128]{1,0:T(8,128)}, bf16[2,128,2048]{2,1,0:T(8,128)(2,1)}) custom-call(f32[32,8,128]{2,1,0:T(8,128)} %bitcast.160, bf16[2,128,2048]{2,1,0:T(8,128)(2,1)} %bitcast.153), custom_call_target="tpu_custom_call" | custom-call | flops 49500000256 | bytes 45000000 | tf_op jit(solution)/shard_map/finish/pallas_call | solution.py:991
  829.4 1.2 slice.58
  830.6 1.2 convert_element_type.228
  831.8 1.3 fusion.29
  833.1 1.3 slice_convert_fusion
  834.5 2.8 reshape.350
  837.3 3.0 copy.57
  840.3 4.7 reshape.345
  845.0 1.4 reshape.351
  846.4 3.0 copy.58
  849.4 4.9 reshape.346
  854.3 1.8 convert_element_type.219
  856.1 1.3 slice_convert_fusion.2
  857.8 0.8 copy.54
  858.7 1.8 reshape.342
  860.9 0.8 copy.55
  861.7 1.8 reshape.343
  863.9 0.8 copy.56
  864.7 1.8 reshape.344
  866.5 1.0 copy.82
  867.5 1.0 copy.83
  (138 shorter events, 14.0 us)
Async XLA Ops:
  7.2 279.7 %all-gather.4.cloned.1.call-start = ((), (), s32[]{:S(2)}) async-start(), calls=%async_computation.6 | async-start | bytes 1310720 | tf_op jit(solution)/shard_map/all_gather | solution.py:1058
  13.5 1.1 copy-start.12
  14.6 1.0 copy-start.13
  18.3 2.8 copy-start.14
  18.3 3.5 copy-start.30
  18.4 3.5 copy-start.31
  18.4 3.5 copy-start.32
  18.4 3.5 copy-start.33
  166.0 1.8 copy-start.19
  166.0 2.6 copy-start
  166.0 2.6 copy-start.2
  166.1 170.4 %all-gather.8.cloned.1.call-start = ((), (), s32[]{:S(2)}) async-start(), calls=%async_computation.8 | async-start | bytes 3276800 | tf_op jit(solution)/shard_map/all_gather | solution.py:1058
  166.8 181.8 %all-gather.6.cloned.1.call-start = ((), (), s32[]{:S(2)}) async-start(), calls=%async_computation.7 | async-start | bytes 6553600 | tf_op jit(solution)/shard_map/all_gather | solution.py:1074
  167.5 316.3 %reduce-scatter.5.cloned.1.call-start = ((), (), s32[]{:S(2)}) async-start(), calls=%async_computation.9 | async-start | bytes 3276800 | tf_op jit(solution)/shard_map/reduce_scatter | solution.py:1065
  168.0 2.7 copy-start.29
  168.6 1.9 copy-start.24
  168.6 2.1 copy-start.26
  170.6 40.3 %copy-start.22 = (f32[2,128]{1,0:T(2,128)}, f32[2,128]{1,0:T(2,128)S(1)}, u32[]{:S(2)}) copy-start(f32[2,128]{1,0:T(2,128)S(1)} %get-tuple-element.106) | copy-start | bytes 3076
  170.6 40.2 %copy-start.16 = (f32[2048]{0:T(1024)}, f32[2048]{0:T(1024)S(1)}, u32[]{:S(2)}) copy-start(f32[2048]{0:T(1024)S(1)} %mul.183) | copy-start | bytes 24580
  171.1 88.8 %copy-start.5 = (pred[2047,32]{1,0:T(8,128)(4,1)}, pred[2047,32]{1,0:T(8,128)(4,1)S(1)}, u32[]{:S(2)}) copy-start(pred[2047,32]{1,0:T(8,128)(4,1)S(1)} %iota_compare_fusion) | copy-start | bytes 196516
  332.9 2.2 copy-start.1
  332.9 2.2 copy-start.18
  415.2 217.9 %reduce-scatter.7.cloned.1.call-start = ((), (), s32[]{:S(2)}) async-start(), calls=%async_computation.10 | async-start | bytes 6553600 | tf_op jit(solution)/shard_map/reduce_scatter | solution.py:1080
  487.3 1.2 copy-start.3
  487.3 1.2 copy-start.28
  487.3 275.2 %reduce-scatter.9.cloned.1.call-start = ((), (), s32[]{:S(2)}) async-start(), calls=%async_computation.11 | async-start | bytes 3932160 | tf_op jit(solution)/shard_map/reduce_scatter | solution.py:1080
  493.3 44.0 %copy-start.4 = (bf16[2048,256]{1,0:T(8,128)(2,1)S(1)}, bf16[2048,256]{1,0:T(8,128)(2,1)}, u32[]{:S(2)}) copy-start(bf16[2048,256]{1,0:T(8,128)(2,1)} %get-tuple-element.56) | copy-start | bytes 3145732
  618.8 1.5 copy-start.10
  618.8 1.8 copy-start.9
  620.7 1.7 copy-start.15
  633.1 0.6 copy-start.25
  637.2 102.8 %copy-start.17 = (f32[2048]{0:T(1024)S(1)}, f32[2048]{0:T(1024)}, u32[]{:S(2)}) copy-start(f32[2048]{0:T(1024)} %copy-done.16) | copy-start | bytes 24580
  637.2 102.8 %copy-start.23 = (f32[2,128]{1,0:T(2,128)S(1)}, f32[2,128]{1,0:T(2,128)}, u32[]{:S(2)}) copy-start(f32[2,128]{1,0:T(2,128)} %copy-done.22) | copy-start | bytes 3076
  742.2 4.4 copy-start.6
  742.2 4.4 copy-start.21
  742.2 7.2 copy-start.20
  742.3 8.0 copy-start.27
  742.3 20.2 %all-to-all-start.1 = ((bf16[8,64,1280]{2,1,0:T(8,128)(2,1)}), bf16[8,64,1280]{2,1,0:T(8,128)(2,1)S(1)}, u32[]{:S(2)}, u32[]{:S(2)}) async-start(bf16[8,64,1280]{2,1,0:T(8,128)(2,1)} %bitcast.149), calls=%async_computation.5 | async-start | bytes 2621440 | tf_op jit(solution)/shard_map/all_to_all | solution.py:1088
  746.6 107.7 %reduce-scatter.11.cloned.1.call-start = ((), (), s32[]{:S(2)}) async-start(), calls=%async_computation.12 | async-start | bytes 1310720 | tf_op jit(solution)/shard_map/reduce_scatter | solution.py:1065
  762.5 93.5 %all-to-all-start = ((bf16[8,64,768]{2,1,0:T(8,128)(2,1)}), bf16[8,64,768]{2,1,0:T(8,128)(2,1)}, u32[]{:S(2)}, u32[]{:S(2)}) async-start(bf16[8,64,768]{2,1,0:T(8,128)(2,1)} %bitcast.154), calls=%async_computation.3 | async-start | bytes 1572864 | tf_op jit(solution)/shard_map/all_to_all | solution.py:1088
  769.3 61.3 %copy-start.11 = (bf16[160,2048]{1,0:T(8,128)(2,1)S(1)}, bf16[160,2048]{1,0:T(8,128)(2,1)}, u32[]{:S(2)}) copy-start(bf16[160,2048]{1,0:T(8,128)(2,1)} %reduce-scatter.5.cloned.1.call-done) | copy-start | bytes 1966084
  863.9 2.6 copy-start.7
  864.7 2.7 copy-start.8
Sparse Core Ops, SparseCore 0:
  166.2 29.1 all-gather.3
  197.0 53.5 all-gather.7
  252.1 96.3 all-gather.5
  415.3 51.9 reduce-scatter.4
  487.4 94.3 reduce-scatter.6
  633.3 108.6 reduce-scatter.8
  754.3 51.1 reduce-scatter.10

commit v3 on v2

--- a/solution.py
+++ b/solution.py
@@ -100,33 +100,31 @@
 
 
 def attn_bwd_kernel(
-    heads, head_dim, block, length, seqs, fs, lens_ref, q_ref, k_ref, v_ref, g_ref, lse_ref, bias_ref,
-    *refs,
+    heads, head_dim, block, length, seqs, fs, lens_ref, q_ref, k_ref, v_ref, g_ref, lse_ref,
+    bias_ref, *refs,
 ):
     seq, blk = pl.program_id(0), pl.program_id(1)
     blocks = length // block
     last_seq, last_blk = seqs - 1, blocks - 1
+    grid_step = seq * blocks + blk
+    steps = seqs * blocks
     if fs:
-        a_ref, w_ref, dq_ref, dk_ref, dv_ref, dbias_ref, sum_ref = refs[:7]
-        refs = refs[7:]
-        plane = Plane(fs)
-
-        def partial(slot, cols):
-            return dotf(a_ref[:, slot].reshape(-1, a_ref.shape[3]), w_ref[:, cols])
-
-        actions = [plane.barrier] + scatter_actions(
-            plane, partial, 256, sum_ref.shape[2], sum_ref, refs[6:]
-        )
-        grid_step = seq * blocks + blk
-        steps = seqs * blocks
-        for step in range(steps):
-            todo = actions[len(actions) * step // steps : len(actions) * (step + 1) // steps]
-
-            @pl.when(grid_step == step)
-            def _(todo=todo):
-                for action in todo:
-                    action()
-
+        x_ref, wg_ref, gu_ref, dq_ref, dk_ref, dv_ref, dbias_ref = refs[:7]
+        out_ref, sum_ref, got_ref = refs[7:10]
+        refs = refs[10:]
+        column = Column(wg_ref, sum_ref, refs[6:9])
+        back = Back((fs, 1, 2), gu_ref, got_ref, refs[9:12])
+        swap = Swap(x_ref, out_ref, refs[12:])
+
+        def begin():
+            plane_and_column_greet()
+            swap.start()
+            column.start()
+            back.start()
+
+        todo = {0: begin, steps // 2: swap.hand_on}
+        for step, action in todo.items():
+            pl.when(grid_step == step)(action)
     else:
         dq_ref, dk_ref, dv_ref, dbias_ref = refs[:4]
         refs = refs[4:]
@@ -188,10 +186,19 @@
                 total = total + (pltpu.roll(part, n - 1 - i, 1) if i < n - 1 else part)[i : i + 1]
             dbias_ref[h : h + 1, :] = total
 
+    if fs:
+
+        @pl.when(grid_step == steps - 1)
+        def _():
+            column.close()
+            back.arrived()
+            back.close()
+            swap.close()
+
 
 def attn_bwd(
-    qkv, grad, lse, offset_bias, lens, heads, head_dim, seqs, block=256, product=None,
-    collective_id=None,
+    qkv, grad, lse, offset_bias, lens, heads, head_dim, seqs, block=256, swapped=None,
+    column=None, spread=None, collective_id=None,
 ):
     rows, width3 = qkv.shape
     width = width3 // 3
@@ -229,16 +236,21 @@
     ]
     args = [lens, qkv, qkv, qkv, grad, lse, offset_bias]
     fs = 0
-    if product is not None:
-        fs = lax.axis_size("fsdp")
-        a, w = product
-        a = a.reshape(seqs, 2 * fs, -1, a.shape[1])
-        args += [a, w]
-        in_specs += [vmem(), vmem()]
-        out_specs.append(vmem())
-        out_shape.append(jax.ShapeDtypeStruct((seqs, a.shape[2], w.shape[1]), jnp.float32))
-        scratch += scatter_scratch(fs, a.shape[2], w.shape[1])
-    out = pl.pallas_call(
+    if swapped is not None:
+        fs, zs = lax.axis_size("fsdp"), lax.axis_size("z")
+        column = column.reshape(zs, -1, column.shape[1])
+        spread = spread.reshape(2 * fs, -1, spread.shape[2])
+        args += [swapped, column, spread]
+        in_specs += [vmem()] * 3
+        out_specs += [anywhere(), vmem(), anywhere()]
+        out_shape += [
+            jax.ShapeDtypeStruct(swapped.shape, swapped.dtype),
+            jax.ShapeDtypeStruct(column.shape[1:], jnp.float32),
+            jax.ShapeDtypeStruct(spread.shape, spread.dtype),
+        ]
+        scratch += Column.scratch(column) + Back.scratch(2 * fs)
+        scratch += Swap.scratch(fs, *swapped.shape)
+    return pl.pallas_call(
         functools.partial(attn_bwd_kernel, heads, head_dim, block, length, seqs, fs),
         grid=(seqs, blocks),
         in_specs=in_specs,
@@ -252,9 +264,6 @@
         cost_estimate=estimate(50),
         name="attn_bwd",
     )(*args)
-    if product is not None:
-        out = list(out[:4]) + [out[4].reshape(-1, w.shape[1])]
-    return out
 
 MESH_ID = pl.DeviceIdType.MESH
 MIB = 1024 * 1024
@@ -272,7 +281,7 @@
 
 
 def estimate(us):
-    return pl.CostEstimate(flops=int(us * 1.1e9), bytes_accessed=int(us * 1e6), transcendentals=0)
+    return pl.CostEstimate(flops=int(us * 0.02 * 1.1e9), bytes_accessed=int(us * 1e5), transcendentals=0)
 
 
 def flip(f, bits):
@@ -324,8 +333,10 @@
     started = []
 
     def remote(*args):
-        started.append(remote_copy(*args))
-        started[-1].start()
+        copy = remote_copy(*args)
+        copy.start()
+        started.append(copy)
+        return copy
 
     def source(p, rel):
         return x_ref.at[p] if rel == 0 else buf_ref.at[p, plane.slot(rel)]
@@ -338,51 +349,44 @@
 
     def to_peer(p, step, rel):
         bit = plane.orders[p][step]
-        remote(
+        return remote(
             source(p, rel), buf_ref.at[p, plane.slot(rel)], send.at[p, step, rel],
             recv.at[p, rel ^ bit], plane.peer(bit),
         )
 
-    for step in range(plane.steps):
+    def finish(pairs):
+        for p, rel in pairs:
+            landed(buf_ref.at[p, plane.slot(rel, True)], mate_recv.at[p, rel])
+            if consume is not None:
+                consume(p, flip(plane.f, rel) * 2)
+
+    first = [to_peer(p, 0, 0) for p in range(2)]
+    for p in range(2):
+        to_mate(p, 0)
+    if consume is not None:
         for p in range(2):
-            to_peer(p, step, 0)
-        if step == 0:
-            for p in range(2):
-                to_mate(p, 0)
-    for p in range(2):
-        consume(p, plane.slot(0), x_ref.at[p])
-
-    def arrived(p, rel):
-        landed(buf_ref.at[p, plane.slot(rel)], recv.at[p, rel])
-
-    def mate_arrived(p, rel):
-        ref = buf_ref.at[p, plane.slot(rel, True)]
-        landed(ref, mate_recv.at[p, rel])
-        consume(p, plane.slot(rel, True), ref)
-
+            buf_ref[p, plane.slot(0)] = x_ref[p]
     have = [[0], [0]]
     pending = [(0, 0), (1, 0)]
     for step in range(plane.steps):
-        fresh = []
         for i in range(len(have[0])):
-            for p in range(2):
-                rel = have[p][i] ^ plane.orders[p][step]
-                fresh.append((p, rel))
-        for p, rel in pending:
-            mate_arrived(p, rel)
-        for p, rel in fresh:
-            arrived(p, rel)
-            to_mate(p, rel)
-            for later in range(step + 1, plane.steps):
-                to_peer(p, later, rel)
-            consume(p, plane.slot(rel), buf_ref.at[p, plane.slot(rel)])
+            finish(pending)
+            if i == 0 and step + 1 < plane.steps:
+                for copy in first:
+                    copy.wait_send()
+                    started[:] = [other for other in started if other is not copy]
+                first = [to_peer(p, step + 1, 0) for p in range(2)]
+            pending = [(p, have[p][i] ^ plane.orders[p][step]) for p in range(2)]
+            for p, rel in pending:
+                landed(buf_ref.at[p, plane.slot(rel)], recv.at[p, rel])
+                to_mate(p, rel)
+                for later in range(step + 1, plane.steps):
+                    to_peer(p, later, rel)
         for p in range(2):
-            have[p] = have[p] + [rel for q, rel in fresh if q == p]
-        pending = fresh
-    for p, rel in pending:
-        mate_arrived(p, rel)
-    for cp in started:
-        cp.wait_send()
+            have[p] = have[p] + [rel ^ plane.orders[p][step] for rel in have[p]]
+    finish(pending)
+    for copy in started:
+        copy.wait_send()
 
 
 def scatter_scratch(fs, b, width):
@@ -519,154 +523,268 @@
     )
 
 
-def gather_kernel(fs, x_ref, out_ref, *sems):
+def gather_dot_kernel(fs, dims, tile, other, x_ref, w_ref, *refs):
     plane = Plane(fs)
     plane.barrier()
-    own_sem = sems[4]
-    own = pltpu.make_async_copy(x_ref, out_ref.at[:, plane.slot(0)], own_sem)
-    own.start()
-    run_gather(plane, x_ref, out_ref, sems[:4], lambda p, slot, ref: None)
-    own.wait()
-
-
-def plane_gather(x, seqs, collective_id):
-    fs = lax.axis_size("fsdp")
-    x = x.reshape(seqs, -1, x.shape[1])
-    _, b, width = x.shape
-    full = pl.pallas_call(
-        functools.partial(gather_kernel, fs),
-        out_shape=jax.ShapeDtypeStruct((seqs, 2 * fs, b, width), x.dtype),
-        in_specs=[vmem()],
-        out_specs=anywhere(),
-        scratch_shapes=gather_sems(fs) + [pltpu.SemaphoreType.DMA],
-        compiler_params=plane_params(collective_id),
-        cost_estimate=estimate(45),
-        name="plane_gather",
-    )(x)
-    return full.reshape(-1, width)
-
-
-def gather_dot_kernel(fs, dims, tile, x_ref, w_ref, full_ref, y_ref, buf_ref, *sems):
-    plane = Plane(fs)
-    plane.barrier()
+    if other:
+        o_ref, full_ref, y_ref, wg_ref, buf_ref, acc_ref = refs[:6]
+        sems = refs[6:]
+        acc_ref[...] = jnp.zeros_like(acc_ref)
+    else:
+        full_ref, y_ref, buf_ref = refs[:3]
+        sems = refs[3:]
     keep_sem = sems[4]
+    b, width = buf_ref.shape[2:]
     columns = y_ref.shape[3]
     kept = []
 
-    def consume(p, slot, ref):
-        cp = pltpu.make_async_copy(ref, full_ref.at[p, slot], keep_sem.at[len(kept)])
+    def consume(p, slot):
+        two = pl.ds(slot, 2)
+        cp = pltpu.make_async_copy(
+            buf_ref.at[p, two], full_ref.at[p, two], keep_sem.at[len(kept)]
+        )
         cp.start()
         kept.append(cp)
 
+        def product(cols):
+            w = w_ref[:, cols] if dims == NN else w_ref[cols, :]
+            y = dotf(buf_ref[p, two].reshape(2 * b, width), w, dims)
+            y_ref[p, two, :, cols] = y.astype(y_ref.dtype).reshape(2, b, tile)
+
         def one(j, carry):
-            cols = pl.ds(pl.multiple_of(j * tile, tile), tile)
-            w = w_ref[:, cols] if dims == NN else w_ref[cols, :]
-            y_ref[p, slot, :, cols] = dotf(ref[...], w, dims).astype(y_ref.dtype)
+            product(pl.ds(pl.multiple_of(j * tile, tile), tile))
             return carry
 
-        lax.fori_loop(0, columns // tile, one, 0)
+        if tile == columns:
+            product(slice(None))
+        else:
+            lax.fori_loop(0, columns // tile, one, 0)
+        if other:
+            o_t = o_ref[p, two].reshape(2 * b, -1).T
+
+            def grad(j, carry):
+                cols = pl.ds(pl.multiple_of(j * 256, 256), 256)
+                acc_ref[:, cols] += dotf(o_t, buf_ref[p, two, :, cols].reshape(2 * b, 256))
+                return carry
+
+            lax.fori_loop(0, width // 256, grad, 0)
 
     run_gather(plane, x_ref, buf_ref, sems[:4], consume)
+    if other:
+        wg_ref[...] = acc_ref[...].astype(wg_ref.dtype)
     for cp in kept:
         cp.wait()
 
 
-def plane_gather_dot(x, w, dims, seqs, collective_id):
+def plane_gather_dot(x, w, dims, seqs, collective_id, other=None, dtype=jnp.bfloat16):
     fs = lax.axis_size("fsdp")
     x = x.reshape(seqs, -1, x.shape[1])
     _, b, width = x.shape
     columns = w.shape[1] if dims == NN else w.shape[0]
-    tile = math.gcd(columns, 256)
-    full, y = pl.pallas_call(
-        functools.partial(gather_dot_kernel, fs, dims, tile),
-        out_shape=[
-            jax.ShapeDtypeStruct((seqs, 2 * fs, b, width), x.dtype),
-            jax.ShapeDtypeStruct((seqs, 2 * fs, b, columns), jnp.bfloat16),
-        ],
-        in_specs=[vmem(), vmem()],
-        out_specs=[anywhere(), vmem()],
-        scratch_shapes=[pltpu.VMEM((seqs, 2 * fs, b, width), x.dtype)]
-        + gather_sems(fs)
-        + [pltpu.SemaphoreType.DMA((seqs * 2 * fs,))],
+    tile = next((t for t in (256, 128) if columns % t == 0), columns)
+    lead = (seqs, 2 * fs, b)
+    out_shape = [
+        jax.ShapeDtypeStruct(lead + (width,), x.dtype),
+        jax.ShapeDtypeStruct(lead + (columns,), dtype),
+    ]
+    args, scratch = [x, w], [pltpu.VMEM(lead + (width,), x.dtype)]
+    if other is not None:
+        args.append(other.reshape(lead + (-1,)))
+        out_shape.append(jax.ShapeDtypeStruct((other.shape[1], width), jnp.bfloat16))
+        scratch.append(pltpu.VMEM((other.shape[1], width), jnp.float32))
+    out = pl.pallas_call(
+        functools.partial(gather_dot_kernel, fs, dims, tile, other is not None),
+        out_shape=out_shape,
+        in_specs=[vmem()] * len(args),
+        out_specs=[anywhere()] + [vmem()] * (len(out_shape) - 1),
+        scratch_shapes=scratch + gather_sems(fs) + [pltpu.SemaphoreType.DMA((seqs * fs,))],
         compiler_params=plane_params(collective_id),
         cost_estimate=estimate(45),
         name="plane_gather_dot",
-    )(x, w)
-    return full.reshape(-1, width), y.reshape(-1, columns)
+    )(*args)
+    return (out[0].reshape(-1, width), out[1].reshape(-1, columns)) + tuple(out[2:])
 
 
 class Swap:
     def __init__(self, x_ref, out_ref, scratch):
         self.x_ref, self.out_ref = x_ref, out_ref
-        self.relay, self.d_sem, self.in_send, self.in_recv, self.on_send, self.on_recv = scratch
+        self.relay, self.own_sem, self.in_send, self.in_recv, self.on_send, self.on_recv = scratch
         self.f, self.z, self.c = (lax.axis_index(a) for a in ("fsdp", "z", "core"))
-        self.zs = self.relay.shape[0]
+        self.fs, self.size = self.relay.shape[:2]
 
     @staticmethod
-    def scratch(zs, b, width):
+    def scratch(fs, rows, width):
         dma = pltpu.SemaphoreType.DMA
         return [
-            pltpu.VMEM((zs, b, width), jnp.bfloat16), dma((2,)), dma, dma((zs,)), dma((zs,)), dma
+            pltpu.VMEM((fs, rows // fs, width), jnp.bfloat16), dma,
+            dma((fs,)), dma((fs,)), dma((fs,)), dma((fs,)),
         ]
+
+    def column(self, d):
+        return lax.rem(self.f + d, self.fs)
+
+    def part(self, ref, k):
+        return ref.at[pl.ds(pl.multiple_of(k * self.size, self.size), self.size)]
 
     def straight(self):
         return remote_copy(
-            self.x_ref.at[0], self.out_ref.at[0], self.d_sem.at[0], self.d_sem.at[1],
-            (self.z, self.f, self.c),
+            self.part(self.x_ref, self.f), self.part(self.out_ref, self.f), self.in_send.at[0],
+            self.on_recv.at[self.f], (self.z, self.f, self.c),
         )
 
-    def inward(self):
+    def inward(self, d):
+        k = self.column(d)
         return remote_copy(
-            self.x_ref.at[1], self.relay.at[self.f], self.in_send, self.in_recv.at[self.f],
-            (self.z, self.z, self.c),
+            self.part(self.x_ref, k), self.relay.at[d], self.in_send.at[d],
+            self.in_recv.at[d], (k, self.z, self.c),
         )
 
-    def onward(self, source):
+    def onward(self, d):
+        source = self.column(self.fs - d)
         return remote_copy(
-            self.relay.at[source], self.out_ref.at[1], self.on_send.at[source], self.on_recv,
-            (self.f, source, self.c),
+            self.relay.at[d], self.part(self.out_ref, self.f), self.on_send.at[d],
+            self.on_recv.at[self.f], (self.z, source, self.c),
         )
 
     def own(self):
-        return pltpu.make_async_copy(self.x_ref, self.out_ref, self.d_sem.at[0])
-
-    def start(self):
+        return pltpu.make_async_copy(self.x_ref, self.out_ref, self.own_sem)
+
+    def start_inward(self):
         @pl.when(self.f != self.z)
         def _():
-            self.inward().start()
+            for d in range(1, self.fs):
+                self.inward(d).start()
+
+    def start_straight(self):
+        @pl.when(self.f != self.z)
+        def _():
             self.straight().start()
 
         @pl.when(self.f == self.z)
         def _():
             self.own().start()
 
+    def start(self):
+        self.start_inward()
+        self.start_straight()
+
+    def relayed(self, body):
+        for d in range(1, self.fs):
+
+            @pl.when(self.column(self.fs - d) != self.z)
+            def _(d=d):
+                body(d)
+
     def hand_on(self):
+        def one(d):
+            landed(self.relay.at[d], self.in_recv.at[d])
+            self.onward(d).start()
+
+        self.relayed(one)
+
+    def close(self):
+        self.relayed(lambda d: self.onward(d).wait_send())
+
         @pl.when(self.f == self.z)
         def _():
-            for source in range(self.zs):
-
-                @pl.when(source != self.z)
-                def _(source=source):
-                    landed(self.relay.at[source], self.in_recv.at[source])
-                    self.onward(source).start()
-
-    def close(self):
-        @pl.when(self.f == self.z)
-        def _():
-            for source in range(self.zs):
-
-                @pl.when(source != self.z)
-                def _(source=source):
-                    self.onward(source).wait_send()
-
             self.own().wait()
 
         @pl.when(self.f != self.z)
         def _():
-            self.inward().wait_send()
             self.straight().wait_send()
-            landed(self.out_ref.at[0], self.d_sem.at[1])
-            landed(self.out_ref.at[1], self.on_recv)
+            for d in range(1, self.fs):
+                self.inward(d).wait_send()
+            for k in range(self.fs):
+                landed(self.part(self.out_ref, k), self.on_recv.at[k])
+
+
+def plane_and_column_greet():
+    fs, zs, cs = (lax.axis_size(a) for a in ("fsdp", "z", "core"))
+    f, z, c = (lax.axis_index(a) for a in ("fsdp", "z", "core"))
+    bar = pltpu.get_barrier_semaphore()
+    places = [(lax.rem(f + df, fs), z, lax.rem(c + dc, cs)) for df in range(fs) for dc in range(cs)]
+    places = places[1:] + [(f, lax.rem(z + dz, zs), c) for dz in range(1, zs)]
+    places += [
+        (lax.rem(f + df, fs), lax.rem(z + dz, zs), c) for df in range(1, fs) for dz in range(1, zs)
+    ]
+    for place in places:
+        pl.semaphore_signal(bar, inc=1, device_id=place, device_id_type=MESH_ID)
+    pl.semaphore_wait(bar, len(places))
+
+
+class Column:
+    def __init__(self, x_ref, sum_ref, scratch):
+        self.x_ref, self.sum_ref = x_ref, sum_ref
+        self.inbox, self.send, self.recv = scratch
+        self.f, self.z, self.c = (lax.axis_index(a) for a in ("fsdp", "z", "core"))
+        self.zs = x_ref.shape[0]
+
+    @staticmethod
+    def scratch(x):
+        dma = pltpu.SemaphoreType.DMA
+        return [pltpu.VMEM(x.shape, x.dtype), dma((x.shape[0],)), dma((x.shape[0],))]
+
+    def copy(self, d):
+        to = lax.rem(self.z + d, self.zs)
+        return remote_copy(
+            self.x_ref.at[to], self.inbox.at[d], self.send.at[d], self.recv.at[d],
+            (self.f, to, self.c),
+        )
+
+    def start(self):
+        for d in range(1, self.zs):
+            self.copy(d).start()
+
+    def close(self):
+        for d in range(1, self.zs):
+            self.copy(d).wait_send()
+            landed(self.inbox.at[d], self.recv.at[d])
+        total = self.x_ref[self.z].astype(jnp.float32)
+        for d in range(1, self.zs):
+            total = total + self.inbox[d].astype(jnp.float32)
+        self.sum_ref[...] = total
+
+
+class Back:
+    def __init__(self, sizes, src_ref, got_ref, scratch):
+        fs, zs, self.cs = sizes
+        self.src_ref, self.got_ref = src_ref, got_ref
+        self.send, self.recv, self.own_sem = scratch
+        self.z = lax.axis_index("z")
+        self.devices = fs * self.cs
+        self.me = lax.axis_index("fsdp") * self.cs + lax.axis_index("core")
+
+    @staticmethod
+    def scratch(devices):
+        dma = pltpu.SemaphoreType.DMA
+        return [dma((devices,)), dma((devices,)), dma]
+
+    def copy(self, d):
+        to = lax.rem(self.me + d, self.devices)
+        return remote_copy(
+            self.src_ref.at[to], self.got_ref.at[self.me], self.send.at[d], self.recv.at[d],
+            (lax.div(to, self.cs), self.z, lax.rem(to, self.cs)),
+        )
+
+    def own(self):
+        return pltpu.make_async_copy(
+            self.src_ref.at[self.me], self.got_ref.at[self.me], self.own_sem
+        )
+
+    def start(self):
+        for d in range(1, self.devices):
+            self.copy(d).start()
+        self.own().start()
+
+    def arrived(self):
+        for d in range(1, self.devices):
+            at = lax.rem(self.me + self.devices - d, self.devices)
+            landed(self.got_ref.at[at], self.recv.at[d])
+        self.own().wait()
+
+    def close(self):
+        for d in range(1, self.devices):
+            self.copy(d).wait_send()
 
 
 class Everyone:
@@ -676,59 +794,62 @@
         f, z, c = (lax.axis_index(a) for a in ("fsdp", "z", "core"))
         self.me = (f * self.zs + z) * self.cs + c
 
-    def place(self, index):
-        zs, cs = self.zs, self.cs
-        return (lax.div(index, zs * cs), lax.rem(lax.div(index, cs), zs), lax.rem(index, cs))
-
-    def other(self, d):
-        return lax.rem(self.me + d, self.n)
-
-    def barrier(self):
+    def place(self, d):
+        f, z, c = (lax.axis_index(a) for a in ("fsdp", "z", "core"))
+        df, dz, dc = d // (self.zs * self.cs), d // self.cs % self.zs, d % self.cs
+        return (lax.rem(f + df, self.fs), lax.rem(z + dz, self.zs), lax.rem(c + dc, self.cs))
+
+    def index(self, place):
+        return (place[0] * self.zs + place[1]) * self.cs + place[2]
+
+    def back(self, d):
+        f, z, c = (lax.axis_index(a) for a in ("fsdp", "z", "core"))
+        df, dz, dc = d // (self.zs * self.cs), d // self.cs % self.zs, d % self.cs
+        return self.index((
+            lax.rem(f + self.fs - df, self.fs), lax.rem(z + self.zs - dz, self.zs),
+            lax.rem(c + self.cs - dc, self.cs),
+        ))
+
+    def greet(self):
         bar = pltpu.get_barrier_semaphore()
-
-        def greet(d, carry):
-            pl.semaphore_signal(
-                bar, inc=1, device_id=self.place(self.other(d)), device_id_type=MESH_ID
-            )
-            return carry
-
-        lax.fori_loop(1, self.n, greet, 0)
-        pl.semaphore_wait(bar, self.n - 1)
+        for d in range(1, self.n):
+            pl.semaphore_signal(bar, inc=1, device_id=self.place(d), device_id_type=MESH_ID)
+
+    def met(self):
+        pl.semaphore_wait(pltpu.get_barrier_semaphore(), self.n - 1)
 
     def copy(self, d, x_ref, spread_out, slots, send, recv):
-        src = x_ref.at[self.other(d)] if spread_out else x_ref.at[0]
-        return remote_copy(
-            src, slots.at[self.me], send.at[d], recv.at[d], self.place(self.other(d))
-        )
+        to = self.place(d)
+        src = x_ref.at[self.index(to)] if spread_out else x_ref.at[0]
+        return remote_copy(src, slots.at[self.me], send.at[d], recv.at[d], to)
 
     def begin(self, x_ref, spread_out, slots, send, recv, own_sem):
-        def one(d, carry):
+        for d in range(1, self.n):
             self.copy(d, x_ref, spread_out, slots, send, recv).start()
-            return carry
-
-        lax.fori_loop(1, self.n, one, 0)
         src = x_ref.at[self.me] if spread_out else x_ref.at[0]
         own = pltpu.make_async_copy(src, slots.at[self.me], own_sem)
         own.start()
         own.wait()
 
     def finish(self, x_ref, spread_out, slots, send, recv):
-        def one(d, carry):
-            landed(slots.at[lax.rem(self.me + self.n - d, self.n)], recv.at[d])
+        for d in range(1, self.n):
+            landed(slots.at[self.back(d)], recv.at[d])
+        for d in range(1, self.n):
             self.copy(d, x_ref, spread_out, slots, send, recv).wait_send()
-            return carry
-
-        lax.fori_loop(1, self.n, one, 0)
-
-
-def dot_scatter_kernel(fs, zs, dims, tile, swaps, a_ref, w_ref, *refs):
+
+
+def dot_scatter_kernel(fs, dims, tile, beside, a_ref, w_ref, *refs):
     plane = Plane(fs)
-    if swaps:
-        Everyone((fs, zs, 2)).barrier()
-        swap = Swap(refs[0], refs[2], refs[3:9])
-        out_ref, scratch = refs[1], refs[9:]
+    plane.barrier()
+    if beside:
+        l_hbm, r_hbm, out_ref, g_ref, l_ref, r_ref, l_sem, r_sem = refs[:8]
+        scratch = refs[8:]
+        loads = [
+            pltpu.make_async_copy(l_hbm, l_ref, l_sem), pltpu.make_async_copy(r_hbm, r_ref, r_sem)
+        ]
+        for load in loads:
+            load.start()
     else:
-        plane.barrier()
         out_ref, scratch = refs[0], refs[1:]
 
     def partial(slot, cols):
@@ -736,101 +857,168 @@
         return dotf(a, w_ref[:, cols] if dims == NN else w_ref[cols, :], dims)
 
     actions = scatter_actions(plane, partial, tile, out_ref.shape[2], out_ref, scratch)
-    if swaps:
-        swap.start()
-    for i, action in enumerate(actions):
+    first = 2 * fs
+    for action in actions[:first]:
         action()
-        if swaps and i == 2 * fs:
-            swap.hand_on()
-    if swaps:
-        swap.close()
-
-
-def plane_dot_scatter(a, w, dims, seqs, collective_id, swapped=None):
-    fs, zs = lax.axis_size("fsdp"), lax.axis_size("z")
+    if beside:
+        for load in loads:
+            load.wait()
+        block = 256
+
+        def one(i, carry):
+            here = pl.ds(pl.multiple_of(i * block, block), block)
+            g_ref[here, :] = dotf(l_ref[:, here].T, r_ref[...]).astype(g_ref.dtype)
+            return carry
+
+        steps = l_ref.shape[1] // block
+        lax.fori_loop(0, steps // 2, one, 0)
+    middle = first + len(actions[first:-1]) - 2
+    for action in actions[first:middle]:
+        action()
+    if beside:
+        lax.fori_loop(steps // 2, steps, one, 0)
+    for action in actions[middle:]:
+        action()
+
+
+def plane_dot_scatter(a, w, dims, seqs, collective_id, beside=None):
+    fs = lax.axis_size("fsdp")
     a = a.reshape(seqs, 2 * fs, -1, a.shape[1])
     b = a.shape[2]
     width = w.shape[1] if dims == NN else w.shape[0]
     out_shape = [jax.ShapeDtypeStruct((seqs, b, width), jnp.float32)]
-    args, scratch = [a, w], scatter_scratch(fs, b, width)
-    if swapped is not None:
-        out_shape.append(jax.ShapeDtypeStruct(swapped.shape, swapped.dtype))
-        args.append(swapped)
-        scratch = Swap.scratch(zs, b, width) + scratch
+    args = [a, w]
+    scratch = scatter_scratch(fs, b, width)
+    if beside is not None:
+        l, r = beside
+        args += [l, r]
+        dma = pltpu.SemaphoreType.DMA
+        scratch = [pltpu.VMEM(l.shape, l.dtype), pltpu.VMEM(r.shape, r.dtype), dma, dma] + scratch
+        out_shape.append(jax.ShapeDtypeStruct((l.shape[1], r.shape[1]), jnp.bfloat16))
     out = pl.pallas_call(
-        functools.partial(dot_scatter_kernel, fs, zs, dims, 256, swapped is not None),
+        functools.partial(dot_scatter_kernel, fs, dims, 256, beside is not None),
         out_shape=out_shape,
-        in_specs=[vmem()] * len(args),
-        out_specs=[vmem()] + [anywhere()] * (len(args) - 2),
+        in_specs=[vmem()] * 2 + [anywhere()] * (len(args) - 2),
+        out_specs=[vmem()] * len(out_shape),
         scratch_shapes=scratch,
-        compiler_params=plane_params(collective_id),
+        compiler_params=plane_params(collective_id, 62),
         cost_estimate=estimate(45),
         name="plane_dot_scatter",
     )(*args)
     rows = out[0].reshape(-1, width)
-    return rows if swapped is None else (rows, out[1])
+    return rows if beside is None else (rows, out[1])
 
 
 GELU_C = math.sqrt(2.0 / math.pi)
 
 
-def gather_ffn_kernel(fs, x_ref, g_ref, wgu_ref, wd_ref, full_ref, h_ref, ggu_ref, buf_ref, *sems):
+def gather_ffn_kernel(
+    fs, x_ref, gh_hbm, g_hbm, wgu_ref, full_ref, h_ref, ggu_ref, wg_ref,
+    buf_ref, gh_ref, g_ref, acc_ref, *sems
+):
     plane = Plane(fs)
+    gh_sem, g_sem = sems[5:]
+    loads = [
+        pltpu.make_async_copy(gh_hbm, gh_ref, gh_sem), pltpu.make_async_copy(g_hbm, g_ref, g_sem)
+    ]
+    for load in loads:
+        load.start()
     plane.barrier()
     keep_sem = sems[4]
-    ff = wd_ref.shape[0]
+    ff = h_ref.shape[3]
+    b, width = buf_ref.shape[2:]
     kept = []
 
-    def consume(p, slot, ref):
-        cp = pltpu.make_async_copy(ref, full_ref.at[p, slot], keep_sem.at[len(kept)])
+    def consume(p, slot):
+        two = pl.ds(slot, 2)
+        cp = pltpu.make_async_copy(
+            buf_ref.at[p, two], full_ref.at[p, two], keep_sem.at[len(kept)]
+        )
         cp.start()
+        if not kept:
+            for load in loads:
+                load.wait()
+            acc_ref[...] = jnp.zeros_like(acc_ref)
         kept.append(cp)
-        gate = dotf(ref[...], wgu_ref[:, :ff])
-        up = dotf(ref[...], wgu_ref[:, ff:])
-        grad_hidden = dotf(g_ref[p, slot], wd_ref[...], NT)
+        rows = buf_ref[p, two].reshape(2 * b, width)
+        gate = dotf(rows, wgu_ref[:, :ff])
+        up = dotf(rows, wgu_ref[:, ff:])
+        grad_hidden = gh_ref[p, two].reshape(2 * b, ff)
         square = gate * gate
         tanh = jnp.tanh(GELU_C * gate * (1.0 + 0.044715 * square))
         half = 0.5 * (1.0 + tanh)
         act = gate * half
         slope = half + (0.5 * GELU_C) * gate * (1.0 - tanh * tanh) * (1.0 + 0.134145 * square)
-        h_ref[p, slot] = (act * up).astype(jnp.bfloat16)
-        ggu_ref[p, slot, :, :ff] = (grad_hidden * up * slope).astype(jnp.bfloat16)
-        ggu_ref[p, slot, :, ff:] = (grad_hidden * act).astype(jnp.bfloat16)
+        hidden = (act * up).astype(jnp.bfloat16)
+
+        def put(ref, cols, value):
+            ref[p, two, :, cols] = value.astype(jnp.bfloat16).reshape(2, b, ff)
+
+        put(h_ref, slice(0, ff), hidden)
+        put(ggu_ref, slice(0, ff), grad_hidden * up * slope)
+        put(ggu_ref, slice(ff, 2 * ff), grad_hidden * act)
+        hidden_t = hidden.T
+
+        def grad(j, carry):
+            cols = pl.ds(pl.multiple_of(j * 256, 256), 256)
+            acc_ref[:, cols] += dotf(hidden_t, g_ref[p, two, :, cols].reshape(2 * b, 256))
+            return carry
+
+        lax.fori_loop(0, width // 256, grad, 0)
 
     run_gather(plane, x_ref, buf_ref, sems[:4], consume)
+    wg_ref[...] = acc_ref[...].astype(jnp.bfloat16)
     for cp in kept:
         cp.wait()
 
 
-def plane_gather_ffn(x, grad, w_gu, w_d, seqs, collective_id):
+def plane_gather_ffn(x, grad_hidden, grad, w_gu, seqs, collective_id):
     fs = lax.axis_size("fsdp")
     x = x.reshape(seqs, -1, x.shape[1])
     _, b, width = x.shape
-    ff = w_d.shape[0]
+    ff = grad_hidden.shape[1]
     lead = (seqs, 2 * fs, b)
-    full, h, ggu = pl.pallas_call(
+    dma = pltpu.SemaphoreType.DMA
+    full, h, ggu, wg = pl.pallas_call(
         functools.partial(gather_ffn_kernel, fs),
         out_shape=[
             jax.ShapeDtypeStruct(lead + (width,), x.dtype),
             jax.ShapeDtypeStruct(lead + (ff,), jnp.bfloat16),
             jax.ShapeDtypeStruct(lead + (2 * ff,), jnp.bfloat16),
+            jax.ShapeDtypeStruct((ff, width), jnp.bfloat16),
         ],
-        in_specs=[vmem()] * 4,
-        out_specs=[anywhere(), vmem(), vmem()],
-        scratch_shapes=[pltpu.VMEM(lead + (width,), x.dtype)]
+        in_specs=[vmem(), anywhere(), anywhere(), vmem()],
+        out_specs=[anywhere(), vmem(), vmem(), vmem()],
+        scratch_shapes=[
+            pltpu.VMEM(lead + (width,), x.dtype),
+            pltpu.VMEM(lead + (ff,), jnp.float32),
+            pltpu.VMEM(lead + (width,), x.dtype),
+            pltpu.VMEM((ff, width), jnp.float32),
+        ]
         + gather_sems(fs)
-        + [pltpu.SemaphoreType.DMA((seqs * 2 * fs,))],
-        compiler_params=plane_params(collective_id),
+        + [dma((seqs * fs,)), dma, dma],
+        compiler_params=plane_params(collective_id, 62),
         cost_estimate=estimate(45),
         name="plane_gather_ffn",
-    )(x, grad.reshape(lead + (width,)), w_gu, w_d)
-    return full.reshape(-1, width), h.reshape(-1, ff), ggu.reshape(-1, 2 * ff)
+    )(x, grad_hidden.reshape(lead + (ff,)), grad.reshape(lead + (width,)), w_gu)
+    return full.reshape(-1, width), h.reshape(-1, ff), ggu.reshape(-1, 2 * ff), wg
+
+def column_runs(sizes, per_device, total, natural):
+    fs, zs, cs = sizes
+    if not natural:
+        size = total // (fs * cs)
+        return [(t * size, t, 0, size) for t in range(fs * cs)]
+    return [
+        (((f * zs + z) * cs + c) * per_device, f * cs + c, z * per_device, per_device)
+        for f in range(fs) for z in range(zs) for c in range(cs)
+    ]
+
 
 def start_kernel(
-    sizes, small_ref, qkv_ref, gu_ref, tok_ref, cot_ref, o_ref, d_ref,
+    sizes, runs, small_ref, q_ref, k_ref, v_ref, gate_ref, up_ref, tok_ref, cot_ref, o_ref, d_ref,
     small_out, wqkv_ref, ggu_ref, x_ref, g_ref, o_out, d_out,
-    slots, s_send, s_recv, own_sem, q_send, q_recv, g_send, g_recv, line_send, line_recv,
-    *swap_scratch,
+    slots, qkv_ref, gu_ref, s_send, s_recv, own_sem, q_send, q_recv, g_send, g_recv,
+    line_send, line_recv, *swap_scratch,
 ):
     fs, zs, cs = sizes
     f, z, c = (lax.axis_index(a) for a in ("fsdp", "z", "core"))
@@ -838,12 +1026,22 @@
     devices = fs * cs
     rows = qkv_ref.shape[1]
     everyone = Everyone(sizes)
-    everyone.barrier()
-    everyone.begin(small_ref, False, slots, s_send, s_recv, own_sem.at[0])
+    everyone.greet()
+
+    def split(pieces_ref, parts, run):
+        size = pieces_ref.shape[2] // len(parts)
+        for i, part in enumerate(parts):
+            for at, device, start, count in run:
+                here = part[:, at : at + count].astype(jnp.bfloat16)
+                pieces_ref[device, :, i * size + start : i * size + start + count] = here
+
+    split(qkv_ref, (q_ref, k_ref, v_ref), runs[1])
     half = len(swap_scratch) // 2
     swaps = [
         Swap(tok_ref, x_ref, swap_scratch[:half]), Swap(cot_ref, g_ref, swap_scratch[half:])
     ]
+    everyone.met()
+    everyone.begin(small_ref, False, slots, s_send, s_recv, own_sem.at[0])
 
     def block(out_ref, index, lead):
         at = pl.ds(pl.multiple_of(lax.rem(index, cs) * rows, rows), rows)
@@ -860,18 +1058,14 @@
 
     own_qkv = pltpu.make_async_copy(qkv_ref.at[me], block(wqkv_ref, me, z), own_sem.at[1])
     own_gu = pltpu.make_async_copy(gu_ref.at[me], block(ggu_ref, me, None), own_sem.at[2])
-    later = [
-        pltpu.make_async_copy(o_ref, o_out, own_sem.at[3]),
-        pltpu.make_async_copy(d_ref, d_out, own_sem.at[4]),
-    ]
-    for copy in later:
-        copy.start()
     own_qkv.start()
     for d in range(1, devices):
         spread_copy(d, qkv_ref, wqkv_ref, z, q_send, q_recv).start()
+    swaps[0].start()
+    split(gu_ref, (gate_ref, up_ref), runs[0])
     own_gu.start()
-
-    swaps[0].start()
+    o_out[...] = o_ref[...].astype(jnp.bfloat16)
+    d_out[...] = d_ref[...].astype(jnp.bfloat16)
     own_qkv.wait()
     for d in range(1, devices):
         landed(block(wqkv_ref, lax.rem(me + devices - d, devices), z), q_recv.at[d])
@@ -903,11 +1097,12 @@
             def _(step=step, way=way):
                 line(step, way).start()
 
-        if step == 1:
-            swaps[1].start()
         if step == 0:
+            swaps[1].start_inward()
             for d in range(1, devices):
                 spread_copy(d, gu_ref, ggu_ref, None, g_send, g_recv).start()
+        if step == 1:
+            swaps[1].start_straight()
         for way in (1, -1):
 
             @pl.when(arrives(step, way))
@@ -920,8 +1115,6 @@
     everyone.finish(small_ref, False, slots, s_send, s_recv)
     small_out[...] = slots[...]
     own_gu.wait()
-    for copy in later:
-        copy.wait()
     for d in range(1, devices):
         landed(block(ggu_ref, lax.rem(me + devices - d, devices), None), g_recv.at[d])
     for d in range(1, devices):
@@ -938,70 +1131,102 @@
         swap.close()
 
 
-def start(small, qkv_pieces, gu_pieces, tokens, cotangent, own_o, own_d, collective_id):
+def start(small, qkv, gu, tokens, cotangent, own_o, own_d, runs, collective_id):
     sizes = tuple(lax.axis_size(a) for a in ("fsdp", "z", "core"))
     fs, zs, cs = sizes
     n = math.prod(sizes)
-    devices, rows, qkv_cols = qkv_pieces.shape
+    devices = fs * cs
+    rows = qkv[0].shape[0]
+    qkv_cols = sum(w.shape[1] for w in qkv) // devices
+    gu_cols = sum(w.shape[1] for w in gu) // devices
     dma = pltpu.SemaphoreType.DMA
     return pl.pallas_call(
-        functools.partial(start_kernel, sizes),
+        functools.partial(start_kernel, sizes, runs),
         out_shape=[
             jax.ShapeDtypeStruct((n, 8, 128), jnp.float32),
             jax.ShapeDtypeStruct((fs, zs, cs * rows, qkv_cols), jnp.bfloat16),
-            jax.ShapeDtypeStruct((fs, cs * rows, gu_pieces.shape[2]), jnp.bfloat16),
+            jax.ShapeDtypeStruct((fs, cs * rows, gu_cols), jnp.bfloat16),
             jax.ShapeDtypeStruct(tokens.shape, tokens.dtype),
             jax.ShapeDtypeStruct(cotangent.shape, cotangent.dtype),
-            jax.ShapeDtypeStruct(own_o.shape, own_o.dtype),
-            jax.ShapeDtypeStruct(own_d.shape, own_d.dtype),
+            jax.ShapeDtypeStruct(own_o.shape, jnp.bfloat16),
+            jax.ShapeDtypeStruct(own_d.shape, jnp.bfloat16),
         ],
-        in_specs=[vmem()] * 7,
-        out_specs=[vmem()] + [anywhere()] * 6,
+        in_specs=[vmem()] * 10,
+        out_specs=[vmem()] + [anywhere()] * 4 + [vmem()] * 2,
         scratch_shapes=[
             pltpu.VMEM((n, 8, 128), jnp.float32),
-            dma((n,)), dma((n,)), dma((5,)),
+            pltpu.VMEM((devices, rows, qkv_cols), jnp.bfloat16),
+            pltpu.VMEM((devices, rows, gu_cols), jnp.bfloat16),
+            dma((n,)), dma((n,)), dma((3,)),
             dma((devices,)), dma((devices,)), dma((devices,)), dma((devices,)),
             dma((2, zs)), dma((2, zs)),
         ]
-        + Swap.scratch(zs, *tokens.shape[1:]) * 2,
+        + Swap.scratch(fs, *tokens.shape) * 2,
         compiler_params=plane_params(collective_id),
         cost_estimate=estimate(120),
         name="start",
-    )(small, qkv_pieces, gu_pieces, tokens, cotangent, own_o, own_d)
+    )(small, *qkv, *gu, tokens, cotangent, own_o, own_d)
 
 
 def finish_kernel(
-    sizes, small_ref, g_ref, small_out, out_ref, slots, send, recv, own_sem, *swap_scratch
+    sizes, runs, small_ref, g_ref, qkv_ref, gu_ref, small_out, out_ref, gate_ref, up_ref,
+    q_ref, k_ref, v_ref, slots, got_qkv, send, recv, own_sem, back_send, back_recv, back_sem,
+    *swap_scratch
 ):
     everyone = Everyone(sizes)
-    everyone.barrier()
+    everyone.greet()
+    back = Back(sizes, qkv_ref, got_qkv, (back_send, back_recv, back_sem))
+    swap = Swap(g_ref, out_ref, swap_scratch)
+    everyone.met()
+    swap.start()
     everyone.begin(small_ref, True, slots, send, recv, own_sem)
-    swap = Swap(g_ref, out_ref, swap_scratch)
-    swap.start()
+    back.start()
     swap.hand_on()
+
+    def join(got_ref, pieces, run):
+        size = got_ref.shape[2] // len(pieces)
+        for i, piece in enumerate(pieces):
+            for to, device, start, count in run:
+                part = got_ref[device, :, i * size + start : i * size + start + count]
+                piece[:, to : to + count] = part.astype(jnp.float32)
+
+    join(gu_ref, (gate_ref, up_ref), runs[0])
+    back.arrived()
+    join(got_qkv, (q_ref, k_ref, v_ref), runs[1])
     everyone.finish(small_ref, True, slots, send, recv)
     small_out[...] = jnp.sum(slots[...], axis=0)
+    back.close()
     swap.close()
 
 
-def finish(small, grad, collective_id):
+def finish(small, grad, sum_qkv, got_gu, runs, columns, collective_id):
     sizes = tuple(lax.axis_size(a) for a in ("fsdp", "z", "core"))
+    fs, zs, cs = sizes
     n = math.prod(sizes)
+    devices = fs * cs
     dma = pltpu.SemaphoreType.DMA
+    sum_qkv = sum_qkv.reshape(devices, -1, sum_qkv.shape[2])
+    wide = [jax.ShapeDtypeStruct((sum_qkv.shape[1], k), jnp.float32) for k in columns]
     return pl.pallas_call(
-        functools.partial(finish_kernel, sizes),
+        functools.partial(finish_kernel, sizes, runs),
         out_shape=[
             jax.ShapeDtypeStruct((8, 128), small.dtype),
             jax.ShapeDtypeStruct(grad.shape, grad.dtype),
-        ],
-        in_specs=[vmem(), vmem()],
-        out_specs=[vmem(), anywhere()],
-        scratch_shapes=[pltpu.VMEM((n, 8, 128), small.dtype), dma((n,)), dma((n,)), dma]
-        + Swap.scratch(sizes[1], *grad.shape[1:]),
+        ]
+        + wide,
+        in_specs=[vmem()] * 4,
+        out_specs=[vmem(), anywhere()] + [vmem()] * len(wide),
+        scratch_shapes=[
+            pltpu.VMEM((n, 8, 128), small.dtype),
+            pltpu.VMEM(sum_qkv.shape, jnp.bfloat16),
+            dma((n,)), dma((n,)), dma,
+        ]
+        + Back.scratch(devices)
+        + Swap.scratch(fs, *grad.shape),
         compiler_params=plane_params(collective_id),
         cost_estimate=estimate(45),
         name="finish",
-    )(small, grad)
+    )(small, grad, sum_qkv, got_gu)
 
 
 def to_tiles(x):
@@ -1060,13 +1285,18 @@
         size = both.shape[0] // self.c
         return lax.dynamic_slice_in_dim(both, lax.axis_index("core") * size, size, 0)
 
-    def scatter(self, g):
+    def whole(self, g):
         if self.natural:
-            return lax.psum_scatter(g, "z", scatter_dimension=0, tiled=True)
+            return g
         size = g.shape[0]
         both = jnp.zeros((size * self.c, g.shape[1]), g.dtype)
         both = lax.dynamic_update_slice_in_dim(both, g, lax.axis_index("core") * size, 0)
-        return lax.psum_scatter(both, ("z", "core"), scatter_dimension=0, tiled=True)
+        both = lax.psum(both, "core").reshape(self.z, self.c, -1, g.shape[1])
+        mine = lax.dynamic_index_in_dim(both, lax.axis_index("core"), 1, keepdims=False)
+        return mine.reshape(-1, g.shape[1])
+
+    def scatter(self, g):
+        return lax.psum_scatter(g, "z", scatter_dimension=0, tiled=True)
 
 
 def over_z(got):
@@ -1079,14 +1309,6 @@
     f, z = lax.axis_size("fsdp"), lax.axis_size("z")
     return lax.psum_scatter(
         grad.reshape(f, grad.shape[0] // f, -1), "z", scatter_dimension=1, tiled=True
-    )
-
-
-def unspread(part):
-    f, cr, cols = part.shape
-    c = lax.axis_size("core")
-    return lax.all_to_all(
-        part.reshape(f * c, cr // c, cols), TP, split_axis=0, concat_axis=0, tiled=True
     )
 
 
@@ -1106,13 +1328,14 @@
 
     own_small = jnp.concatenate([norm1_gain, norm2_gain, rel_bias]).astype(BF).astype(F32)
     own_small = jnp.concatenate([own_small, lengths.astype(F32)])
-    qkv_pieces = jnp.concatenate(
-        [head_cols.split(w.astype(BF)) for w in (w_query, w_key, w_value)], axis=2
+    sizes = (fs, zs, cs)
+    runs = (
+        column_runs(sizes, ff_cols.per_device, w_gate.shape[1], True),
+        column_runs(sizes, head_cols.per_device, w_query.shape[1], head_cols.natural),
     )
-    ff_pieces = jnp.concatenate([ff_cols.split(w.astype(BF)) for w in (w_gate, w_up)], axis=2)
     small, w_qkv, got_gu, x_in, cot, own_o, own_d = start(
-        to_tiles(own_small[None]), qkv_pieces, ff_pieces, tokens, cotangent,
-        w_attn_out.astype(BF), w_down.astype(BF), 9,
+        to_tiles(own_small[None]), (w_query, w_key, w_value), (w_gate, w_up),
+        tokens.reshape(rows, width), cotangent.reshape(rows, width), w_attn_out, w_down, runs, 9,
     )
     w_qkv = w_qkv.reshape(width, -1)
     w_o = head_cols.gather(own_o)
@@ -1141,50 +1364,47 @@
     x = x_in.reshape(rows, width).astype(F32)
     scale_one = rms_scale(x)
     grad_rows = cot.reshape(rows, width).astype(F32) * valid
-    grad_branch = plane_gather(grad_rows.astype(BF), seqs, 1)
 
     normed, qkv = plane_gather_dot((x * scale_one * gain_one).astype(BF), w_qkv, NN, seqs, 2)
     attended, lse = attn_fwd(qkv, offset_bias, lens, heads, head_dim, seqs)
-    hidden_one = x + plane_dot_scatter(attended, w_o, NN, seqs, 3)
+    attn_sum = plane_dot_scatter(attended, w_o, NN, seqs, 3)
+    branch = grad_rows.astype(BF)
+    branch, attn_sum = lax.optimization_barrier((branch, attn_sum))
+    grad_branch, grad_hidden = plane_gather_dot(branch, w_d, NT, seqs, 1, dtype=F32)
+    hidden_one = x + attn_sum
     scale_two = rms_scale(hidden_one)
-    normed_two, hidden_ff, grad_gu = plane_gather_ffn(
-        (hidden_one * scale_two * gain_two).astype(BF), grad_branch, w_gu, w_d, seqs, 4
+    normed_two, hidden_ff, grad_gu, grad_w_down = plane_gather_ffn(
+        (hidden_one * scale_two * gain_two).astype(BF), grad_hidden, grad_branch, w_gu, seqs, 4
     )
-    grad_w_down = jnp.einsum("rf,rd->fd", hidden_ff, grad_branch, preferred_element_type=F32)
-    grad_w_gu = jnp.einsum("rd,rf->df", normed_two, grad_gu, preferred_element_type=F32)
-    grad_w_down, grad_gu = lax.optimization_barrier((grad_w_down.astype(BF), grad_gu))
     sum_down = ff_cols.scatter(grad_w_down)
-    grad_w_gu, grad_gu = lax.optimization_barrier((grad_w_gu.astype(BF), grad_gu))
-    grad_normed_two = plane_dot_scatter(grad_gu, w_gu, NT, seqs, 5)
-    grad_w_gu, grad_normed_two, sum_down = lax.optimization_barrier(
-        (grad_w_gu, grad_normed_two, sum_down)
-    )
-    sum_gu = reduce_z(grad_w_gu)
-    gain_two_part = jnp.sum(grad_normed_two * hidden_one * scale_two, axis=0)
-    grad_hidden_one = grad_rows + norm_back(grad_normed_two, hidden_one, scale_two, gain_two)
-    grad_attn, grad_attended = plane_gather_dot(grad_hidden_one.astype(BF), w_o, NT, seqs, 6)
-
-
-    grad_w_o = jnp.einsum("rk,rd->kd", attended, grad_attn, preferred_element_type=F32)
-    grad_w_o, grad_attended = lax.optimization_barrier((grad_w_o.astype(BF), grad_attended))
     if fs <= 4:
-        dq, dk, dv, grad_offset, ff_sum = attn_bwd(
-            qkv, grad_attended, lse, offset_bias, lens, heads, head_dim, seqs,
-            product=(hidden_ff, w_d), collective_id=7,
+        ff_sum, grad_w_gu = plane_dot_scatter(
+            hidden_ff, w_d, NN, seqs, 7, beside=(normed_two, grad_gu)
         )
     else:
         ff_sum = plane_dot_scatter(hidden_ff, w_d, NN, seqs, 7)
-        dq, dk, dv, grad_offset = attn_bwd(
-            qkv, grad_attended, lse, offset_bias, lens, heads, head_dim, seqs
-        )
-    result = ((hidden_one + ff_sum) * valid).astype(BF).reshape(seqs, block_len, width)
+        grad_w_gu = jnp.einsum("rd,rf->df", normed_two, grad_gu, preferred_element_type=F32)
+        grad_w_gu = grad_w_gu.astype(BF)
+    result = ((hidden_one + ff_sum) * valid).astype(BF)
+    grad_w_gu, sum_down, grad_gu = lax.optimization_barrier((grad_w_gu, sum_down, grad_gu))
+    sum_gu = reduce_z(grad_w_gu)
+    grad_normed_two = plane_dot_scatter(grad_gu, w_gu, NT, seqs, 5)
+    gain_two_part = jnp.sum(grad_normed_two * hidden_one * scale_two, axis=0)
+    grad_hidden_one = grad_rows + norm_back(grad_normed_two, hidden_one, scale_two, gain_two)
+    grad_attn, grad_attended, grad_w_o = plane_gather_dot(
+        grad_hidden_one.astype(BF), w_o, NT, seqs, 6, other=attended
+    )
+    dq, dk, dv, grad_offset, output, sum_o, got_gu = attn_bwd(
+        qkv, grad_attended, lse, offset_bias, lens, heads, head_dim, seqs,
+        swapped=result, column=head_cols.whole(grad_w_o), spread=sum_gu, collective_id=11,
+    )
+    output = output.reshape(seqs, block_len, width)
     dqkv = jnp.concatenate([dq, dk, dv], axis=1)
     grad_w_qkv = jnp.einsum("rd,rk->dk", normed, dqkv, preferred_element_type=F32)
     grad_w_qkv, dqkv = lax.optimization_barrier((grad_w_qkv.astype(BF), dqkv))
-    grad_w_qkv, grad_w_o, sum_gu = lax.optimization_barrier((grad_w_qkv, grad_w_o, sum_gu))
+    grad_w_qkv, sum_gu = lax.optimization_barrier((grad_w_qkv, sum_gu))
     sum_qkv = reduce_z(grad_w_qkv)
-    sum_o = head_cols.scatter(grad_w_o)
-    grad_normed, output = plane_dot_scatter(dqkv, w_qkv, NT, seqs, 8, swapped=result)
+    grad_normed = plane_dot_scatter(dqkv, w_qkv, NT, seqs, 8)
     gain_one_part = jnp.sum(grad_normed * x * scale_one, axis=0)
     grad_x = grad_hidden_one + norm_back(grad_normed, x, scale_one, gain_one)
 
@@ -1201,30 +1421,24 @@
         ],
         axis=1,
     )
-    small_sum, grad_tokens = finish(
-        to_tiles(small_grad), grad_x.astype(BF).reshape(seqs, block_len, width), 10
+    columns = (w_gate.shape[1],) * 2 + (w_query.shape[1],) * 3
+    small_sum, grad_tokens, grad_gate_w, grad_up_w, grad_q_w, grad_k_w, grad_v_w = finish(
+        to_tiles(small_grad), grad_x.astype(BF), sum_qkv, got_gu, runs, columns, 10
     )
+    grad_tokens = grad_tokens.reshape(seqs, block_len, width)
     small_grad = small_sum.reshape(-1)[: small_grad.shape[1]]
-
-    got_gu = unspread(sum_gu)
-    got_qkv = unspread(sum_qkv)
-    hw = heads * head_dim
-    grads_qkv = [
-        head_cols.join(got_qkv[:, :, i * hw : (i + 1) * hw]).astype(F32) for i in range(3)
-    ]
-    grads_gu = [ff_cols.join(got_gu[:, :, i * ff : (i + 1) * ff]).astype(F32) for i in range(2)]
     return (
         output,
         grad_tokens,
         small_grad[:g],
         small_grad[2 * g :],
-        grads_qkv[0],
-        grads_qkv[1],
-        grads_qkv[2],
-        sum_o.astype(F32),
+        grad_q_w,
+        grad_k_w,
+        grad_v_w,
+        sum_o,
         small_grad[g : 2 * g],
-        grads_gu[0],
-        grads_gu[1],
+        grad_gate_w,
+        grad_up_w,
         sum_down.astype(F32),
     )
 

time: 883 us -> 728 us (0.82)
  Pallas kernels: 690 us -> 636 us
  matrix products: 45.8 us -> 13.2 us
  local copies, waits for them, and re-layouts: 51 us -> 18.8 us
  other arithmetic: 40.1 us -> 23.3 us
  starting transfers between devices: 11.7 us -> 0.41 us
    dot_general x3 -> x0, matrix products: 33.5 us -> none  [the longest x1 16.8 us: shards(): jnp.einsum('rd,rf->df', normed_two, grad_gu, preferred_element_type=F32)]
    pallas_call x8 -> x9, Pallas kernels: 533 us -> 504 us  [the longest x4 199 us: plane_dot_scatter(): pl.pallas_call(functools.partial(dot_scatter_kernel, fs, dims, 256, besid...]
    convert_element_type x15 -> x0, local copies, waits for them, and re-layouts: 28.8 us -> none  [the longest x6 19.8 us: shards(): ff_cols.join(got_gu[:, :, i * ff:(i + 1) * ff]).astype(F32)]
    pallas_call x1, Pallas kernels: 74.8 us -> 53.1 us  [attn_bwd(): pl.pallas_call(functools.partial(attn_bwd_kernel, heads, head_dim, block,...]
    convert_element_type x12 -> x1, other arithmetic: 18.6 us -> 3.22 us  [shards(): grad_x.astype(BF)]
    all_to_all x2 -> x0, starting transfers between devices: 11 us -> none  [unspread(): lax.all_to_all(part.reshape(f * c, cr // c, cols), TP, split_axis=0, conc...]
  transfers between devices with their start and end apart: 9 -> 6, of which waited for: 2 -> 3; matrix products, arithmetic and copies ran while one was open for 10% -> 4% of each run, Pallas kernels for 56% -> 52%
where the time goes in v3:
time: 728 us; the launch traced here: 723 us
  Pallas kernels  636 us (87%)
  other arithmetic  23.3 us (3%)
  local copies, waits for them, and re-layouts  18.8 us (3%)
  waiting for transfers between devices  16.6 us (2%)
  between operations  14.7 us (2%)
  matrix products  13.2 us (2%)
    pallas_call x4, Pallas kernels, plane_dot_scatter(): pl.pallas_call(functools.partial(dot_scatter_kernel, fs, dims, 256, besid...  199 us
    pallas_call x3, Pallas kernels, plane_gather_dot(): pl.pallas_call(functools.partial(gather_dot_kernel, fs, dims, tile, other...  155 us
    pallas_call x1, Pallas kernels, start(): pl.pallas_call(functools.partial(start_kernel, sizes, runs), out_shape=[j...  106 us
    pallas_call x1, Pallas kernels, plane_gather_ffn(): pl.pallas_call(functools.partial(gather_ffn_kernel, fs), out_shape=[jax.S...  53.7 us
    pallas_call x1, Pallas kernels, attn_bwd(): pl.pallas_call(functools.partial(attn_bwd_kernel, heads, head_dim, block,...  53.1 us
    pallas_call x1, Pallas kernels, finish(): pl.pallas_call(functools.partial(finish_kernel, sizes, runs), out_shape=[...  43.4 us
    pallas_call x1, Pallas kernels, attn_fwd(): pl.pallas_call(functools.partial(attn_fwd_kernel, heads, head_dim, block,...  25.6 us
  transfers between devices with their start and end apart: 6, of which 3 were waited for; matrix products, arithmetic and copies ran while one was open for 4% of the time, Pallas kernels for 52%

profile of v3, /device:TPU:22, one launch (start us, length us, event | category | flops | bytes accessed | tf_op | source)
XLA Modules:
  0.0 723.1 jit_solution(3230053611915331930)
XLA Ops:
  7.2 0.7 convert.12
  7.9 0.7 convert.13
  8.5 0.7 convert.14
  9.2 0.7 convert_element_type.60
  9.9 0.1 maximum_convert_fusion
  9.9 0.1 pad_maximum_fusion
  10.0 0.6 pad.15
  10.6 106.4 %start.1 = (f32[32,8,128]{2,1,0:T(8,128)}, bf16[4,4,128,768]{3,2,1,0:T(8,128)(2,1)}, bf16[4,128,1280]{2,1,0:T(8,128)(2,1)}, bf16[256,2048]{1,0:T(8,128)(2,1)}, b...) custom-call(f32[1,8,128]{2,1,0:T(8,128)} %bitcast.123, f32[64,2048]{1,0:T(8,128)} %q_ref.1, ...), custom_call_target="tpu_custom_call" | custom-call | flops 2640000000 | bytes 12000000 | tf_op jit(solution)/shard_map/start/pallas_call | solution.py:1143
  117.1 0.7 all-gather.6.cloned.1.call-update
  117.9 0.7 all-gather.8.cloned.1.call-update
  118.6 0.2 reduce-scatter.4.cloned.1.call-start
  118.8 0.1 slice.45
  118.9 0.1 fusion.29
  119.1 0.1 broadcast_in_dim.30
  119.2 0.1 mul.164
  119.3 0.3 fusion.8
  119.6 0.1 fusion.24
  119.7 1.7 fusion.2
  121.4 65.1 %plane_gather_dot.3 = (bf16[2,8,128,2048]{3,2,1,0:T(8,128)(2,1)}, bf16[2,8,128,768]{3,2,1,0:T(8,128)(2,1)}) custom-call(bf16[2,128,2048]{2,1,0:T(8,128)(2,1)} %bitcast.102, bf16[2048,768]{1,0:T(8,128)(2,1)} %bitcast.94), custom_call_target="tpu_custom_call" | custom-call | flops 990000000 | bytes 4500000 | tf_op jit(solution)/shard_map/plane_gather_dot/pallas_call | solution.py:595
  186.5 0.3 iota_compare_fusion
  186.8 1.2 fusion.17.bias_ref
  188.0 25.6 %attn_fwd.1 = (bf16[2048,256]{1,0:T(8,128)(2,1)}, f32[2048,128]{1,0:T(8,128)}) custom-call(s32[2]{0:T(128)} %copy-done.21, bf16[2048,768]{1,0:T(8,128)(2,1)} %bitcast.85, bf16[2048,768]{1,0:T(8,128)(2,1)} %bitcast.86, bf16[2048,768]{1,0:T(8,128)(2,1)} %bitcast.87, f32[4,2048]{1,0:T(4,128)} %fusion.17.bias_ref), custom_call_target="tpu_custom_call" | custom-call | flops 572000000 | bytes 2600000 | tf_op jit(solution)/shard_map/attn_fwd/pallas_call | solution.py:70
  213.6 46.0 %plane_dot_scatter.4 = f32[2,128,2048]{2,1,0:T(8,128)} custom-call(bf16[2,8,128,256]{3,2,1,0:T(8,128)(2,1)} %bitcast.112, bf16[256,2048]{1,0:T(8,128)(2,1)} %all-gather.4.cloned.1.call-done.w_ref), custom_call_target="tpu_custom_call" | custom-call | flops 990000000 | bytes 4500000 | tf_op jit(solution)/shard_map/plane_dot_scatter/pallas_call | solution.py:898
  259.6 2.0 multiply_reduce_fusion.1
  261.6 1.3 copy-done
  262.9 1.2 multiply_convert_fusion
  264.1 46.0 %plane_gather_dot.4 = (bf16[2,8,128,2048]{3,2,1,0:T(8,128)(2,1)}, f32[2,8,128,640]{3,2,1,0:T(8,128)}) custom-call(bf16[2,128,2048]{2,1,0:T(8,128)(2,1)} %bitcast.101, bf16[640,2048]{1,0:T(8,128)(2,1)} %all-gather.6.cloned.1.call-done.w_ref), custom_call_target="tpu_custom_call" | custom-call | flops 990000000 | bytes 4500000 | tf_op jit(solution)/shard_map/plane_gather_dot/pallas_call | solution.py:595
  310.1 10.0 %all-gather.8.cloned.1.call-done = bf16[4,512,1280]{2,1,0:T(8,128)(2,1)} async-done(((bf16[4,128,1280]{2,1,0:T(8,128)(2,1)}), bf16[4,512,1280]{2,1,0:T(8,128)(2,1)}) %all-gather.8.cloned.1.call-update) | async-done | bytes 5242896 | tf_op jit(solution)/shard_map/all_gather | solution.py:1304
  320.0 53.7 %plane_gather_ffn.1 = (bf16[2,8,128,2048]{3,2,1,0:T(8,128)(2,1)}, bf16[2,8,128,640]{3,2,1,0:T(8,128)(2,1)}, bf16[2,8,128,1280]{3,2,1,0:T(8,128)(2,1)}, bf16[640,2048]{1,0:T(8,128)(2,1)}) custom-call(bf16[2,128,2048]{2,1,0:T(8,128)(2,1)} %bitcast.100, f32[2,8,128,640]{3,2,1,0:T(8,128)} %get-tuple-element.65.gh_hbm, ...), custom_call_target="tpu_custom_call" | custom-call | flops 990000000 | bytes 4500000 | tf_op jit(solution)/shard_map/plane_gather_ffn/pallas_call | solution.py:982
  373.8 50.0 %plane_dot_scatter.5 = (f32[2,128,2048]{2,1,0:T(8,128)}, bf16[2048,1280]{1,0:T(8,128)(2,1)}) custom-call(bf16[2,8,128,640]{3,2,1,0:T(8,128)(2,1)} %get-tuple-element.68.a_ref, bf16[640,2048]{1,0:T(8,128)(2,1)} %all-gather.6.cloned.1.call-done.w_ref, bf16[2048,2048]{1,0:T(8,128)(2,1)} %bitcast.96, bf16[2048,1280]{1,0:T(8,128)(2,1)} %bitcast.91), custom_call_target="tpu_custom_call" | custom-call | flops 990000000 | bytes 4500000 | tf_op jit(solution)/shard_map/plane_dot_scatter/pallas_call | solution.py:898
  423.8 2.5 reduce-scatter.4.cloned.1.call-done
  426.4 51.9 %plane_dot_scatter.6 = f32[2,128,2048]{2,1,0:T(8,128)} custom-call(bf16[2,8,128,1280]{3,2,1,0:T(8,128)(2,1)} %get-tuple-element.70, bf16[2048,1280]{1,0:T(8,128)(2,1)} %bitcast.93), custom_call_target="tpu_custom_call" | custom-call | flops 990000000 | bytes 4500000 | tf_op jit(solution)/shard_map/plane_dot_scatter/pallas_call | solution.py:898
  478.3 2.9 fusion.15
  481.3 0.5 copy-done.4
  481.8 5.2 fusion.28
  487.0 43.8 %plane_gather_dot.5 = (bf16[2,8,128,2048]{3,2,1,0:T(8,128)(2,1)}, bf16[2,8,128,256]{3,2,1,0:T(8,128)(2,1)}, bf16[256,2048]{1,0:T(8,128)(2,1)}) custom-call(bf16[2,128,2048]{2,1,0:T(8,128)(2,1)} %bitcast.109, bf16[256,2048]{1,0:T(8,128)(2,1)} %all-gather.4.cloned.1.call-done.w_ref, bf16[2,8,128,256]{3,2,1,0:T(8,128)(2,1)} %bitcast.113), custom_call_target="tpu_custom_call" | custom-call | flops 990000000 | bytes 4500000 | tf_op jit(solution)/shard_map/plane_gather_dot/pallas_call | solution.py:595
  530.8 53.1 %attn_bwd.1 = (bf16[2048,256]{1,0:T(8,128)(2,1)}, bf16[2048,256]{1,0:T(8,128)(2,1)}, bf16[2048,256]{1,0:T(8,128)(2,1)}, f32[4,2048]{1,0:T(4,128)}, bf16[256,2048...) custom-call(s32[2]{0:T(128)} %copy-done.21, bf16[2048,768]{1,0:T(8,128)(2,1)} %bitcast.88, ...), custom_call_target="tpu_custom_call" | custom-call | flops 1100000000 | bytes 5000000 | tf_op jit(solution)/shard_map/attn_bwd/pallas_call | solution.py:253
  583.9 1.4 constant_dynamic-update-slice_fusion.2
  585.4 0.1 copy-done.12
  585.5 0.2 copy-done.10
  585.8 11.6 %convolution_convert_fusion = bf16[2048,768]{1,0:T(8,128)(2,1)} fusion(bf16[2048,2048]{1,0:T(8,128)(2,1)} %bitcast.127, bf16[2048,768]{1,0:T(8,128)(2,1)S(1)} %constant_dynamic-update-slice_fusion), kind=kOutput, calls=%fused_computation.5 | convolution fusion | flops 6444023808 | bytes 14680064 | tf_op jit(solution)/shard_map/rd,rk->dk/dot_general | solution.py:1403
  597.5 0.1 reshape.217
  597.6 1.0 copy-done.13
  598.5 1.2 convert_element_type.74
  599.7 51.1 %plane_dot_scatter.7 = f32[2,128,2048]{2,1,0:T(8,128)} custom-call(bf16[2,8,128,768]{3,2,1,0:T(8,128)(2,1)} %bitcast.98, bf16[2048,768]{1,0:T(8,128)(2,1)} %bitcast.95), custom_call_target="tpu_custom_call" | custom-call | flops 990000000 | bytes 4500000 | tf_op jit(solution)/shard_map/plane_dot_scatter/pallas_call | solution.py:898
  650.9 2.3 fusion.11
  653.2 0.4 fusion.19
  653.7 1.0 broadcast_in_dim.34
  654.8 1.2 slice.41
  656.0 0.1 fusion.21
  656.1 0.7 copy.31
  656.8 3.2 fusion.7.g_ref
  660.0 2.7 reduce-scatter.8.cloned.1.call-done
  662.7 43.4 %finish.1 = (f32[8,128]{1,0:T(8,128)}, bf16[256,2048]{1,0:T(8,128)(2,1)}, f32[64,5120]{1,0:T(8,128)}, f32[64,5120]{1,0:T(8,128)}, f32[64,2048]{1,0:T(8,128)}, /*index=5*/f32[64,2048]{1,0:T(8,128)}, f32[64,2048]{1,0:T(8,128)}) custom-call(f32[32,8,128]{2,1,0:T(8,128)} %bitcast.118, bf16[256,2048]{1,0:T(8,128)(2,1)} %fusion.7.g_ref, ...), custom_call_target="tpu_custom_call" | custom-call | flops 990000000 | bytes 4500000 | tf_op jit(solution)/shard_map/finish/pallas_call | solution.py:1210
  706.1 1.4 fusion.30
  707.5 1.2 slice.43
  708.7 1.0 copy.45
  709.7 1.0 copy.46
  710.7 0.8 copy.47
  711.4 0.8 copy.48
  712.2 0.8 copy.49
  713.0 0.8 copy.50
  713.8 1.1 copy.51
  714.9 1.1 copy.52
  (68 shorter events, 0.8 us)
Async XLA Ops:
  7.2 206.4 %all-gather.4.cloned.1.call-start = ((), (), s32[]{:S(2)}) async-start(), calls=%async_computation.3 | async-start | bytes 1310720 | tf_op jit(solution)/shard_map/all_gather | solution.py:1283
  117.0 1.8 copy-start.18
  117.0 2.2 copy-start.2
  117.1 147.0 %all-gather.6.cloned.1.call-start = ((), (), s32[]{:S(2)}) async-start(), calls=%async_computation.4 | async-start | bytes 3276800 | tf_op jit(solution)/shard_map/all_gather | solution.py:1283
  117.8 1.8 copy-start.6
  117.8 202.2 %all-gather.8.cloned.1.call-start = ((), (), s32[]{:S(2)}) async-start(), calls=%async_computation.5 | async-start | bytes 6553600 | tf_op jit(solution)/shard_map/all_gather | solution.py:1304
  118.6 307.7 %reduce-scatter.4.cloned.1.call-start = ((), (), s32[]{:S(2)}) async-start(), calls=%async_computation.6 | async-start | bytes 3276800 | tf_op jit(solution)/shard_map/reduce_scatter | solution.py:1299
  119.3 2.1 copy-start.21
  121.4 65.1 %copy-start.20 = (s32[2047]{0:T(1024)S(1)}, s32[2047]{0:T(1024)}, u32[]{:S(2)}) copy-start(s32[2047]{0:T(1024)} %param.17) | copy-start | bytes 24568
  261.5 1.3 copy-start
  373.8 157.0 %reduce-scatter.6.cloned.1.call-start = ((), (), s32[]{:S(2)}) async-start(), calls=%async_computation.7 | async-start | bytes 6553600 | tf_op jit(solution)/shard_map/reduce_scatter | solution.py:1310
  426.3 236.4 %reduce-scatter.8.cloned.1.call-start = ((), (), s32[]{:S(2)}) async-start(), calls=%async_computation.8 | async-start | bytes 3932160 | tf_op jit(solution)/shard_map/reduce_scatter | solution.py:1310
  478.3 3.0 copy-start.1
  478.3 3.5 copy-start.4
  583.9 1.5 copy-start.12
  583.9 1.8 copy-start.10
  585.8 11.6 %copy-start.5 = (bf16[2048,768]{1,0:T(8,128)(2,1)}, bf16[2048,768]{1,0:T(8,128)(2,1)S(1)}, u32[]{:S(2)}) copy-start(bf16[2048,768]{1,0:T(8,128)(2,1)S(1)} %constant_dynamic-update-slice_fusion) | copy-start | bytes 9437188
  597.5 1.1 copy-start.13
  650.9 2.4 copy-start.19
  650.9 5.9 copy-start.3
  660.0 48.7 %copy-start.9 = (bf16[256,2048]{1,0:T(8,128)(2,1)S(1)}, bf16[256,2048]{1,0:T(8,128)(2,1)}, u32[]{:S(2)}) copy-start(bf16[256,2048]{1,0:T(8,128)(2,1)} %get-tuple-element.79) | copy-start | bytes 3145732
  706.1 3.5 copy-start.11
  708.7 2.0 copy-start.17
  709.7 1.8 copy-start.16
  709.7 2.6 copy-start.15
  710.6 2.4 copy-start.14
  710.6 3.2 copy-start.8
  713.0 1.9 copy-start.7
Sparse Core Ops, SparseCore 0:
  117.2 49.5 all-gather.3
  168.4 53.5 all-gather.5
  223.6 96.4 all-gather.7
  373.9 52.3 reduce-scatter.3
  428.4 94.2 reduce-scatter.5
  597.6 65.0 reduce-scatter.7

commit v4 on v3

--- a/solution.py
+++ b/solution.py
@@ -5,6 +5,7 @@
 from jax.experimental.pallas import tpu as pltpu
 
 MASKED = -1e30
+EPSILON = 1e-06
 NT = (((1,), (1,)), ((), ()))
 NN = (((1,), (0,)), ((), ()))
 
@@ -26,13 +27,27 @@
 
 
 def attn_fwd_kernel(
-    heads, head_dim, block, length, lens_ref, q_ref, k_ref, v_ref, bias_ref, out_ref, lse_ref,
-    skew_ref, kt_ref,
+    heads, head_dim, block, length, seqs, fs, lens_ref, q_ref, k_ref, v_ref, bias_ref, x_ref,
+    out_ref, lse_ref, full_ref, skew_ref, kt_ref, *sems
 ):
     seq, blk = pl.program_id(0), pl.program_id(1)
+    blocks = length // block
+    grid_step = seq * blocks + blk
+    steps = seqs * blocks
     width = heads * head_dim
-
-    @pl.when((seq == 0) & (blk == 0))
+    plane = Plane(fs)
+    actions = gather_actions(plane, x_ref, full_ref, sems[:4], sems[4])
+
+    @pl.when(grid_step == 0)
+    def _():
+        plane.barrier()
+        actions[0]()
+
+    @pl.when(grid_step == steps // 2)
+    def _():
+        actions[1]()
+
+    @pl.when(grid_step == 0)
     def _():
         fill_skew(bias_ref, skew_ref, heads, block, length)
 
@@ -60,43 +75,57 @@
     out_ref[...] = out.astype(jnp.bfloat16)
     lse_ref[...] = lse_all
 
-
-def attn_fwd(qkv, offset_bias, lens, heads, head_dim, seqs, block=256):
+    @pl.when(grid_step == steps - 1)
+    def _():
+        for action in actions[2:]:
+            action()
+
+
+def attn_fwd(qkv, offset_bias, lens, heads, head_dim, seqs, gathered, collective_id, block=256):
     rows, width3 = qkv.shape
     width = width3 // 3
     length = rows // seqs
     block = min(block, length)
     blocks = length // block
-    return pl.pallas_call(
-        functools.partial(attn_fwd_kernel, heads, head_dim, block, length),
-        grid_spec=pltpu.PrefetchScalarGridSpec(
-            num_scalar_prefetch=1,
-            grid=(seqs, blocks),
-            in_specs=[
-                pl.BlockSpec((block, width), lambda s, i, lens: (s * blocks + i, 0)),
-                pl.BlockSpec((length, width), lambda s, i, lens: (s, 1)),
-                pl.BlockSpec((length, width), lambda s, i, lens: (s, 2)),
-                pl.BlockSpec((heads, 2 * length), lambda s, i, lens: (0, 0)),
-            ],
-            out_specs=[
-                pl.BlockSpec((block, width), lambda s, i, lens: (s * blocks + i, 0)),
-                pl.BlockSpec((block, 128), lambda s, i, lens: (s * blocks + i, 0)),
-            ],
-            scratch_shapes=[
-                pltpu.VMEM((heads, block, 2 * length - block), jnp.float32),
-                pltpu.VMEM((width, length), jnp.bfloat16),
-            ],
-        ),
+    fs = lax.axis_size("fsdp")
+    wide = gathered.shape[1]
+    gathered = gathered.reshape(seqs, -1, wide)
+    b = gathered.shape[1]
+    attended, lse, full = pl.pallas_call(
+        functools.partial(attn_fwd_kernel, heads, head_dim, block, length, seqs, fs),
+        grid=(seqs, blocks),
+        in_specs=[
+            pl.BlockSpec(memory_space=pltpu.SMEM),
+            pl.BlockSpec((block, width), lambda s, i: (s * blocks + i, 0)),
+            pl.BlockSpec((length, width), lambda s, i: (s, 1)),
+            pl.BlockSpec((length, width), lambda s, i: (s, 2)),
+            pl.BlockSpec((heads, 2 * length), lambda s, i: (0, 0)),
+            vmem(),
+        ],
+        out_specs=[
+            pl.BlockSpec((block, width), lambda s, i: (s * blocks + i, 0)),
+            pl.BlockSpec((block, 128), lambda s, i: (s * blocks + i, 0)),
+            anywhere(),
+        ],
+        scratch_shapes=[
+            pltpu.VMEM((heads, block, 2 * length - block), jnp.float32),
+            pltpu.VMEM((width, length), jnp.bfloat16),
+        ]
+        + gather_sems(fs)
+        + [pltpu.SemaphoreType.DMA],
         out_shape=[
             jax.ShapeDtypeStruct((rows, width), jnp.bfloat16),
             jax.ShapeDtypeStruct((rows, 128), jnp.float32),
+            jax.ShapeDtypeStruct((seqs, 2 * fs, b, wide), gathered.dtype),
         ],
         compiler_params=pltpu.CompilerParams(
-            dimension_semantics=("arbitrary", "arbitrary"), vmem_limit_bytes=56 * 1024 * 1024
+            dimension_semantics=("arbitrary", "arbitrary"), vmem_limit_bytes=56 * 1024 * 1024,
+            collective_id=collective_id, has_side_effects=True,
         ),
         cost_estimate=estimate(26),
         name="attn_fwd",
-    )(lens, qkv, qkv, qkv, offset_bias)
+    )(lens, qkv, qkv, qkv, offset_bias, gathered)
+    return attended, lse, full.reshape(-1, wide)
 
 
 def attn_bwd_kernel(
@@ -280,6 +309,10 @@
     pltpu.make_async_copy(ref, ref, sem).wait()
 
 
+def wide_tile(width):
+    return math.gcd(width // 2, 1024)
+
+
 def estimate(us):
     return pl.CostEstimate(flops=int(us * 0.02 * 1.1e9), bytes_accessed=int(us * 1e5), transcendentals=0)
 
@@ -311,11 +344,11 @@
         c = 1 - self.c if other else self.c
         return flip(self.f, rel) * 2 + c
 
-    def barrier(self):
+    def barrier(self, more=0):
         bar = pltpu.get_barrier_semaphore()
         for dev in [self.mate()] + [self.peer(b) for b in self.bits]:
             pl.semaphore_signal(bar, inc=1, device_id=dev, device_id_type=MESH_ID)
-        pl.semaphore_wait(bar, 1 + self.steps)
+        pl.semaphore_wait(bar, 1 + self.steps + more)
 
 
 def gather_sems(fs):
@@ -389,6 +422,140 @@
         copy.wait_send()
 
 
+def gather_actions(plane, x_ref, out_ref, sems, own_sem):
+    send, recv, mate_send, mate_recv = sems
+
+    def source(p, rel):
+        return x_ref.at[p] if rel == 0 else out_ref.at[p, plane.slot(rel)]
+
+    def to_mate(p, rel):
+        return remote_copy(
+            source(p, rel), out_ref.at[p, plane.slot(rel)], mate_send.at[p, rel],
+            mate_recv.at[p, rel], plane.mate(),
+        )
+
+    def to_peer(p, step, rel):
+        bit = plane.orders[p][step]
+        return remote_copy(
+            source(p, rel), out_ref.at[p, plane.slot(rel)], send.at[p, step, rel],
+            recv.at[p, rel ^ bit], plane.peer(bit),
+        )
+
+    def own():
+        return pltpu.make_async_copy(x_ref, out_ref.at[:, plane.slot(0)], own_sem)
+
+    held = [[[0]], [[0]]]
+    for step in range(plane.steps):
+        for p in range(2):
+            bit = plane.orders[p][step]
+            held[p].append(held[p][-1] + [rel ^ bit for rel in held[p][-1]])
+
+    def begin():
+        for p in range(2):
+            to_peer(p, 0, 0).start()
+        for p in range(2):
+            to_mate(p, 0).start()
+        own().start()
+
+    def group(step, i):
+        if i == 0 and step + 1 < plane.steps:
+            for p in range(2):
+                to_peer(p, step, 0).wait_send()
+                to_peer(p, step + 1, 0).start()
+        for p in range(2):
+            rel = held[p][step][i] ^ plane.orders[p][step]
+            landed(out_ref.at[p, plane.slot(rel)], recv.at[p, rel])
+            to_mate(p, rel).start()
+            for later in range(step + 1, plane.steps):
+                to_peer(p, later, rel).start()
+
+    def close():
+        for p in range(2):
+            for rel in range(plane.fs):
+                landed(out_ref.at[p, plane.slot(rel, True)], mate_recv.at[p, rel])
+                to_mate(p, rel).wait_send()
+            for step in range(plane.steps):
+                for rel in held[p][step]:
+                    if rel or step + 1 == plane.steps:
+                        to_peer(p, step, rel).wait_send()
+        own().wait()
+
+    groups = [
+        functools.partial(group, step, i)
+        for step in range(plane.steps) for i in range(2**step)
+    ]
+    return [begin] + groups + [close]
+
+
+class Line:
+    def __init__(self, x_ref, out_ref, scratch):
+        self.x_ref, self.out_ref = x_ref, out_ref
+        self.send, self.recv, self.own_sem = scratch
+        self.f, self.z, self.c = (lax.axis_index(a) for a in ("fsdp", "z", "core"))
+        self.zs = out_ref.shape[0]
+
+    @staticmethod
+    def scratch(zs):
+        dma = pltpu.SemaphoreType.DMA
+        return [dma((2, zs)), dma((2, zs)), dma]
+
+    def greet(self):
+        bar = pltpu.get_barrier_semaphore()
+        for way in (1, -1):
+            to = lax.rem(self.z + way + self.zs, self.zs)
+            pl.semaphore_signal(
+                bar, inc=1, device_id=(self.f, to, self.c), device_id_type=MESH_ID
+            )
+
+    def copy(self, step, way):
+        source = lax.rem(self.z - way * step + self.zs, self.zs)
+        to = lax.rem(self.z + way + self.zs, self.zs)
+        k = 0 if way > 0 else 1
+        ref = self.out_ref.at[source]
+        return remote_copy(
+            ref if step else self.x_ref, ref, self.send.at[k, step], self.recv.at[k, step],
+            (self.f, to, self.c),
+        )
+
+    def sends(self, step, way):
+        if way > 0:
+            return (self.z >= step) & (self.z < self.zs - 1)
+        return (self.z < self.zs - step) & (self.z > 0)
+
+    def arrived(self, step, way):
+        k = 0 if way > 0 else 1
+        source = lax.rem(self.z - way * (step + 1) + self.zs, self.zs)
+        here = (self.z > step) if way > 0 else (self.z < self.zs - 1 - step)
+
+        @pl.when(here)
+        def _():
+            landed(self.out_ref.at[source], self.recv.at[k, step])
+
+    def own(self):
+        return pltpu.make_async_copy(self.x_ref, self.out_ref.at[self.z], self.own_sem)
+
+    def go(self, step):
+        if step == 0:
+            self.own().start()
+        for way in (1, -1):
+            if step:
+                self.arrived(step - 1, way)
+            if step < self.zs - 1:
+
+                @pl.when(self.sends(step, way))
+                def _(way=way):
+                    self.copy(step, way).start()
+
+    def close(self):
+        self.own().wait()
+        for step in range(self.zs - 1):
+            for way in (1, -1):
+
+                @pl.when(self.sends(step, way))
+                def _(step=step, way=way):
+                    self.copy(step, way).wait_send()
+
+
 def scatter_scratch(fs, b, width):
     return [
         pltpu.VMEM((2, fs, b, width), jnp.bfloat16),
@@ -396,25 +563,23 @@
         pltpu.VMEM((2, fs // 2, b, width), jnp.float32),
         pltpu.VMEM((2, fs, b, width), jnp.bfloat16),
         pltpu.VMEM((2, fs - 1, b, width), jnp.bfloat16),
-        pltpu.SemaphoreType.DMA((fs,)),
-        pltpu.SemaphoreType.DMA((fs,)),
+        pltpu.SemaphoreType.DMA((fs, 2)),
+        pltpu.SemaphoreType.DMA((fs, 2)),
         pltpu.SemaphoreType.DMA((2, fs)),
         pltpu.SemaphoreType.DMA((2, fs - 1)),
     ]
 
 
-def scatter_actions(plane, partial, tile, width, out_ref, scratch):
+def scatter_actions(plane, partial, width, out_ref, scratch):
     give, got, total, outbox, inbox, give_sem, got_sem, send, recv = scratch
     b = out_ref.shape[1]
     rels = sorted(range(plane.fs), key=lambda r: (-bin(r).count("1"), r))
-    tiles = width // tile
-
-    def each_tile(body):
-        def one(j, carry):
-            body(pl.ds(pl.multiple_of(j * tile, tile), tile))
-            return carry
-
-        lax.fori_loop(0, tiles, one, 0)
+    whole = slice(0, width)
+
+    def pieces(rel):
+        if rel == rels[0]:
+            return [slice(0, width // 2), slice(width // 2, width)]
+        return [whole]
 
     def leaves(p, rel):
         for step, bit in enumerate(plane.orders[p]):
@@ -437,9 +602,11 @@
             outbox.at[p, rel], inbox.at[p, at], send.at[p, rel], recv.at[p, at], plane.peer(bit)
         )
 
-    def to_mate(rel):
+    def to_mate(rel, i):
+        cols = pieces(rel)[i]
         return remote_copy(
-            give.at[:, rel], got.at[:, rel], give_sem.at[rel], got_sem.at[rel], plane.mate()
+            give.at[:, rel, :, cols], got.at[:, rel, :, cols], give_sem.at[rel, i],
+            got_sem.at[rel, i], plane.mate(),
         )
 
     def give_part(rel):
@@ -450,12 +617,12 @@
             give[0, rel, :, cols] = part[:b]
             give[1, rel, :, cols] = part[b:]
 
-        each_tile(body)
-        to_mate(rel).start()
+        for i, cols in enumerate(pieces(rel)):
+            body(cols)
+            to_mate(rel, i).start()
 
     def own_part(rel):
         mine = plane.slot(rel)
-        landed(got.at[:, rel], got_sem.at[rel])
 
         def body(cols):
             part = partial(mine, cols)
@@ -466,7 +633,9 @@
                 else:
                     total[p, held(p, rel), :, cols] = here
 
-        each_tile(body)
+        for i, cols in enumerate(pieces(rel)):
+            landed(got.at[:, rel, :, cols], got_sem.at[rel, i])
+            body(cols)
         for p in range(2):
             if leaves(p, rel) == 0:
                 to_peer(p, rel).start()
@@ -485,22 +654,23 @@
             else:
                 total[p, held(p, rel), :, cols] = here
 
-        each_tile(body)
+        body(whole)
         if sends and step + 1 < plane.steps:
             to_peer(p, rel).start()
 
     def close():
         for rel in rels:
-            to_mate(rel).wait_send()
+            for i in range(len(pieces(rel))):
+                to_mate(rel, i).wait_send()
             for p in range(2):
                 if leaves(p, rel) < plane.steps:
                     to_peer(p, rel).wait_send()
 
-    actions = [functools.partial(give_part, rels[0])]
-    for i, rel in enumerate(rels):
-        if i + 1 < len(rels):
-            actions.append(functools.partial(give_part, rels[i + 1]))
-        actions.append(functools.partial(own_part, rel))
+    order = [(give_part, rels[0]), (own_part, rels[0]), (give_part, rels[1])]
+    for i in range(2, len(rels)):
+        order += [(give_part, rels[i]), (own_part, rels[i - 1])]
+    order.append((own_part, rels[-1]))
+    actions = [functools.partial(part, rel) for part, rel in order]
     for step in range(plane.steps):
         for rel in rels:
             for p in range(2):
@@ -523,16 +693,44 @@
     )
 
 
-def gather_dot_kernel(fs, dims, tile, other, x_ref, w_ref, *refs):
+class Staged:
+    def __init__(self, refs, scratch):
+        self.held = scratch[: len(refs)]
+        self.loads = [
+            pltpu.make_async_copy(ref, held, sem)
+            for ref, held, sem in zip(refs, self.held, scratch[len(refs) :])
+        ]
+        for load in self.loads:
+            load.start()
+
+    @staticmethod
+    def scratch(*arrays):
+        dma = pltpu.SemaphoreType.DMA
+        return [pltpu.VMEM(x.shape, x.dtype) for x in arrays] + [dma] * len(arrays)
+
+    def wait(self):
+        for load in self.loads:
+            load.wait()
+
+
+def gather_dot_kernel(fs, dims, tile, other, line, x_ref, *refs):
+    count = 2 if other else 1
+    hbm, refs = refs[:count], refs[count:]
+    if line:
+        l_ref, refs = refs[0], refs[1:]
+    full_ref, y_ref, refs = refs[0], refs[1], refs[2:]
+    if line:
+        line, refs = Line(l_ref, refs[0], refs[1:4]), refs[4:]
+    staged = Staged(hbm, refs[: 2 * count])
+    buf_ref, sems = refs[2 * count], refs[2 * count + 1 :]
     plane = Plane(fs)
-    plane.barrier()
-    if other:
-        o_ref, full_ref, y_ref, wg_ref, buf_ref, acc_ref = refs[:6]
-        sems = refs[6:]
-        acc_ref[...] = jnp.zeros_like(acc_ref)
-    else:
-        full_ref, y_ref, buf_ref = refs[:3]
-        sems = refs[3:]
+    if line:
+        line.greet()
+    plane.barrier(2 if line else 0)
+    if line:
+        line.go(0)
+    w_ref = staged.held[0]
+    a_ref = staged.held[1] if other else buf_ref
     keep_sem = sems[4]
     b, width = buf_ref.shape[2:]
     columns = y_ref.shape[3]
@@ -544,11 +742,13 @@
             buf_ref.at[p, two], full_ref.at[p, two], keep_sem.at[len(kept)]
         )
         cp.start()
+        if not kept:
+            staged.wait()
         kept.append(cp)
 
         def product(cols):
             w = w_ref[:, cols] if dims == NN else w_ref[cols, :]
-            y = dotf(buf_ref[p, two].reshape(2 * b, width), w, dims)
+            y = dotf(a_ref[p, two].reshape(2 * b, -1), w, dims)
             y_ref[p, two, :, cols] = y.astype(y_ref.dtype).reshape(2, b, tile)
 
         def one(j, carry):
@@ -559,45 +759,50 @@
             product(slice(None))
         else:
             lax.fori_loop(0, columns // tile, one, 0)
-        if other:
-            o_t = o_ref[p, two].reshape(2 * b, -1).T
-
-            def grad(j, carry):
-                cols = pl.ds(pl.multiple_of(j * 256, 256), 256)
-                acc_ref[:, cols] += dotf(o_t, buf_ref[p, two, :, cols].reshape(2 * b, 256))
-                return carry
-
-            lax.fori_loop(0, width // 256, grad, 0)
+        if line and len(kept) % 2 == 0 and len(kept) // 2 < line.zs:
+            line.go(len(kept) // 2)
 
     run_gather(plane, x_ref, buf_ref, sems[:4], consume)
-    if other:
-        wg_ref[...] = acc_ref[...].astype(wg_ref.dtype)
+    if line:
+        for step in range(len(kept) // 2 + 1, line.zs):
+            line.go(step)
+        line.close()
     for cp in kept:
         cp.wait()
 
 
-def plane_gather_dot(x, w, dims, seqs, collective_id, other=None, dtype=jnp.bfloat16):
-    fs = lax.axis_size("fsdp")
+def plane_gather_dot(
+    x, w, dims, seqs, collective_id, other=None, line=None, dtype=jnp.bfloat16
+):
+    fs, zs = lax.axis_size("fsdp"), lax.axis_size("z")
     x = x.reshape(seqs, -1, x.shape[1])
     _, b, width = x.shape
     columns = w.shape[1] if dims == NN else w.shape[0]
-    tile = next((t for t in (256, 128) if columns % t == 0), columns)
+    tile = next((t for t in (1024, 768, 256, 128) if columns % t == 0), columns)
     lead = (seqs, 2 * fs, b)
+    staged = [w] if other is None else [w, other.reshape(lead + (-1,))]
     out_shape = [
         jax.ShapeDtypeStruct(lead + (width,), x.dtype),
         jax.ShapeDtypeStruct(lead + (columns,), dtype),
     ]
-    args, scratch = [x, w], [pltpu.VMEM(lead + (width,), x.dtype)]
-    if other is not None:
-        args.append(other.reshape(lead + (-1,)))
-        out_shape.append(jax.ShapeDtypeStruct((other.shape[1], width), jnp.bfloat16))
-        scratch.append(pltpu.VMEM((other.shape[1], width), jnp.float32))
+    args, scratch = [x] + staged, []
+    in_specs, out_specs = [vmem()] + [anywhere()] * len(staged), [anywhere(), vmem()]
+    if line is not None:
+        args.append(line)
+        in_specs.append(vmem())
+        out_shape.append(jax.ShapeDtypeStruct((zs,) + line.shape, line.dtype))
+        out_specs.append(anywhere())
+        scratch += Line.scratch(zs)
     out = pl.pallas_call(
-        functools.partial(gather_dot_kernel, fs, dims, tile, other is not None),
+        functools.partial(gather_dot_kernel, fs, dims, tile, other is not None, line is not None),
         out_shape=out_shape,
-        in_specs=[vmem()] * len(args),
-        out_specs=[anywhere()] + [vmem()] * (len(out_shape) - 1),
-        scratch_shapes=scratch + gather_sems(fs) + [pltpu.SemaphoreType.DMA((seqs * fs,))],
+        in_specs=in_specs,
+        out_specs=out_specs,
+        scratch_shapes=scratch
+        + Staged.scratch(*staged)
+        + [pltpu.VMEM(lead + (width,), x.dtype)]
+        + gather_sems(fs)
+        + [pltpu.SemaphoreType.DMA((seqs * fs,))],
         compiler_params=plane_params(collective_id),
         cost_estimate=estimate(45),
         name="plane_gather_dot",
@@ -838,31 +1043,33 @@
             self.copy(d, x_ref, spread_out, slots, send, recv).wait_send()
 
 
-def dot_scatter_kernel(fs, dims, tile, beside, a_ref, w_ref, *refs):
-    plane = Plane(fs)
-    plane.barrier()
-    if beside:
-        l_hbm, r_hbm, out_ref, g_ref, l_ref, r_ref, l_sem, r_sem = refs[:8]
-        scratch = refs[8:]
-        loads = [
-            pltpu.make_async_copy(l_hbm, l_ref, l_sem), pltpu.make_async_copy(r_hbm, r_ref, r_sem)
-        ]
-        for load in loads:
-            load.start()
-    else:
-        out_ref, scratch = refs[0], refs[1:]
-
+def slot_product(a_ref, w_ref, dims):
     def partial(slot, cols):
         a = a_ref[:, slot].reshape(-1, a_ref.shape[3])
         return dotf(a, w_ref[:, cols] if dims == NN else w_ref[cols, :], dims)
 
-    actions = scatter_actions(plane, partial, tile, out_ref.shape[2], out_ref, scratch)
+    return partial
+
+
+def dot_scatter_kernel(fs, dims, beside, *refs):
+    if beside:
+        staged = Staged(refs[:2], refs[6:10])
+        later = Staged(refs[2:4], refs[10:14])
+        out_ref, g_ref, scratch = refs[4], refs[5], refs[14:]
+        l_ref, r_ref = later.held
+    else:
+        staged = Staged(refs[:2], refs[3:7])
+        out_ref, scratch = refs[2], refs[7:]
+    plane = Plane(fs)
+    plane.barrier()
+    staged.wait()
+    partial = slot_product(*staged.held, dims)
+    actions = scatter_actions(plane, partial, out_ref.shape[2], out_ref, scratch)
     first = 2 * fs
     for action in actions[:first]:
         action()
     if beside:
-        for load in loads:
-            load.wait()
+        later.wait()
         block = 256
 
         def one(i, carry):
@@ -888,19 +1095,18 @@
     width = w.shape[1] if dims == NN else w.shape[0]
     out_shape = [jax.ShapeDtypeStruct((seqs, b, width), jnp.float32)]
     args = [a, w]
-    scratch = scatter_scratch(fs, b, width)
+    scratch = Staged.scratch(a, w)
     if beside is not None:
         l, r = beside
         args += [l, r]
-        dma = pltpu.SemaphoreType.DMA
-        scratch = [pltpu.VMEM(l.shape, l.dtype), pltpu.VMEM(r.shape, r.dtype), dma, dma] + scratch
         out_shape.append(jax.ShapeDtypeStruct((l.shape[1], r.shape[1]), jnp.bfloat16))
+        scratch += Staged.scratch(l, r)
     out = pl.pallas_call(
-        functools.partial(dot_scatter_kernel, fs, dims, 256, beside is not None),
+        functools.partial(dot_scatter_kernel, fs, dims, beside is not None),
         out_shape=out_shape,
-        in_specs=[vmem()] * 2 + [anywhere()] * (len(args) - 2),
+        in_specs=[anywhere()] * len(args),
         out_specs=[vmem()] * len(out_shape),
-        scratch_shapes=scratch,
+        scratch_shapes=scratch + scatter_scratch(fs, b, width),
         compiler_params=plane_params(collective_id, 62),
         cost_estimate=estimate(45),
         name="plane_dot_scatter",
@@ -909,99 +1115,151 @@
     return rows if beside is None else (rows, out[1])
 
 
-GELU_C = math.sqrt(2.0 / math.pi)
-
-
-def gather_ffn_kernel(
-    fs, x_ref, gh_hbm, g_hbm, wgu_ref, full_ref, h_ref, ggu_ref, wg_ref,
-    buf_ref, gh_ref, g_ref, acc_ref, *sems
+def norm_turn_kernel(
+    fs, a_hbm, w_hbm, hid_ref, cot_ref, gain_ref, wo_ref, o_ref, y_ref, wg_ref, grad_ref, gsum_ref,
+    a_ref, w_ref, a_sem, w_sem, sum_ref, x_ref, buf_ref, acc_ref, *scratch
 ):
+    staged = Staged((a_hbm, w_hbm), (a_ref, w_ref, a_sem, w_sem))
     plane = Plane(fs)
-    gh_sem, g_sem = sems[5:]
-    loads = [
-        pltpu.make_async_copy(gh_hbm, gh_ref, gh_sem), pltpu.make_async_copy(g_hbm, g_ref, g_sem)
-    ]
-    for load in loads:
-        load.start()
     plane.barrier()
-    keep_sem = sems[4]
-    ff = h_ref.shape[3]
-    b, width = buf_ref.shape[2:]
-    kept = []
+    acc_ref[...] = jnp.zeros_like(acc_ref)
+    staged.wait()
+    b, width = x_ref.shape[1:]
+    partial = slot_product(a_ref, w_ref, NT)
+    for action in scatter_actions(plane, partial, width, sum_ref, scratch[4:]):
+        action()
+    block = 32
+    tile = wide_tile(width)
+    gain = gain_ref[...]
+
+    def turn(i, total):
+        p, at = lax.div(i, b // block), pl.multiple_of(lax.rem(i, b // block) * block, block)
+        here = pl.ds(at, block)
+        grad, hidden = sum_ref[p, here, :], hid_ref[p, here, :]
+        scale = lax.rsqrt(jnp.mean(hidden * hidden, axis=1, keepdims=True) + EPSILON)
+        weighted = grad * gain
+        inner = jnp.mean(weighted * hidden, axis=1, keepdims=True)
+        back = scale * (weighted - hidden * scale * scale * inner)
+        back = cot_ref[p, here, :].astype(jnp.float32) + back
+        grad_ref[p, here, :] = back
+        x_ref[p, here, :] = back.astype(jnp.bfloat16)
+        return total + grad * hidden * scale
+
+    total = lax.fori_loop(
+        0, 2 * (b // block), turn, jnp.zeros((block, width), jnp.float32)
+    )
+    gsum_ref[...] = jnp.sum(total, axis=0, keepdims=True)
 
     def consume(p, slot):
         two = pl.ds(slot, 2)
-        cp = pltpu.make_async_copy(
-            buf_ref.at[p, two], full_ref.at[p, two], keep_sem.at[len(kept)]
-        )
-        cp.start()
-        if not kept:
-            for load in loads:
-                load.wait()
-            acc_ref[...] = jnp.zeros_like(acc_ref)
-        kept.append(cp)
         rows = buf_ref[p, two].reshape(2 * b, width)
-        gate = dotf(rows, wgu_ref[:, :ff])
-        up = dotf(rows, wgu_ref[:, ff:])
-        grad_hidden = gh_ref[p, two].reshape(2 * b, ff)
-        square = gate * gate
-        tanh = jnp.tanh(GELU_C * gate * (1.0 + 0.044715 * square))
-        half = 0.5 * (1.0 + tanh)
-        act = gate * half
-        slope = half + (0.5 * GELU_C) * gate * (1.0 - tanh * tanh) * (1.0 + 0.134145 * square)
-        hidden = (act * up).astype(jnp.bfloat16)
-
-        def put(ref, cols, value):
-            ref[p, two, :, cols] = value.astype(jnp.bfloat16).reshape(2, b, ff)
-
-        put(h_ref, slice(0, ff), hidden)
-        put(ggu_ref, slice(0, ff), grad_hidden * up * slope)
-        put(ggu_ref, slice(ff, 2 * ff), grad_hidden * act)
-        hidden_t = hidden.T
+        y = dotf(rows, wo_ref[...], NT)
+        y_ref[p, two] = y.astype(y_ref.dtype).reshape(2, b, -1)
+        o_t = o_ref[p, two].reshape(2 * b, -1).T
 
         def grad(j, carry):
-            cols = pl.ds(pl.multiple_of(j * 256, 256), 256)
-            acc_ref[:, cols] += dotf(hidden_t, g_ref[p, two, :, cols].reshape(2 * b, 256))
+            cols = pl.ds(pl.multiple_of(j * tile, tile), tile)
+            acc_ref[:, cols] += dotf(o_t, buf_ref[p, two, :, cols].reshape(2 * b, tile))
             return carry
 
-        lax.fori_loop(0, width // 256, grad, 0)
-
-    run_gather(plane, x_ref, buf_ref, sems[:4], consume)
-    wg_ref[...] = acc_ref[...].astype(jnp.bfloat16)
-    for cp in kept:
-        cp.wait()
-
-
-def plane_gather_ffn(x, grad_hidden, grad, w_gu, seqs, collective_id):
+        lax.fori_loop(0, width // tile, grad, 0)
+
+    run_gather(plane, x_ref, buf_ref, scratch[:4], consume)
+    wg_ref[...] = acc_ref[...].astype(wg_ref.dtype)
+
+
+def norm_turn(a, w, hidden, cot, gain, w_o, attended, seqs, collective_id):
     fs = lax.axis_size("fsdp")
-    x = x.reshape(seqs, -1, x.shape[1])
-    _, b, width = x.shape
+    lead = (seqs, 2 * fs, a.shape[0] // (2 * fs * seqs))
+    b, width = lead[2], hidden.shape[1]
+    own = (seqs, b, width)
+    a = a.reshape(lead + (-1,))
+    attended = attended.reshape(lead + (-1,))
+    k = attended.shape[3]
+    y, wg, grad, gsum = pl.pallas_call(
+        functools.partial(norm_turn_kernel, fs),
+        out_shape=[
+            jax.ShapeDtypeStruct(lead + (k,), jnp.bfloat16),
+            jax.ShapeDtypeStruct((k, width), jnp.bfloat16),
+            jax.ShapeDtypeStruct(own, jnp.float32),
+            jax.ShapeDtypeStruct((1, width), jnp.float32),
+        ],
+        in_specs=[anywhere()] * 2 + [vmem()] * 5,
+        out_specs=[vmem()] * 4,
+        scratch_shapes=Staged.scratch(a, w)
+        + [
+            pltpu.VMEM(own, jnp.float32),
+            pltpu.VMEM(own, jnp.bfloat16),
+            pltpu.VMEM(lead + (width,), jnp.bfloat16),
+            pltpu.VMEM((k, width), jnp.float32),
+        ]
+        + gather_sems(fs)
+        + scatter_scratch(fs, b, width),
+        compiler_params=plane_params(collective_id, 62),
+        cost_estimate=estimate(45),
+        name="norm_turn",
+    )(a, w, hidden.reshape(own), cot.reshape(own), gain, w_o, attended)
+    return y.reshape(-1, k), wg, grad.reshape(-1, width), gsum[0]
+
+
+GELU_C = math.sqrt(2.0 / math.pi)
+
+
+def ffn_kernel(x_ref, gh_ref, g_ref, wgu_ref, h_ref, ggu_ref, wg_ref, acc_ref):
+    step = pl.program_id(0)
+    ff = h_ref.shape[1]
+
+    @pl.when(step == 0)
+    def _():
+        acc_ref[...] = jnp.zeros_like(acc_ref)
+
+    gate = dotf(x_ref[...], wgu_ref[:, :ff])
+    up = dotf(x_ref[...], wgu_ref[:, ff:])
+    grad_hidden = gh_ref[...]
+    square = gate * gate
+    tanh = jnp.tanh(GELU_C * gate * (1.0 + 0.044715 * square))
+    half = 0.5 * (1.0 + tanh)
+    act = gate * half
+    slope = half + (0.5 * GELU_C) * gate * (1.0 - tanh * tanh) * (1.0 + 0.134145 * square)
+    hidden = (act * up).astype(jnp.bfloat16)
+    h_ref[...] = hidden
+    ggu_ref[:, :ff] = (grad_hidden * up * slope).astype(jnp.bfloat16)
+    ggu_ref[:, ff:] = (grad_hidden * act).astype(jnp.bfloat16)
+    acc_ref[...] += dotf(hidden.T, g_ref[...])
+
+    @pl.when(step == pl.num_programs(0) - 1)
+    def _():
+        wg_ref[...] = acc_ref[...].astype(jnp.bfloat16)
+
+
+def ffn(x, grad_hidden, grad, w_gu):
+    rows, width = x.shape
     ff = grad_hidden.shape[1]
-    lead = (seqs, 2 * fs, b)
-    dma = pltpu.SemaphoreType.DMA
-    full, h, ggu, wg = pl.pallas_call(
-        functools.partial(gather_ffn_kernel, fs),
+    block = math.gcd(rows, 512)
+
+    def blocks(columns):
+        return pl.BlockSpec((block, columns), lambda i: (i, 0))
+
+    def held(shape):
+        return pl.BlockSpec(shape, lambda i: (0, 0), pipeline_mode=pl.Buffered(1))
+
+    return pl.pallas_call(
+        ffn_kernel,
+        grid=(rows // block,),
         out_shape=[
-            jax.ShapeDtypeStruct(lead + (width,), x.dtype),
-            jax.ShapeDtypeStruct(lead + (ff,), jnp.bfloat16),
-            jax.ShapeDtypeStruct(lead + (2 * ff,), jnp.bfloat16),
+            jax.ShapeDtypeStruct((rows, ff), jnp.bfloat16),
+            jax.ShapeDtypeStruct((rows, 2 * ff), jnp.bfloat16),
             jax.ShapeDtypeStruct((ff, width), jnp.bfloat16),
         ],
-        in_specs=[vmem(), anywhere(), anywhere(), vmem()],
-        out_specs=[anywhere(), vmem(), vmem(), vmem()],
-        scratch_shapes=[
-            pltpu.VMEM(lead + (width,), x.dtype),
-            pltpu.VMEM(lead + (ff,), jnp.float32),
-            pltpu.VMEM(lead + (width,), x.dtype),
-            pltpu.VMEM((ff, width), jnp.float32),
-        ]
-        + gather_sems(fs)
-        + [dma((seqs * fs,)), dma, dma],
-        compiler_params=plane_params(collective_id, 62),
-        cost_estimate=estimate(45),
-        name="plane_gather_ffn",
-    )(x, grad_hidden.reshape(lead + (ff,)), grad.reshape(lead + (width,)), w_gu)
-    return full.reshape(-1, width), h.reshape(-1, ff), ggu.reshape(-1, 2 * ff), wg
+        in_specs=[blocks(width), blocks(ff), blocks(width), held(w_gu.shape)],
+        out_specs=[blocks(ff), blocks(2 * ff), pl.BlockSpec((ff, width), lambda i: (0, 0))],
+        scratch_shapes=[pltpu.VMEM((ff, width), jnp.float32)],
+        compiler_params=pltpu.CompilerParams(
+            dimension_semantics=("arbitrary",), vmem_limit_bytes=60 * MIB
+        ),
+        cost_estimate=estimate(30),
+        name="ffn",
+    )(x, grad_hidden, grad, w_gu)
 
 def column_runs(sizes, per_device, total, natural):
     fs, zs, cs = sizes
@@ -1066,16 +1324,17 @@
     own_gu.start()
     o_out[...] = o_ref[...].astype(jnp.bfloat16)
     d_out[...] = d_ref[...].astype(jnp.bfloat16)
-    own_qkv.wait()
-    for d in range(1, devices):
-        landed(block(wqkv_ref, lax.rem(me + devices - d, devices), z), q_recv.at[d])
-
-    def line(step, way):
+    def chip(p):
+        return lax.rem(f + p, fs)
+
+    def line(step, way, p):
         source = lax.rem(z - way * step + zs, zs)
         to = lax.rem(z + way + zs, zs)
         k = 0 if way > 0 else 1
-        ref = wqkv_ref.at[:, source]
-        return remote_copy(ref, ref, line_send.at[k, step], line_recv.at[k, step], (f, to, c))
+        ref = wqkv_ref.at[chip(p), source]
+        return remote_copy(
+            ref, ref, line_send.at[k, step, p], line_recv.at[k, step, p], (f, to, c)
+        )
 
     def sends(step, way):
         if way > 0:
@@ -1085,32 +1344,48 @@
     def arrives(step, way):
         return (z > step) if way > 0 else (z < zs - 1 - step)
 
-    def arrive(step, way):
+    def arrive(step, way, p):
         k = 0 if way > 0 else 1
         source = lax.rem(z - way * (step + 1) + zs, zs)
-        landed(wqkv_ref.at[:, source], line_recv.at[k, step])
+        landed(wqkv_ref.at[chip(p), source], line_recv.at[k, step, p])
+
+    def spread_arrive(df, dc):
+        index = chip(df) * cs + lax.rem(c + dc, cs)
+        d = lax.rem(me - index + devices, devices)
+        landed(block(wqkv_ref, index, z), q_recv.at[d])
 
     for step in range(zs - 1):
-        for way in (1, -1):
-
-            @pl.when(sends(step, way))
-            def _(step=step, way=way):
-                line(step, way).start()
+        for p in range(fs):
+            if step == 0:
+                if p == 0:
+                    own_qkv.wait()
+                for dc in range(cs):
+                    if p or dc:
+                        spread_arrive(p, dc)
+            for way in (1, -1):
+                if step:
+
+                    @pl.when(arrives(step - 1, way))
+                    def _(step=step, way=way, p=p):
+                        arrive(step - 1, way, p)
+
+                @pl.when(sends(step, way))
+                def _(step=step, way=way, p=p):
+                    line(step, way, p).start()
 
         if step == 0:
-            swaps[1].start_inward()
+            swaps[0].hand_on()
+            swaps[1].start()
             for d in range(1, devices):
                 spread_copy(d, gu_ref, ggu_ref, None, g_send, g_recv).start()
         if step == 1:
-            swaps[1].start_straight()
+            swaps[1].hand_on()
+    for p in range(fs):
         for way in (1, -1):
 
-            @pl.when(arrives(step, way))
-            def _(step=step, way=way):
-                arrive(step, way)
-
-        if step < 2:
-            swaps[step].hand_on()
+            @pl.when(arrives(zs - 2, way))
+            def _(way=way, p=p):
+                arrive(zs - 2, way, p)
 
     everyone.finish(small_ref, False, slots, s_send, s_recv)
     small_out[...] = slots[...]
@@ -1121,11 +1396,12 @@
         spread_copy(d, qkv_ref, wqkv_ref, z, q_send, q_recv).wait_send()
         spread_copy(d, gu_ref, ggu_ref, None, g_send, g_recv).wait_send()
     for step in range(zs - 1):
-        for way in (1, -1):
-
-            @pl.when(sends(step, way))
-            def _(step=step, way=way):
-                line(step, way).wait_send()
+        for p in range(fs):
+            for way in (1, -1):
+
+                @pl.when(sends(step, way))
+                def _(step=step, way=way, p=p):
+                    line(step, way, p).wait_send()
 
     for swap in swaps:
         swap.close()
@@ -1159,7 +1435,7 @@
             pltpu.VMEM((devices, rows, gu_cols), jnp.bfloat16),
             dma((n,)), dma((n,)), dma((3,)),
             dma((devices,)), dma((devices,)), dma((devices,)), dma((devices,)),
-            dma((2, zs)), dma((2, zs)),
+            dma((2, zs, fs)), dma((2, zs, fs)),
         ]
         + Swap.scratch(fs, *tokens.shape) * 2,
         compiler_params=plane_params(collective_id),
@@ -1236,7 +1512,6 @@
 from jax.sharding import PartitionSpec as P
 
 H = 32
-EPSILON = 1e-06
 HIGHEST = lax.Precision.HIGHEST
 BF = jnp.bfloat16
 F32 = jnp.float32
@@ -1365,17 +1640,20 @@
     scale_one = rms_scale(x)
     grad_rows = cot.reshape(rows, width).astype(F32) * valid
 
-    normed, qkv = plane_gather_dot((x * scale_one * gain_one).astype(BF), w_qkv, NN, seqs, 2)
-    attended, lse = attn_fwd(qkv, offset_bias, lens, heads, head_dim, seqs)
+    normed = (x * scale_one * gain_one).astype(BF)
+    normed, qkv = plane_gather_dot(normed, w_qkv, NN, seqs, 2)
+    branch = grad_rows.astype(BF)
+    attended, lse, grad_branch = attn_fwd(
+        qkv, offset_bias, lens, heads, head_dim, seqs, branch, 1
+    )
     attn_sum = plane_dot_scatter(attended, w_o, NN, seqs, 3)
-    branch = grad_rows.astype(BF)
-    branch, attn_sum = lax.optimization_barrier((branch, attn_sum))
-    grad_branch, grad_hidden = plane_gather_dot(branch, w_d, NT, seqs, 1, dtype=F32)
     hidden_one = x + attn_sum
     scale_two = rms_scale(hidden_one)
-    normed_two, hidden_ff, grad_gu, grad_w_down = plane_gather_ffn(
-        (hidden_one * scale_two * gain_two).astype(BF), grad_hidden, grad_branch, w_gu, seqs, 4
+    normed_two, grad_hidden = plane_gather_dot(
+        (hidden_one * scale_two * gain_two).astype(BF), w_d, NT, seqs, 4, other=grad_branch,
+        dtype=F32,
     )
+    hidden_ff, grad_gu, grad_w_down = ffn(normed_two, grad_hidden, grad_branch, w_gu)
     sum_down = ff_cols.scatter(grad_w_down)
     if fs <= 4:
         ff_sum, grad_w_gu = plane_dot_scatter(
@@ -1388,12 +1666,19 @@
     result = ((hidden_one + ff_sum) * valid).astype(BF)
     grad_w_gu, sum_down, grad_gu = lax.optimization_barrier((grad_w_gu, sum_down, grad_gu))
     sum_gu = reduce_z(grad_w_gu)
-    grad_normed_two = plane_dot_scatter(grad_gu, w_gu, NT, seqs, 5)
-    gain_two_part = jnp.sum(grad_normed_two * hidden_one * scale_two, axis=0)
-    grad_hidden_one = grad_rows + norm_back(grad_normed_two, hidden_one, scale_two, gain_two)
-    grad_attn, grad_attended, grad_w_o = plane_gather_dot(
-        grad_hidden_one.astype(BF), w_o, NT, seqs, 6, other=attended
-    )
+    if fs <= 4:
+        grad_attended, grad_w_o, grad_hidden_one, gain_two_part = norm_turn(
+            grad_gu, w_gu, hidden_one, branch, gain_two, w_o, attended, seqs, 5
+        )
+    else:
+        grad_normed_two = plane_dot_scatter(grad_gu, w_gu, NT, seqs, 5)
+        gain_two_part = jnp.sum(grad_normed_two * hidden_one * scale_two, axis=0)
+        grad_hidden_one = grad_rows + norm_back(grad_normed_two, hidden_one, scale_two, gain_two)
+        grad_attn, grad_attended = plane_gather_dot(
+            grad_hidden_one.astype(BF), w_o, NT, seqs, 6
+        )
+        grad_w_o = jnp.einsum("rk,rd->kd", attended, grad_attn, preferred_element_type=F32)
+        grad_w_o = grad_w_o.astype(BF)
     dq, dk, dv, grad_offset, output, sum_o, got_gu = attn_bwd(
         qkv, grad_attended, lse, offset_bias, lens, heads, head_dim, seqs,
         swapped=result, column=head_cols.whole(grad_w_o), spread=sum_gu, collective_id=11,

time: 728 us -> 699 us (0.960); the launches traced: 723 us -> 686 us
  Pallas kernels: 636 us -> 602 us
    pallas_call x3 -> x2, Pallas kernels: 155 us -> 103 us  [plane_gather_dot(): pl.pallas_call(functools.partial(gather_dot_kernel, fs, dims, tile, other...]
    pallas_call x1, Pallas kernels: 25.6 us -> 45.1 us  [attn_fwd(): pl.pallas_call(functools.partial(attn_fwd_kernel, heads, head_dim, block,...]
    pallas_call x1, Pallas kernels: 106 us -> 94.9 us  [start(): pl.pallas_call(functools.partial(start_kernel, sizes, runs), out_shape=[j...]
    pallas_call x5, Pallas kernels: 253 us -> 264 us  [the longest x3 136 us: plane_dot_scatter(): pl.pallas_call(functools.partial(dot_scatter_kernel, fs, dims, beside is...]
    all_gather x1, waiting for transfers between devices: 9.97 us -> 0.02 us  [over_z(): full = lax.all_gather(got, 'z', axis=1, tiled=True)]
  transfers between devices with their start and end apart: 6 -> 6, of which waited for: 3 -> 3; matrix products, arithmetic and copies ran while one was open for 4% -> 3% of each run, Pallas kernels for 52% -> 55%
where the time goes in v4:
time: 699 us; the launch traced here: 686 us
  Pallas kernels  602 us (86%)
  local copies, waits for them, and re-layouts  19.3 us (3%)
  other arithmetic  18.7 us (3%)
  waiting for transfers between devices  16.8 us (2%)
  between operations  14.9 us (2%)
  matrix products  13.2 us (2%)
    pallas_call x3, Pallas kernels, plane_dot_scatter(): pl.pallas_call(functools.partial(dot_scatter_kernel, fs, dims, beside is...  136 us
    pallas_call x2, Pallas kernels, plane_gather_dot(): pl.pallas_call(functools.partial(gather_dot_kernel, fs, dims, tile, other...  103 us
    pallas_call x1, Pallas kernels, start(): pl.pallas_call(functools.partial(start_kernel, sizes, runs), out_shape=[j...  94.9 us
    pallas_call x1, Pallas kernels, norm_turn(): pl.pallas_call(functools.partial(norm_turn_kernel, fs), out_shape=[jax.Sh...  91.5 us
    pallas_call x1, Pallas kernels, attn_bwd(): pl.pallas_call(functools.partial(attn_bwd_kernel, heads, head_dim, block,...  52 us
    pallas_call x1, Pallas kernels, attn_fwd(): pl.pallas_call(functools.partial(attn_fwd_kernel, heads, head_dim, block,...  45.1 us
    pallas_call x1, Pallas kernels, finish(): pl.pallas_call(functools.partial(finish_kernel, sizes, runs), out_shape=[...  43 us
    pallas_call x1, Pallas kernels, ffn(): pl.pallas_call(ffn_kernel, grid=(rows // block,), out_shape=[jax.ShapeDty...  36.3 us
  transfers between devices with their start and end apart: 6, of which 3 were waited for; matrix products, arithmetic and copies ran while one was open for 3% of the time, Pallas kernels for 55%

profile of v4, /device:TPU:22, one launch (start us, length us, event | category | flops | bytes accessed | tf_op | source)
XLA Modules:
  0.0 686.0 jit_solution(13372552396122289188)
XLA Ops:
  7.2 0.7 convert.12
  7.9 0.7 convert.13
  8.5 0.7 convert.14
  9.2 0.7 convert_element_type.57
  9.9 0.1 maximum_convert_fusion
  9.9 0.1 pad_maximum_fusion
  10.0 0.6 pad.15
  10.6 94.9 %start.1 = (f32[32,8,128]{2,1,0:T(8,128)}, bf16[4,4,128,768]{3,2,1,0:T(8,128)(2,1)}, bf16[4,128,1280]{2,1,0:T(8,128)(2,1)}, bf16[256,2048]{1,0:T(8,128)(2,1)}, b...) custom-call(f32[1,8,128]{2,1,0:T(8,128)} %bitcast.121, f32[64,2048]{1,0:T(8,128)} %q_ref.1, ...), custom_call_target="tpu_custom_call" | custom-call | flops 2640000000 | bytes 12000000 | tf_op jit(solution)/shard_map/start/pallas_call | solution.py:1419
  105.6 0.7 all-gather.6.cloned.1.call-update
  106.4 0.7 all-gather.8.cloned.1.call-update
  107.2 0.1 slice.45
  107.3 0.1 fusion.25
  107.4 0.1 broadcast_in_dim.29
  107.6 0.3 fusion.8
  107.9 0.1 fusion.21
  108.0 1.7 fusion.2
  109.7 58.9 %plane_gather_dot.2 = (bf16[2,8,128,2048]{3,2,1,0:T(8,128)(2,1)}, bf16[2,8,128,768]{3,2,1,0:T(8,128)(2,1)}) custom-call(bf16[2,128,2048]{2,1,0:T(8,128)(2,1)} %bitcast.102, bf16[2048,768]{1,0:T(8,128)(2,1)} %bitcast.92), custom_call_target="tpu_custom_call" | custom-call | flops 990000000 | bytes 4500000 | tf_op jit(solution)/shard_map/plane_gather_dot/pallas_call | solution.py:796
  168.7 0.3 iota_compare_fusion
  169.0 1.2 fusion.14.bias_ref
  170.2 45.1 %attn_fwd.1 = (bf16[2048,256]{1,0:T(8,128)(2,1)}, f32[2048,128]{1,0:T(8,128)}, bf16[2,8,128,2048]{3,2,1,0:T(8,128)(2,1)}) custom-call(s32[2]{0:T(128)} %copy-done.21, bf16[2048,768]{1,0:T(8,128)(2,1)} %bitcast.79, bf16[2048,768]{1,0:T(8,128)(2,1)} %bitcast.80, bf16[2048,768]{1,0:T(8,128)(2,1)} %bitcast.81, f32[4,2048]{1,0:T(4,128)} %fusion.14.bias_ref, ...), custom_call_target="tpu_custom_call" | custom-call | flops 572000000 | bytes 2600000 | tf_op jit(solution)/shard_map/attn_fwd/pallas_call | solution.py:94
  215.4 43.0 %plane_dot_scatter.3 = f32[2,128,2048]{2,1,0:T(8,128)} custom-call(bf16[2,8,128,256]{3,2,1,0:T(8,128)(2,1)} %bitcast.100, bf16[256,2048]{1,0:T(8,128)(2,1)} %all-gather.4.cloned.1.call-done.refs_1_.wo_ref), custom_call_target="tpu_custom_call" | custom-call | flops 990000000 | bytes 4500000 | tf_op jit(solution)/shard_map/plane_dot_scatter/pallas_call | solution.py:1104
  258.4 2.0 multiply_reduce_fusion
  260.4 1.3 copy-done
  261.7 1.2 multiply_convert_fusion
  262.9 44.4 %plane_gather_dot.3 = (bf16[2,8,128,2048]{3,2,1,0:T(8,128)(2,1)}, f32[2,8,128,640]{3,2,1,0:T(8,128)}) custom-call(bf16[2,128,2048]{2,1,0:T(8,128)(2,1)} %bitcast.99, bf16[640,2048]{1,0:T(8,128)(2,1)} %all-gather.6.cloned.1.call-done.refs_0_.refs_1_, bf16[2,8,128,2048]{3,2,1,0:T(8,128)(2,1)} %get-tuple-element.63.refs_1_), custom_call_target="tpu_custom_call" | custom-call | flops 990000000 | bytes 4500000 | tf_op jit(solution)/shard_map/plane_gather_dot/pallas_call | solution.py:796
  307.3 36.3 %ffn.1 = (bf16[2048,640]{1,0:T(8,128)(2,1)}, bf16[2048,1280]{1,0:T(8,128)(2,1)}, bf16[640,2048]{1,0:T(8,128)(2,1)}) custom-call(bf16[2048,2048]{1,0:T(8,128)(2,1)} %bitcast.87, f32[2048,640]{1,0:T(8,128)} %bitcast.98, bf16[2048,2048]{1,0:T(8,128)(2,1)} %bitcast.86, bf16[2048,1280]{1,0:T(8,128)(2,1)} %bitcast.90), custom_call_target="tpu_custom_call" | custom-call | flops 660000000 | bytes 3000000 | tf_op jit(solution)/shard_map/ffn/pallas_call | solution.py:1246
  343.8 46.0 %plane_dot_scatter.4 = (f32[2,128,2048]{2,1,0:T(8,128)}, bf16[2048,1280]{1,0:T(8,128)(2,1)}) custom-call(bf16[2,8,128,640]{3,2,1,0:T(8,128)(2,1)} %bitcast.104, bf16[640,2048]{1,0:T(8,128)(2,1)} %all-gather.6.cloned.1.call-done.refs_0_.refs_1_, bf16[2048,2048]{1,0:T(8,128)(2,1)} %bitcast.88, bf16[2048,1280]{1,0:T(8,128)(2,1)} %get-tuple-element.71.refs_3_), custom_call_target="tpu_custom_call" | custom-call | flops 990000000 | bytes 4500000 | tf_op jit(solution)/shard_map/plane_dot_scatter/pallas_call | solution.py:1104
  389.8 8.7 %reduce-scatter.4.cloned.1.call-done = bf16[160,2048]{1,0:T(8,128)(2,1)} async-done(((bf16[640,2048]{1,0:T(8,128)(2,1)}), bf16[160,2048]{1,0:T(8,128)(2,1)}) %reduce-scatter.4.cloned.1.call-update) | async-done | bytes 655376 | tf_op jit(solution)/shard_map/reduce_scatter | solution.py:1574
  398.5 0.4 reduce-scatter.8.cloned.1.call-start
  398.9 0.7 reshape.210.gain_ref
  399.6 0.4 copy-done.1
  400.1 2.8 fusion.13.refs_0_
  402.9 91.5 %norm_turn.1 = (bf16[2,8,128,256]{3,2,1,0:T(8,128)(2,1)}, bf16[256,2048]{1,0:T(8,128)(2,1)}, f32[2,128,2048]{2,1,0:T(8,128)}, f32[1,2048]{1,0:T(1,128)}) custom-call(bf16[2,8,128,1280]{3,2,1,0:T(8,128)(2,1)} %bitcast.89, bf16[2048,1280]{1,0:T(8,128)(2,1)} %bitcast.91, f32[2,128,2048]{2,1,0:T(8,128)} %bitcast.85, bf16[2,128,2048]{2,1,0:T(8,128)(2,1)} %bitcast.95, ...), custom_call_target="tpu_custom_call" | custom-call | flops 990000000 | bytes 4500000 | tf_op jit(solution)/shard_map/norm_turn/pallas_call | solution.py:1179
  494.3 0.6 reduce-scatter.6.cloned.1.call-done
  494.9 52.0 %attn_bwd.1 = (bf16[2048,256]{1,0:T(8,128)(2,1)}, bf16[2048,256]{1,0:T(8,128)(2,1)}, bf16[2048,256]{1,0:T(8,128)(2,1)}, f32[4,2048]{1,0:T(4,128)}, bf16[256,2048...) custom-call(s32[2]{0:T(128)} %copy-done.21, bf16[2048,768]{1,0:T(8,128)(2,1)} %bitcast.82, ...), custom_call_target="tpu_custom_call" | custom-call | flops 1100000000 | bytes 5000000 | tf_op jit(solution)/shard_map/attn_bwd/pallas_call | solution.py:282
  546.9 1.4 constant_dynamic-update-slice_fusion.2
  548.4 0.1 copy-done.10
  548.5 0.2 copy-done.8
  548.9 11.6 %convolution_convert_fusion = bf16[2048,768]{1,0:T(8,128)(2,1)} fusion(bf16[2048,2048]{1,0:T(8,128)(2,1)} %bitcast.125, bf16[2048,768]{1,0:T(8,128)(2,1)S(1)} %constant_dynamic-update-slice_fusion), kind=kOutput, calls=%fused_computation.5 | convolution fusion | flops 6444023808 | bytes 14680064 | tf_op jit(solution)/shard_map/rd,rk->dk/dot_general | solution.py:1688
  560.5 0.5 broadcast.69
  561.0 0.2 copy-done.20
  561.2 0.7 reduce.3
  561.9 1.2 convert_element_type.70
  563.1 47.3 %plane_dot_scatter.5 = f32[2,128,2048]{2,1,0:T(8,128)} custom-call(bf16[2,8,128,768]{3,2,1,0:T(8,128)(2,1)} %bitcast.96, bf16[2048,768]{1,0:T(8,128)(2,1)} %bitcast.93), custom_call_target="tpu_custom_call" | custom-call | flops 990000000 | bytes 4500000 | tf_op jit(solution)/shard_map/plane_dot_scatter/pallas_call | solution.py:1104
  610.4 2.3 fusion.11
  612.8 0.4 fusion.16
  613.2 0.3 dynamic_update_slice.4
  613.5 1.0 broadcast_in_dim.33
  614.6 1.2 slice.41
  615.8 0.1 fusion.18
  615.9 0.7 copy.31
  616.6 3.3 fusion.7.g_ref
  619.9 6.0 reduce-scatter.8.cloned.1.call-done
  625.9 43.0 %finish.1 = (f32[8,128]{1,0:T(8,128)}, bf16[256,2048]{1,0:T(8,128)(2,1)}, f32[64,5120]{1,0:T(8,128)}, f32[64,5120]{1,0:T(8,128)}, f32[64,2048]{1,0:T(8,128)}, /*index=5*/f32[64,2048]{1,0:T(8,128)}, f32[64,2048]{1,0:T(8,128)}) custom-call(f32[32,8,128]{2,1,0:T(8,128)} %bitcast.116, bf16[256,2048]{1,0:T(8,128)(2,1)} %fusion.7.g_ref, ...), custom_call_target="tpu_custom_call" | custom-call | flops 990000000 | bytes 4500000 | tf_op jit(solution)/shard_map/finish/pallas_call | solution.py:1486
  668.9 1.3 fusion.26
  670.2 1.2 slice.43
  671.4 1.0 copy.45
  672.4 1.0 copy.46
  673.4 0.8 copy.47
  674.2 0.8 copy.48
  675.0 0.8 copy.49
  675.8 0.8 copy.50
  676.6 1.1 copy.51
  677.6 1.1 copy.52
  (68 shorter events, 0.9 us)
Async XLA Ops:
  7.2 208.2 %all-gather.4.cloned.1.call-start = ((), (), s32[]{:S(2)}) async-start(), calls=%async_computation.3 | async-start | bytes 1310720 | tf_op jit(solution)/shard_map/all_gather | solution.py:1558
  105.5 1.6 copy-start.17
  105.6 2.1 copy-start.2
  105.6 157.3 %all-gather.6.cloned.1.call-start = ((), (), s32[]{:S(2)}) async-start(), calls=%async_computation.4 | async-start | bytes 3276800 | tf_op jit(solution)/shard_map/all_gather | solution.py:1558
  106.3 1.7 copy-start.11
  106.4 201.0 %all-gather.8.cloned.1.call-start = ((), (), s32[]{:S(2)}) async-start(), calls=%async_computation.5 | async-start | bytes 6553600 | tf_op jit(solution)/shard_map/all_gather | solution.py:1579
  107.1 291.4 %reduce-scatter.4.cloned.1.call-start = ((), (), s32[]{:S(2)}) async-start(), calls=%async_computation.6 | async-start | bytes 3276800 | tf_op jit(solution)/shard_map/reduce_scatter | solution.py:1574
  107.6 2.1 copy-start.21
  109.7 58.9 %copy-start.19 = (s32[2047]{0:T(1024)S(1)}, s32[2047]{0:T(1024)}, u32[]{:S(2)}) copy-start(s32[2047]{0:T(1024)} %param.17) | copy-start | bytes 24568
  260.3 1.3 copy-start
  343.7 151.2 %reduce-scatter.6.cloned.1.call-start = ((), (), s32[]{:S(2)}) async-start(), calls=%async_computation.7 | async-start | bytes 6553600 | tf_op jit(solution)/shard_map/reduce_scatter | solution.py:1585
  398.5 1.6 copy-start.1
  398.5 227.4 %reduce-scatter.8.cloned.1.call-start = ((), (), s32[]{:S(2)}) async-start(), calls=%async_computation.8 | async-start | bytes 3932160 | tf_op jit(solution)/shard_map/reduce_scatter | solution.py:1585
  546.9 1.5 copy-start.10
  546.9 1.8 copy-start.8
  548.8 11.6 %copy-start.4 = (bf16[2048,768]{1,0:T(8,128)(2,1)}, bf16[2048,768]{1,0:T(8,128)(2,1)S(1)}, u32[]{:S(2)}) copy-start(bf16[2048,768]{1,0:T(8,128)(2,1)S(1)} %constant_dynamic-update-slice_fusion) | copy-start | bytes 9437188
  560.5 0.7 copy-start.20
  560.5 1.4 copy-start.12
  610.4 2.4 copy-start.18
  610.4 6.1 copy-start.3
  619.9 51.6 %copy-start.7 = (bf16[256,2048]{1,0:T(8,128)(2,1)S(1)}, bf16[256,2048]{1,0:T(8,128)(2,1)}, u32[]{:S(2)}) copy-start(bf16[256,2048]{1,0:T(8,128)(2,1)} %get-tuple-element.77) | copy-start | bytes 3145732
  668.9 3.5 copy-start.9
  671.4 2.0 copy-start.16
  672.4 1.8 copy-start.15
  672.4 2.6 copy-start.14
  673.4 2.4 copy-start.13
  673.4 3.2 copy-start.6
  675.8 1.9 copy-start.5
Sparse Core Ops, SparseCore 0:
  105.7 45.3 all-gather.3
  152.7 53.5 all-gather.5
  207.9 96.3 all-gather.7
  343.8 54.5 reduce-scatter.3
  400.6 94.2 reduce-scatter.5
  560.6 65.1 reduce-scatter.7

commit v5 on v4

--- a/solution.py
+++ b/solution.py
@@ -1051,20 +1051,38 @@
     return partial
 
 
-def dot_scatter_kernel(fs, dims, beside, *refs):
+def row_blocks(ref, block, body):
+    per = ref.shape[1] // block
+
+    def one(i, carry):
+        here = pl.ds(pl.multiple_of(lax.rem(i, per) * block, block), block)
+        body(lax.div(i, per), here)
+        return carry
+
+    lax.fori_loop(0, 2 * per, one, 0)
+
+
+def dot_scatter_kernel(fs, dims, beside, then, *refs):
+    hbm, refs = refs[:2], refs[2:]
     if beside:
-        staged = Staged(refs[:2], refs[6:10])
-        later = Staged(refs[2:4], refs[10:14])
-        out_ref, g_ref, scratch = refs[4], refs[5], refs[14:]
+        later, refs = refs[:2], refs[2:]
+    if then:
+        (base_ref, factor_ref), refs = refs[:2], refs[2:]
+    outs, refs = refs[: 2 if then == "norm" else 1], refs[2 if then == "norm" else 1 :]
+    if beside:
+        g_ref, refs = refs[0], refs[1:]
+    staged, refs = Staged(hbm, refs[:4]), refs[4:]
+    if beside:
+        later, refs = Staged(later, refs[:4]), refs[4:]
         l_ref, r_ref = later.held
-    else:
-        staged = Staged(refs[:2], refs[3:7])
-        out_ref, scratch = refs[2], refs[7:]
+    sum_ref = outs[0]
+    if then:
+        sum_ref, refs = refs[0], refs[1:]
     plane = Plane(fs)
     plane.barrier()
     staged.wait()
     partial = slot_product(*staged.held, dims)
-    actions = scatter_actions(plane, partial, out_ref.shape[2], out_ref, scratch)
+    actions = scatter_actions(plane, partial, sum_ref.shape[2], sum_ref, refs)
     first = 2 * fs
     for action in actions[:first]:
         action()
@@ -1087,32 +1105,63 @@
     for action in actions[middle:]:
         action()
 
-
-def plane_dot_scatter(a, w, dims, seqs, collective_id, beside=None):
+    def normed(p, here):
+        hidden = base_ref[p, here, :].astype(jnp.float32) + sum_ref[p, here, :]
+        outs[0][p, here, :] = hidden
+        scale = lax.rsqrt(jnp.mean(hidden * hidden, axis=1, keepdims=True) + EPSILON)
+        outs[1][p, here, :] = (hidden * scale * factor_ref[...]).astype(jnp.bfloat16)
+
+    def result(p, here):
+        hidden = base_ref[p, here, :] + sum_ref[p, here, :]
+        outs[0][p, here, :] = (hidden * factor_ref[p, here, :]).astype(jnp.bfloat16)
+
+    if then:
+        row_blocks(sum_ref, 32, normed if then == "norm" else result)
+
+
+def plane_dot_scatter(
+    a, w, dims, seqs, collective_id, beside=None, norm=None, result=None
+):
     fs = lax.axis_size("fsdp")
     a = a.reshape(seqs, 2 * fs, -1, a.shape[1])
     b = a.shape[2]
     width = w.shape[1] if dims == NN else w.shape[0]
-    out_shape = [jax.ShapeDtypeStruct((seqs, b, width), jnp.float32)]
+    own = (seqs, b, width)
     args = [a, w]
+    in_specs = [anywhere()] * 2
     scratch = Staged.scratch(a, w)
+    out_shape = [jax.ShapeDtypeStruct(own, jnp.bfloat16 if result else jnp.float32)]
     if beside is not None:
-        l, r = beside
-        args += [l, r]
-        out_shape.append(jax.ShapeDtypeStruct((l.shape[1], r.shape[1]), jnp.bfloat16))
-        scratch += Staged.scratch(l, r)
+        args += beside
+        in_specs += [anywhere()] * 2
+        scratch += Staged.scratch(*beside)
+    if norm is not None:
+        args += [norm[0].reshape(own), norm[1]]
+        out_shape.append(jax.ShapeDtypeStruct(own, jnp.bfloat16))
+    if result is not None:
+        args += [result[0].reshape(own), result[1].reshape(seqs, b, 1)]
+    if norm is not None or result is not None:
+        in_specs += [vmem()] * 2
+        scratch.append(pltpu.VMEM(own, jnp.float32))
+    if beside is not None:
+        out_shape.append(
+            jax.ShapeDtypeStruct((beside[0].shape[1], beside[1].shape[1]), jnp.bfloat16)
+        )
+    then = "norm" if norm is not None else "result" if result is not None else ""
     out = pl.pallas_call(
-        functools.partial(dot_scatter_kernel, fs, dims, beside is not None),
+        functools.partial(dot_scatter_kernel, fs, dims, beside is not None, then),
         out_shape=out_shape,
-        in_specs=[anywhere()] * len(args),
+        in_specs=in_specs,
         out_specs=[vmem()] * len(out_shape),
         scratch_shapes=scratch + scatter_scratch(fs, b, width),
         compiler_params=plane_params(collective_id, 62),
         cost_estimate=estimate(45),
         name="plane_dot_scatter",
     )(*args)
-    rows = out[0].reshape(-1, width)
-    return rows if beside is None else (rows, out[1])
+    out = [out[0].reshape(-1, width)] + list(out[1:])
+    if norm is not None:
+        out[1] = out[1].reshape(-1, width)
+    return out if len(out) > 1 else out[0]
 
 
 def norm_turn_kernel(
@@ -1646,24 +1695,23 @@
     attended, lse, grad_branch = attn_fwd(
         qkv, offset_bias, lens, heads, head_dim, seqs, branch, 1
     )
-    attn_sum = plane_dot_scatter(attended, w_o, NN, seqs, 3)
-    hidden_one = x + attn_sum
-    scale_two = rms_scale(hidden_one)
+    hidden_one, normed_two = plane_dot_scatter(
+        attended, w_o, NN, seqs, 3, norm=(x_in, gain_two)
+    )
     normed_two, grad_hidden = plane_gather_dot(
-        (hidden_one * scale_two * gain_two).astype(BF), w_d, NT, seqs, 4, other=grad_branch,
-        dtype=F32,
+        normed_two, w_d, NT, seqs, 4, other=grad_branch, dtype=F32
     )
     hidden_ff, grad_gu, grad_w_down = ffn(normed_two, grad_hidden, grad_branch, w_gu)
     sum_down = ff_cols.scatter(grad_w_down)
+    last = (hidden_one, valid)
     if fs <= 4:
-        ff_sum, grad_w_gu = plane_dot_scatter(
-            hidden_ff, w_d, NN, seqs, 7, beside=(normed_two, grad_gu)
+        result, grad_w_gu = plane_dot_scatter(
+            hidden_ff, w_d, NN, seqs, 7, beside=(normed_two, grad_gu), result=last
         )
     else:
-        ff_sum = plane_dot_scatter(hidden_ff, w_d, NN, seqs, 7)
+        result = plane_dot_scatter(hidden_ff, w_d, NN, seqs, 7, result=last)
         grad_w_gu = jnp.einsum("rd,rf->df", normed_two, grad_gu, preferred_element_type=F32)
         grad_w_gu = grad_w_gu.astype(BF)
-    result = ((hidden_one + ff_sum) * valid).astype(BF)
     grad_w_gu, sum_down, grad_gu = lax.optimization_barrier((grad_w_gu, sum_down, grad_gu))
     sum_gu = reduce_z(grad_w_gu)
     if fs <= 4:
@@ -1672,6 +1720,7 @@
         )
     else:
         grad_normed_two = plane_dot_scatter(grad_gu, w_gu, NT, seqs, 5)
+        scale_two = rms_scale(hidden_one)
         gain_two_part = jnp.sum(grad_normed_two * hidden_one * scale_two, axis=0)
         grad_hidden_one = grad_rows + norm_back(grad_normed_two, hidden_one, scale_two, gain_two)
         grad_attn, grad_attended = plane_gather_dot(

time: 699 us -> 681 us (0.974)
    pallas_call x1, Pallas kernels: 36.3 us -> 27.3 us  [ffn(): pl.pallas_call(ffn_kernel, grid=(rows // block,), out_shape=[jax.ShapeDty...]
  transfers between devices with their start and end apart: 6 -> 6, of which waited for: 3 -> 3; matrix products, arithmetic and copies ran while one was open for 3% -> 3% of each run, Pallas kernels for 55% -> 56%
where the time goes in v5:
time: 681 us; the launch traced here: 674 us
  Pallas kernels  596 us (88%)
  waiting for transfers between devices  18.9 us (3%)
  local copies, waits for them, and re-layouts  18 us (3%)
  between operations  14.7 us (2%)
  other arithmetic  13.4 us (2%)
  matrix products  13.1 us (2%)
    pallas_call x3, Pallas kernels, plane_dot_scatter(): pl.pallas_call(functools.partial(dot_scatter_kernel, fs, dims, beside is...  141 us
    pallas_call x2, Pallas kernels, plane_gather_dot(): pl.pallas_call(functools.partial(gather_dot_kernel, fs, dims, tile, other...  103 us
    pallas_call x1, Pallas kernels, start(): pl.pallas_call(functools.partial(start_kernel, sizes, runs), out_shape=[j...  95 us
    pallas_call x1, Pallas kernels, norm_turn(): pl.pallas_call(functools.partial(norm_turn_kernel, fs), out_shape=[jax.Sh...  90.8 us
    pallas_call x1, Pallas kernels, attn_bwd(): pl.pallas_call(functools.partial(attn_bwd_kernel, heads, head_dim, block,...  50.3 us
    pallas_call x1, Pallas kernels, attn_fwd(): pl.pallas_call(functools.partial(attn_fwd_kernel, heads, head_dim, block,...  44.9 us
    pallas_call x1, Pallas kernels, finish(): pl.pallas_call(functools.partial(finish_kernel, sizes, runs), out_shape=[...  43 us
    pallas_call x1, Pallas kernels, ffn(): pl.pallas_call(ffn_kernel, grid=(rows // block,), out_shape=[jax.ShapeDty...  27.3 us
  transfers between devices with their start and end apart: 6, of which 3 were waited for; matrix products, arithmetic and copies ran while one was open for 3% of the time, Pallas kernels for 56%

profile of v5, /device:TPU:22, one launch (start us, length us, event | category | flops | bytes accessed | tf_op | source)
XLA Modules:
  0.0 674.1 jit_solution(3957036901885495244)
XLA Ops:
  7.2 0.7 convert.12
  7.9 0.7 convert.13
  8.5 0.7 convert.14
  9.2 0.7 convert_element_type.60
  9.9 0.1 maximum_convert_fusion
  9.9 0.1 pad_maximum_fusion
  10.0 0.6 pad.15
  10.6 95.0 %start.1 = (f32[32,8,128]{2,1,0:T(8,128)}, bf16[4,4,128,768]{3,2,1,0:T(8,128)(2,1)}, bf16[4,128,1280]{2,1,0:T(8,128)(2,1)}, bf16[256,2048]{1,0:T(8,128)(2,1)}, b...) custom-call(f32[1,8,128]{2,1,0:T(8,128)} %bitcast.112, f32[64,2048]{1,0:T(8,128)} %q_ref.1, ...), custom_call_target="tpu_custom_call" | custom-call | flops 2640000000 | bytes 12000000 | tf_op jit(solution)/shard_map/start/pallas_call | solution.py:1468
  105.7 0.7 all-gather.6.cloned.1.call-update
  106.4 0.7 all-gather.8.cloned.1.call-update
  107.1 0.2 reduce-scatter.4.cloned.1.call-start
  107.4 0.1 slice.45
  107.5 0.1 fusion.23
  107.5 0.1 mul.42
  107.6 0.1 broadcast_in_dim.28
  107.7 0.7 reshape.233.refs_3_.gain_ref
  108.4 0.3 fusion.8
  108.7 0.1 fusion.19
  108.8 1.7 fusion.2
  110.5 59.0 %plane_gather_dot.2 = (bf16[2,8,128,2048]{3,2,1,0:T(8,128)(2,1)}, bf16[2,8,128,768]{3,2,1,0:T(8,128)(2,1)}) custom-call(bf16[2,128,2048]{2,1,0:T(8,128)(2,1)} %bitcast.90, bf16[2048,768]{1,0:T(8,128)(2,1)} %bitcast.83), custom_call_target="tpu_custom_call" | custom-call | flops 990000000 | bytes 4500000 | tf_op jit(solution)/shard_map/plane_gather_dot/pallas_call | solution.py:796
  169.6 0.3 iota_compare_fusion
  169.9 1.2 fusion.12.bias_ref
  171.1 44.9 %attn_fwd.1 = (bf16[2048,256]{1,0:T(8,128)(2,1)}, f32[2048,128]{1,0:T(8,128)}, bf16[2,8,128,2048]{3,2,1,0:T(8,128)(2,1)}) custom-call(s32[2]{0:T(128)} %copy-done.20, bf16[2048,768]{1,0:T(8,128)(2,1)} %bitcast.70, bf16[2048,768]{1,0:T(8,128)(2,1)} %bitcast.71, bf16[2048,768]{1,0:T(8,128)(2,1)} %bitcast.72, f32[4,2048]{1,0:T(4,128)} %fusion.12.bias_ref, ...), custom_call_target="tpu_custom_call" | custom-call | flops 572000000 | bytes 2600000 | tf_op jit(solution)/shard_map/attn_fwd/pallas_call | solution.py:94
  216.1 45.5 %plane_dot_scatter.3 = (f32[2,128,2048]{2,1,0:T(8,128)}, bf16[2,128,2048]{2,1,0:T(8,128)(2,1)}) custom-call(bf16[2,8,128,256]{3,2,1,0:T(8,128)(2,1)} %bitcast.96, bf16[256,2048]{1,0:T(8,128)(2,1)} %all-gather.4.cloned.1.call-done.refs_1_.wo_ref, bf16[2,128,2048]{2,1,0:T(8,128)(2,1)} %bitcast.82, f32[1,2048]{1,0:T(1,128)} %reshape.233.refs_3_.gain_ref), custom_call_target="tpu_custom_call" | custom-call | flops 990000000 | bytes 4500000 | tf_op jit(solution)/shard_map/plane_dot_scatter/pallas_call | solution.py:1151
  261.7 44.4 %plane_gather_dot.3 = (bf16[2,8,128,2048]{3,2,1,0:T(8,128)(2,1)}, f32[2,8,128,640]{3,2,1,0:T(8,128)}) custom-call(bf16[2,128,2048]{2,1,0:T(8,128)(2,1)} %get-tuple-element.64.x_ref, bf16[640,2048]{1,0:T(8,128)(2,1)} %all-gather.6.cloned.1.call-done.refs_0_.refs_1_, bf16[2,8,128,2048]{3,2,1,0:T(8,128)(2,1)} %get-tuple-element.66.refs_1_), custom_call_target="tpu_custom_call" | custom-call | flops 990000000 | bytes 4500000 | tf_op jit(solution)/shard_map/plane_gather_dot/pallas_call | solution.py:796
  306.1 27.3 %ffn.1 = (bf16[2048,640]{1,0:T(8,128)(2,1)}, bf16[2048,1280]{1,0:T(8,128)(2,1)}, bf16[640,2048]{1,0:T(8,128)(2,1)}) custom-call(bf16[2048,2048]{1,0:T(8,128)(2,1)} %bitcast.76, f32[2048,640]{1,0:T(8,128)} %bitcast.89, bf16[2048,2048]{1,0:T(8,128)(2,1)} %bitcast.78, bf16[2048,1280]{1,0:T(8,128)(2,1)} %bitcast.80), custom_call_target="tpu_custom_call" | custom-call | flops 660000000 | bytes 3000000 | tf_op jit(solution)/shard_map/ffn/pallas_call | solution.py:1295
  333.5 0.6 copy-done.21
  334.0 0.7 compare_convert_fusion.refs_5_
  334.8 47.8 %plane_dot_scatter.4 = (bf16[2,128,2048]{2,1,0:T(8,128)(2,1)}, bf16[2048,1280]{1,0:T(8,128)(2,1)}) custom-call(bf16[2,8,128,640]{3,2,1,0:T(8,128)(2,1)} %bitcast.92, bf16[640,2048]{1,0:T(8,128)(2,1)} %all-gather.6.cloned.1.call-done.refs_0_.refs_1_, bf16[2048,2048]{1,0:T(8,128)(2,1)} %bitcast.77, bf16[2048,1280]{1,0:T(8,128)(2,1)} %get-tuple-element.75.refs_3_, ...), custom_call_target="tpu_custom_call" | custom-call | flops 990000000 | bytes 4500000 | tf_op jit(solution)/shard_map/plane_dot_scatter/pallas_call | solution.py:1151
  382.5 5.8 reduce-scatter.4.cloned.1.call-done
  388.4 90.8 %norm_turn.1 = (bf16[2,8,128,256]{3,2,1,0:T(8,128)(2,1)}, bf16[256,2048]{1,0:T(8,128)(2,1)}, f32[2,128,2048]{2,1,0:T(8,128)}, f32[1,2048]{1,0:T(1,128)}) custom-call(bf16[2,8,128,1280]{3,2,1,0:T(8,128)(2,1)} %bitcast.79, bf16[2048,1280]{1,0:T(8,128)(2,1)} %bitcast.81, f32[2,128,2048]{2,1,0:T(8,128)} %get-tuple-element.72.refs_4_.hid_ref, ...), custom_call_target="tpu_custom_call" | custom-call | flops 990000000 | bytes 4500000 | tf_op jit(solution)/shard_map/norm_turn/pallas_call | solution.py:1228
  479.2 5.6 reduce-scatter.6.cloned.1.call-done
  484.8 50.3 %attn_bwd.1 = (bf16[2048,256]{1,0:T(8,128)(2,1)}, bf16[2048,256]{1,0:T(8,128)(2,1)}, bf16[2048,256]{1,0:T(8,128)(2,1)}, f32[4,2048]{1,0:T(4,128)}, bf16[256,2048...) custom-call(s32[2]{0:T(128)} %copy-done.20, bf16[2048,768]{1,0:T(8,128)(2,1)} %bitcast.73, ...), custom_call_target="tpu_custom_call" | custom-call | flops 1100000000 | bytes 5000000 | tf_op jit(solution)/shard_map/attn_bwd/pallas_call | solution.py:282
  535.2 1.4 constant_dynamic-update-slice_fusion.2
  536.6 0.1 copy-done.9
  536.8 0.2 copy-done.7
  537.1 11.5 %convolution_convert_fusion = bf16[2048,768]{1,0:T(8,128)(2,1)} fusion(bf16[2048,2048]{1,0:T(8,128)(2,1)} %bitcast.116, bf16[2048,768]{1,0:T(8,128)(2,1)S(1)} %constant_dynamic-update-slice_fusion), kind=kOutput, calls=%fused_computation.4 | convolution fusion | flops 6444023808 | bytes 14680064 | tf_op jit(solution)/shard_map/rd,rk->dk/dot_general | solution.py:1737
  548.7 0.5 broadcast.88
  549.2 0.2 copy-done.19
  549.3 0.7 reduce.3
  550.0 0.1 reshape_squeeze.3
  550.1 1.2 convert_element_type.72
  551.3 47.6 %plane_dot_scatter.5 = f32[2,128,2048]{2,1,0:T(8,128)} custom-call(bf16[2,8,128,768]{3,2,1,0:T(8,128)(2,1)} %bitcast.87, bf16[2048,768]{1,0:T(8,128)(2,1)} %bitcast.84), custom_call_target="tpu_custom_call" | custom-call | flops 990000000 | bytes 4500000 | tf_op jit(solution)/shard_map/plane_dot_scatter/pallas_call | solution.py:1151
  598.9 2.3 fusion.11
  601.2 0.1 reshape.249
  601.3 0.4 fusion.14
  601.7 0.2 dynamic_update_slice.4
  601.9 1.0 broadcast_in_dim.32
  603.0 1.2 slice.41
  604.2 0.1 fusion.16
  604.3 0.7 copy.35
  605.0 3.3 fusion.7.g_ref
  608.3 6.0 reduce-scatter.8.cloned.1.call-done
  614.2 43.0 %finish.1 = (f32[8,128]{1,0:T(8,128)}, bf16[256,2048]{1,0:T(8,128)(2,1)}, f32[64,5120]{1,0:T(8,128)}, f32[64,5120]{1,0:T(8,128)}, f32[64,2048]{1,0:T(8,128)}, /*index=5*/f32[64,2048]{1,0:T(8,128)}, f32[64,2048]{1,0:T(8,128)}) custom-call(f32[32,8,128]{2,1,0:T(8,128)} %bitcast.107, bf16[256,2048]{1,0:T(8,128)(2,1)} %fusion.7.g_ref, ...), custom_call_target="tpu_custom_call" | custom-call | flops 990000000 | bytes 4500000 | tf_op jit(solution)/shard_map/finish/pallas_call | solution.py:1535
  657.2 1.3 fusion.24
  658.6 1.2 slice.43
  659.8 1.0 copy.49
  660.7 1.0 copy.50
  661.7 0.8 copy.51
  662.5 0.8 copy.52
  663.3 0.8 copy.53
  664.1 0.8 copy.54
  664.9 1.1 copy.55
  666.0 1.1 copy.56
  (64 shorter events, 0.7 us)
Async XLA Ops:
  7.2 208.9 %all-gather.4.cloned.1.call-start = ((), (), s32[]{:S(2)}) async-start(), calls=%async_computation.3 | async-start | bytes 1310720 | tf_op jit(solution)/shard_map/all_gather | solution.py:1607
  105.6 1.8 copy-start.16
  105.6 2.9 copy-start.1
  105.6 156.0 %all-gather.6.cloned.1.call-start = ((), (), s32[]{:S(2)}) async-start(), calls=%async_computation.4 | async-start | bytes 3276800 | tf_op jit(solution)/shard_map/all_gather | solution.py:1607
  106.4 2.4 copy-start.10
  106.4 199.7 %all-gather.8.cloned.1.call-start = ((), (), s32[]{:S(2)}) async-start(), calls=%async_computation.5 | async-start | bytes 6553600 | tf_op jit(solution)/shard_map/all_gather | solution.py:1628
  107.1 281.2 %reduce-scatter.4.cloned.1.call-start = ((), (), s32[]{:S(2)}) async-start(), calls=%async_computation.6 | async-start | bytes 3276800 | tf_op jit(solution)/shard_map/reduce_scatter | solution.py:1623
  108.4 2.1 copy-start.20
  110.5 59.1 %copy-start.18 = (s32[2047]{0:T(1024)S(1)}, s32[2047]{0:T(1024)}, u32[]{:S(2)}) copy-start(s32[2047]{0:T(1024)} %param.17) | copy-start | bytes 24568
  333.4 0.7 copy-start.21
  333.4 151.4 %reduce-scatter.6.cloned.1.call-start = ((), (), s32[]{:S(2)}) async-start(), calls=%async_computation.7 | async-start | bytes 6553600 | tf_op jit(solution)/shard_map/reduce_scatter | solution.py:1634
  388.4 225.9 %reduce-scatter.8.cloned.1.call-start = ((), (), s32[]{:S(2)}) async-start(), calls=%async_computation.8 | async-start | bytes 3932160 | tf_op jit(solution)/shard_map/reduce_scatter | solution.py:1634
  535.1 1.5 copy-start.9
  535.2 1.8 copy-start.7
  537.1 11.5 %copy-start.3 = (bf16[2048,768]{1,0:T(8,128)(2,1)}, bf16[2048,768]{1,0:T(8,128)(2,1)S(1)}, u32[]{:S(2)}) copy-start(bf16[2048,768]{1,0:T(8,128)(2,1)S(1)} %constant_dynamic-update-slice_fusion) | copy-start | bytes 9437188
  548.6 0.7 copy-start.19
  548.6 1.4 copy-start.11
  551.3 47.6 %copy-start.2 = (bf16[256,2048]{1,0:T(8,128)(2,1)S(1)}, bf16[256,2048]{1,0:T(8,128)(2,1)}, u32[]{:S(2)}) copy-start(bf16[256,2048]{1,0:T(8,128)(2,1)} %get-tuple-element.58) | copy-start | bytes 3145732
  598.9 2.4 copy-start.17
  598.9 6.1 copy-start
  608.3 51.5 %copy-start.6 = (bf16[256,2048]{1,0:T(8,128)(2,1)S(1)}, bf16[256,2048]{1,0:T(8,128)(2,1)}, u32[]{:S(2)}) copy-start(bf16[256,2048]{1,0:T(8,128)(2,1)} %get-tuple-element.81) | copy-start | bytes 3145732
  657.2 3.5 copy-start.8
  659.8 2.0 copy-start.15
  660.7 1.8 copy-start.14
  660.7 2.6 copy-start.13
  661.7 2.4 copy-start.12
  661.7 3.2 copy-start.5
  664.1 1.9 copy-start.4
Sparse Core Ops, SparseCore 0:
  105.7 45.3 all-gather.3
  152.7 53.6 all-gather.5
  208.0 96.3 all-gather.7
  333.5 54.7 reduce-scatter.3
  390.5 94.2 reduce-scatter.5
  548.8 65.4 reduce-scatter.7

commit v6 on v5

--- a/solution.py
+++ b/solution.py
@@ -137,26 +137,24 @@
     last_seq, last_blk = seqs - 1, blocks - 1
     grid_step = seq * blocks + blk
     steps = seqs * blocks
-    if fs:
-        x_ref, wg_ref, gu_ref, dq_ref, dk_ref, dv_ref, dbias_ref = refs[:7]
-        out_ref, sum_ref, got_ref = refs[7:10]
-        refs = refs[10:]
-        column = Column(wg_ref, sum_ref, refs[6:9])
-        back = Back((fs, 1, 2), gu_ref, got_ref, refs[9:12])
-        swap = Swap(x_ref, out_ref, refs[12:])
-
-        def begin():
-            plane_and_column_greet()
-            swap.start()
-            column.start()
-            back.start()
-
-        todo = {0: begin, steps // 2: swap.hand_on}
-        for step, action in todo.items():
-            pl.when(grid_step == step)(action)
-    else:
-        dq_ref, dk_ref, dv_ref, dbias_ref = refs[:4]
-        refs = refs[4:]
+    x_ref, wg_ref, gu_ref, n_hbm, dqkv_ref, dbias_ref, dw_ref = refs[:7]
+    out_ref, sum_ref, got_ref = refs[7:10]
+    refs = refs[10:]
+    n_ref, n_sem, dw_acc = refs[6:9]
+    refs = refs[:6] + refs[9:]
+    column = Column(wg_ref, sum_ref, refs[6:9])
+    back = Back((fs, 1, 2), gu_ref, got_ref, refs[9:12])
+    swap = Swap(x_ref, out_ref, refs[12:])
+
+    def begin():
+        plane_and_column_greet()
+        swap.start()
+        column.start()
+        back.start()
+
+    todo = {0: begin, steps // 2: swap.hand_on}
+    for step, action in todo.items():
+        pl.when(grid_step == step)(action)
     skew_ref, kt_ref, vt_ref, acc_ref, dkt_ref, dvt_ref = refs[:6]
     width = heads * head_dim
 
@@ -164,9 +162,14 @@
     def _():
         fill_skew(bias_ref, skew_ref, heads, block, length)
         acc_ref[...] = jnp.zeros_like(acc_ref)
+        dw_acc[...] = jnp.zeros_like(dw_acc)
+
+    rows = pl.ds(pl.multiple_of(seq * length, length), length)
+    load = pltpu.make_async_copy(n_hbm.at[rows], n_ref, n_sem)
 
     @pl.when(blk == 0)
     def _():
+        load.start()
         kt_ref[...] = k_ref[...].T
         vt_ref[...] = v_ref[...].T
         dkt_ref[...] = jnp.zeros_like(dkt_ref)
@@ -193,12 +196,23 @@
         acc_ref[h, :, pl.ds(start, length)] += ds.astype(jnp.float32)
         dkt_ref[...] += dotf(q_t * rmask, ds)
         dvt_ref[...] += dotf(g_t * rmask, probs.astype(jnp.bfloat16))
-    dq_ref[...] = dq.astype(jnp.bfloat16)
+    here = pl.ds(pl.multiple_of(blk * block, block), block)
+    dqkv_ref[here, :width] = dq.astype(jnp.bfloat16)
 
     @pl.when(blk == last_blk)
     def _():
-        dk_ref[...] = dkt_ref[...].astype(jnp.bfloat16).T
-        dv_ref[...] = dvt_ref[...].astype(jnp.bfloat16).T
+        dqkv_ref[:, width : 2 * width] = dkt_ref[...].astype(jnp.bfloat16).T
+        dqkv_ref[:, 2 * width :] = dvt_ref[...].astype(jnp.bfloat16).T
+        load.wait()
+
+        def weight(i, carry):
+            cols = pl.ds(pl.multiple_of(i * 256, 256), 256)
+            part = dw_acc[cols, :] + dotf(n_ref[:, cols].T, dqkv_ref[...])
+            dw_acc[cols, :] = part
+            dw_ref[cols, :] = part.astype(jnp.bfloat16)
+            return carry
+
+        lax.fori_loop(0, n_ref.shape[1] // 256, weight, 0)
 
     @pl.when((seq == last_seq) & (blk == last_blk))
     def _():
@@ -215,84 +229,75 @@
                 total = total + (pltpu.roll(part, n - 1 - i, 1) if i < n - 1 else part)[i : i + 1]
             dbias_ref[h : h + 1, :] = total
 
-    if fs:
-
-        @pl.when(grid_step == steps - 1)
-        def _():
-            column.close()
-            back.arrived()
-            back.close()
-            swap.close()
+    @pl.when(grid_step == steps - 1)
+    def _():
+        column.close()
+        back.arrived()
+        back.close()
+        swap.close()
 
 
 def attn_bwd(
-    qkv, grad, lse, offset_bias, lens, heads, head_dim, seqs, block=256, swapped=None,
-    column=None, spread=None, collective_id=None,
+    qkv, grad, lse, offset_bias, lens, heads, head_dim, seqs, normed, swapped, column, spread,
+    collective_id, block=256,
 ):
     rows, width3 = qkv.shape
     width = width3 // 3
     length = rows // seqs
     block = min(block, length)
     blocks = length // block
-    in_specs = [
-        pl.BlockSpec(memory_space=pltpu.SMEM),
-        pl.BlockSpec((block, width), lambda s, i: (s * blocks + i, 0)),
-        pl.BlockSpec((length, width), lambda s, i: (s, 1)),
-        pl.BlockSpec((length, width), lambda s, i: (s, 2)),
-        pl.BlockSpec((block, width), lambda s, i: (s * blocks + i, 0)),
-        pl.BlockSpec((block, 128), lambda s, i: (s * blocks + i, 0)),
-        pl.BlockSpec((heads, 2 * length), lambda s, i: (0, 0)),
-    ]
-    out_specs = [
-        pl.BlockSpec((block, width), lambda s, i: (s * blocks + i, 0)),
-        pl.BlockSpec((length, width), lambda s, i: (s, 0)),
-        pl.BlockSpec((length, width), lambda s, i: (s, 0)),
-        pl.BlockSpec((heads, 2 * length), lambda s, i: (0, 0)),
-    ]
-    out_shape = [
-        jax.ShapeDtypeStruct((rows, width), jnp.bfloat16),
-        jax.ShapeDtypeStruct((rows, width), jnp.bfloat16),
-        jax.ShapeDtypeStruct((rows, width), jnp.bfloat16),
-        jax.ShapeDtypeStruct((heads, 2 * length), jnp.float32),
-    ]
-    scratch = [
-        pltpu.VMEM((heads, block, 2 * length - block), jnp.float32),
-        pltpu.VMEM((width, length), jnp.bfloat16),
-        pltpu.VMEM((width, length), jnp.bfloat16),
-        pltpu.VMEM((heads, block, 2 * length - block), jnp.float32),
-        pltpu.VMEM((width, length), jnp.float32),
-        pltpu.VMEM((width, length), jnp.float32),
-    ]
-    args = [lens, qkv, qkv, qkv, grad, lse, offset_bias]
-    fs = 0
-    if swapped is not None:
-        fs, zs = lax.axis_size("fsdp"), lax.axis_size("z")
-        column = column.reshape(zs, -1, column.shape[1])
-        spread = spread.reshape(2 * fs, -1, spread.shape[2])
-        args += [swapped, column, spread]
-        in_specs += [vmem()] * 3
-        out_specs += [anywhere(), vmem(), anywhere()]
-        out_shape += [
+    fs, zs = lax.axis_size("fsdp"), lax.axis_size("z")
+    column = column.reshape(zs, -1, column.shape[1])
+    spread = spread.reshape(2 * fs, -1, spread.shape[2])
+    wide = normed.shape[1]
+    return pl.pallas_call(
+        functools.partial(attn_bwd_kernel, heads, head_dim, block, length, seqs, fs),
+        grid=(seqs, blocks),
+        in_specs=[
+            pl.BlockSpec(memory_space=pltpu.SMEM),
+            pl.BlockSpec((block, width), lambda s, i: (s * blocks + i, 0)),
+            pl.BlockSpec((length, width), lambda s, i: (s, 1)),
+            pl.BlockSpec((length, width), lambda s, i: (s, 2)),
+            pl.BlockSpec((block, width), lambda s, i: (s * blocks + i, 0)),
+            pl.BlockSpec((block, 128), lambda s, i: (s * blocks + i, 0)),
+            pl.BlockSpec((heads, 2 * length), lambda s, i: (0, 0)),
+        ]
+        + [vmem()] * 3
+        + [anywhere()],
+        out_specs=[
+            pl.BlockSpec((length, width3), lambda s, i: (s, 0)),
+            pl.BlockSpec((heads, 2 * length), lambda s, i: (0, 0)),
+            vmem(), anywhere(), vmem(), anywhere(),
+        ],
+        out_shape=[
+            jax.ShapeDtypeStruct((rows, width3), jnp.bfloat16),
+            jax.ShapeDtypeStruct((heads, 2 * length), jnp.float32),
+            jax.ShapeDtypeStruct((wide, width3), jnp.bfloat16),
             jax.ShapeDtypeStruct(swapped.shape, swapped.dtype),
             jax.ShapeDtypeStruct(column.shape[1:], jnp.float32),
             jax.ShapeDtypeStruct(spread.shape, spread.dtype),
+        ],
+        scratch_shapes=[
+            pltpu.VMEM((heads, block, 2 * length - block), jnp.float32),
+            pltpu.VMEM((width, length), jnp.bfloat16),
+            pltpu.VMEM((width, length), jnp.bfloat16),
+            pltpu.VMEM((heads, block, 2 * length - block), jnp.float32),
+            pltpu.VMEM((width, length), jnp.float32),
+            pltpu.VMEM((width, length), jnp.float32),
+            pltpu.VMEM((length, wide), jnp.bfloat16),
+            pltpu.SemaphoreType.DMA,
+            pltpu.VMEM((wide, width3), jnp.float32),
         ]
-        scratch += Column.scratch(column) + Back.scratch(2 * fs)
-        scratch += Swap.scratch(fs, *swapped.shape)
-    return pl.pallas_call(
-        functools.partial(attn_bwd_kernel, heads, head_dim, block, length, seqs, fs),
-        grid=(seqs, blocks),
-        in_specs=in_specs,
-        out_specs=out_specs,
-        out_shape=out_shape,
-        scratch_shapes=scratch,
+        + Column.scratch(column)
+        + Back.scratch(2 * fs)
+        + Swap.scratch(fs, *swapped.shape),
         compiler_params=pltpu.CompilerParams(
             dimension_semantics=("arbitrary", "arbitrary"), vmem_limit_bytes=62 * 1024 * 1024,
-            collective_id=collective_id, has_side_effects=fs > 0,
+            collective_id=collective_id, has_side_effects=True,
         ),
         cost_estimate=estimate(50),
         name="attn_bwd",
-    )(*args)
+    )(lens, qkv, qkv, qkv, grad, lse, offset_bias, swapped, column, spread, normed)
 
 MESH_ID = pl.DeviceIdType.MESH
 MIB = 1024 * 1024
@@ -1728,15 +1733,11 @@
         )
         grad_w_o = jnp.einsum("rk,rd->kd", attended, grad_attn, preferred_element_type=F32)
         grad_w_o = grad_w_o.astype(BF)
-    dq, dk, dv, grad_offset, output, sum_o, got_gu = attn_bwd(
-        qkv, grad_attended, lse, offset_bias, lens, heads, head_dim, seqs,
-        swapped=result, column=head_cols.whole(grad_w_o), spread=sum_gu, collective_id=11,
+    dqkv, grad_offset, grad_w_qkv, output, sum_o, got_gu = attn_bwd(
+        qkv, grad_attended, lse, offset_bias, lens, heads, head_dim, seqs, normed,
+        result, head_cols.whole(grad_w_o), sum_gu, 11,
     )
     output = output.reshape(seqs, block_len, width)
-    dqkv = jnp.concatenate([dq, dk, dv], axis=1)
-    grad_w_qkv = jnp.einsum("rd,rk->dk", normed, dqkv, preferred_element_type=F32)
-    grad_w_qkv, dqkv = lax.optimization_barrier((grad_w_qkv.astype(BF), dqkv))
-    grad_w_qkv, sum_gu = lax.optimization_barrier((grad_w_qkv, sum_gu))
     sum_qkv = reduce_z(grad_w_qkv)
     grad_normed = plane_dot_scatter(dqkv, w_qkv, NT, seqs, 8)
     gain_one_part = jnp.sum(grad_normed * x * scale_one, axis=0)

time: 681 us -> 672 us (0.987)
  matrix products: 13.1 us -> 1.61 us
    dot_general x1 -> x0, matrix products: 11.5 us -> none  [shards(): jnp.einsum('rd,rk->dk', normed, dqkv, preferred_element_type=F32)]
    pallas_call x1, Pallas kernels: 50.3 us -> 58.7 us  [attn_bwd(): pl.pallas_call(functools.partial(attn_bwd_kernel, heads, head_dim, block,...]
  transfers between devices with their start and end apart: 6 -> 6, of which waited for: 3 -> 3; matrix products, arithmetic and copies ran while one was open for 3% -> 3% of each run, Pallas kernels for 56% -> 57%
where the time goes in v6:
time: 672 us; the launch traced here: 665 us
  Pallas kernels  601 us (89%)
  waiting for transfers between devices  18 us (3%)
  local copies, waits for them, and re-layouts  15.9 us (2%)
  between operations  14.6 us (2%)
  other arithmetic  13.4 us (2%)
    pallas_call x3, Pallas kernels, plane_dot_scatter(): pl.pallas_call(functools.partial(dot_scatter_kernel, fs, dims, beside is...  138 us
    pallas_call x2, Pallas kernels, plane_gather_dot(): pl.pallas_call(functools.partial(gather_dot_kernel, fs, dims, tile, other...  103 us
    pallas_call x1, Pallas kernels, start(): pl.pallas_call(functools.partial(start_kernel, sizes, runs), out_shape=[j...  94.9 us
    pallas_call x1, Pallas kernels, norm_turn(): pl.pallas_call(functools.partial(norm_turn_kernel, fs), out_shape=[jax.Sh...  90.8 us
    pallas_call x1, Pallas kernels, attn_bwd(): pl.pallas_call(functools.partial(attn_bwd_kernel, heads, head_dim, block,...  58.7 us
    pallas_call x1, Pallas kernels, attn_fwd(): pl.pallas_call(functools.partial(attn_fwd_kernel, heads, head_dim, block,...  44.9 us
    pallas_call x1, Pallas kernels, finish(): pl.pallas_call(functools.partial(finish_kernel, sizes, runs), out_shape=[...  43 us
    pallas_call x1, Pallas kernels, ffn(): pl.pallas_call(ffn_kernel, grid=(rows // block,), out_shape=[jax.ShapeDty...  27.3 us
  transfers between devices with their start and end apart: 6, of which 3 were waited for; matrix products, arithmetic and copies ran while one was open for 3% of the time, Pallas kernels for 57%

profile of v6, /device:TPU:22, one launch (start us, length us, event | category | flops | bytes accessed | tf_op | source)
XLA Modules:
  0.0 664.9 jit_solution(16069525966407645521)
XLA Ops:
  7.2 0.0 all-gather.4.cloned.1.call-start
  7.2 0.7 convert.12
  7.9 0.7 convert.13
  8.5 0.7 convert.14
  9.2 0.7 convert_element_type.57
  9.9 0.1 maximum_convert_fusion
  9.9 0.1 pad_maximum_fusion
  10.0 0.6 pad.15
  10.6 94.9 %start.1 = (f32[32,8,128]{2,1,0:T(8,128)}, bf16[4,4,128,768]{3,2,1,0:T(8,128)(2,1)}, bf16[4,128,1280]{2,1,0:T(8,128)(2,1)}, bf16[256,2048]{1,0:T(8,128)(2,1)}, b...) custom-call(f32[1,8,128]{2,1,0:T(8,128)} %bitcast.111, f32[64,2048]{1,0:T(8,128)} %q_ref.1, ...), custom_call_target="tpu_custom_call" | custom-call | flops 2640000000 | bytes 12000000 | tf_op jit(solution)/shard_map/start/pallas_call | solution.py:1473
  105.6 0.0 all-gather.6.cloned.1.call-start
  105.7 0.7 all-gather.6.cloned.1.call-update
  106.4 0.0 all-gather.8.cloned.1.call-start
  106.4 0.7 all-gather.8.cloned.1.call-update
  107.1 0.2 reduce-scatter.4.cloned.1.call-start
  107.4 0.1 slice.45
  107.4 0.1 fusion.23
  107.5 0.1 mul.42
  107.6 0.1 broadcast_in_dim.28
  107.7 0.7 reshape.233.refs_3_.gain_ref
  108.4 0.3 fusion.8
  108.7 0.1 fusion.19
  108.8 1.7 fusion.2
  110.5 59.0 %plane_gather_dot.2 = (bf16[2,8,128,2048]{3,2,1,0:T(8,128)(2,1)}, bf16[2,8,128,768]{3,2,1,0:T(8,128)(2,1)}) custom-call(bf16[2,128,2048]{2,1,0:T(8,128)(2,1)} %bitcast.88, bf16[2048,768]{1,0:T(8,128)(2,1)} %bitcast.81), custom_call_target="tpu_custom_call" | custom-call | flops 990000000 | bytes 4500000 | tf_op jit(solution)/shard_map/plane_gather_dot/pallas_call | solution.py:801
  169.6 0.3 iota_compare_fusion
  169.9 1.2 fusion.12.bias_ref
  171.1 44.9 %attn_fwd.1 = (bf16[2048,256]{1,0:T(8,128)(2,1)}, f32[2048,128]{1,0:T(8,128)}, bf16[2,8,128,2048]{3,2,1,0:T(8,128)(2,1)}) custom-call(s32[2]{0:T(128)} %copy-done.15, bf16[2048,768]{1,0:T(8,128)(2,1)} %bitcast.68, bf16[2048,768]{1,0:T(8,128)(2,1)} %bitcast.69, bf16[2048,768]{1,0:T(8,128)(2,1)} %bitcast.70, f32[4,2048]{1,0:T(4,128)} %fusion.12.bias_ref, ...), custom_call_target="tpu_custom_call" | custom-call | flops 572000000 | bytes 2600000 | tf_op jit(solution)/shard_map/attn_fwd/pallas_call | solution.py:94
  216.1 45.6 %plane_dot_scatter.3 = (f32[2,128,2048]{2,1,0:T(8,128)}, bf16[2,128,2048]{2,1,0:T(8,128)(2,1)}) custom-call(bf16[2,8,128,256]{3,2,1,0:T(8,128)(2,1)} %bitcast.95, bf16[256,2048]{1,0:T(8,128)(2,1)} %all-gather.4.cloned.1.call-done.refs_1_.wo_ref, bf16[2,128,2048]{2,1,0:T(8,128)(2,1)} %bitcast.80, f32[1,2048]{1,0:T(1,128)} %reshape.233.refs_3_.gain_ref), custom_call_target="tpu_custom_call" | custom-call | flops 990000000 | bytes 4500000 | tf_op jit(solution)/shard_map/plane_dot_scatter/pallas_call | solution.py:1156
  261.7 44.4 %plane_gather_dot.3 = (bf16[2,8,128,2048]{3,2,1,0:T(8,128)(2,1)}, f32[2,8,128,640]{3,2,1,0:T(8,128)}) custom-call(bf16[2,128,2048]{2,1,0:T(8,128)(2,1)} %get-tuple-element.60.x_ref, bf16[640,2048]{1,0:T(8,128)(2,1)} %all-gather.6.cloned.1.call-done.refs_0_.refs_1_, bf16[2,8,128,2048]{3,2,1,0:T(8,128)(2,1)} %get-tuple-element.62.refs_1_), custom_call_target="tpu_custom_call" | custom-call | flops 990000000 | bytes 4500000 | tf_op jit(solution)/shard_map/plane_gather_dot/pallas_call | solution.py:801
  306.1 27.3 %ffn.1 = (bf16[2048,640]{1,0:T(8,128)(2,1)}, bf16[2048,1280]{1,0:T(8,128)(2,1)}, bf16[640,2048]{1,0:T(8,128)(2,1)}) custom-call(bf16[2048,2048]{1,0:T(8,128)(2,1)} %bitcast.74, f32[2048,640]{1,0:T(8,128)} %bitcast.87, bf16[2048,2048]{1,0:T(8,128)(2,1)} %bitcast.76, bf16[2048,1280]{1,0:T(8,128)(2,1)} %bitcast.78), custom_call_target="tpu_custom_call" | custom-call | flops 660000000 | bytes 3000000 | tf_op jit(solution)/shard_map/ffn/pallas_call | solution.py:1300
  333.5 0.0 reduce-scatter.6.cloned.1.call-start
  333.5 0.6 copy-done.16
  334.1 0.7 compare_convert_fusion.refs_5_
  334.8 47.8 %plane_dot_scatter.4 = (bf16[2,128,2048]{2,1,0:T(8,128)(2,1)}, bf16[2048,1280]{1,0:T(8,128)(2,1)}) custom-call(bf16[2,8,128,640]{3,2,1,0:T(8,128)(2,1)} %bitcast.91, bf16[640,2048]{1,0:T(8,128)(2,1)} %all-gather.6.cloned.1.call-done.refs_0_.refs_1_, bf16[2048,2048]{1,0:T(8,128)(2,1)} %bitcast.75, bf16[2048,1280]{1,0:T(8,128)(2,1)} %get-tuple-element.71.refs_3_, ...), custom_call_target="tpu_custom_call" | custom-call | flops 990000000 | bytes 4500000 | tf_op jit(solution)/shard_map/plane_dot_scatter/pallas_call | solution.py:1156
  382.6 5.8 reduce-scatter.4.cloned.1.call-done
  388.4 0.0 reduce-scatter.8.cloned.1.call-start
  388.5 90.8 %norm_turn.1 = (bf16[2,8,128,256]{3,2,1,0:T(8,128)(2,1)}, bf16[256,2048]{1,0:T(8,128)(2,1)}, f32[2,128,2048]{2,1,0:T(8,128)}, f32[1,2048]{1,0:T(1,128)}) custom-call(bf16[2,8,128,1280]{3,2,1,0:T(8,128)(2,1)} %bitcast.77, bf16[2048,1280]{1,0:T(8,128)(2,1)} %bitcast.79, f32[2,128,2048]{2,1,0:T(8,128)} %get-tuple-element.68.refs_4_.hid_ref, ...), custom_call_target="tpu_custom_call" | custom-call | flops 990000000 | bytes 4500000 | tf_op jit(solution)/shard_map/norm_turn/pallas_call | solution.py:1233
  479.3 5.6 reduce-scatter.6.cloned.1.call-done
  484.8 58.7 %attn_bwd.1 = (bf16[2048,768]{1,0:T(8,128)(2,1)}, f32[4,2048]{1,0:T(4,128)}, bf16[2048,768]{1,0:T(8,128)(2,1)}, bf16[256,2048]{1,0:T(8,128)(2,1)}, f32[64,2048]{1,0:T(8,128)}, /*index=5*/bf16[8,64,1280]{2,1,0:T(8,128)(2,1)}) custom-call(s32[2]{0:T(128)} %copy-done.15, bf16[2048,768]{1,0:T(8,128)(2,1)} %bitcast.71, bf16[2048,768]{1,0:T(8,128)(2,1)} %bitcast.72, ...), custom_call_target="tpu_custom_call" | custom-call | flops 1100000000 | bytes 5000000 | tf_op jit(solution)/shard_map/attn_bwd/pallas_call | solution.py:253
  543.6 0.5 broadcast.88
  544.1 0.1 copy-done.18
  544.3 0.7 reduce.3
  544.9 0.1 reshape_squeeze.3
  545.0 1.2 convert_element_type.68
  546.2 44.6 %plane_dot_scatter.5 = f32[2,128,2048]{2,1,0:T(8,128)} custom-call(bf16[2,8,128,768]{3,2,1,0:T(8,128)(2,1)} %bitcast.90, bf16[2048,768]{1,0:T(8,128)(2,1)} %bitcast.82), custom_call_target="tpu_custom_call" | custom-call | flops 990000000 | bytes 4500000 | tf_op jit(solution)/shard_map/plane_dot_scatter/pallas_call | solution.py:1156
  590.8 2.3 fusion.11
  593.1 0.1 reshape.249
  593.2 0.4 fusion.14
  593.7 1.0 broadcast_in_dim.32
  594.7 1.2 slice.41
  595.9 0.1 fusion.16
  596.0 0.7 copy.35
  596.7 3.2 fusion.7.g_ref
  599.9 5.1 reduce-scatter.8.cloned.1.call-done
  605.0 43.0 %finish.1 = (f32[8,128]{1,0:T(8,128)}, bf16[256,2048]{1,0:T(8,128)(2,1)}, f32[64,5120]{1,0:T(8,128)}, f32[64,5120]{1,0:T(8,128)}, f32[64,2048]{1,0:T(8,128)}, /*index=5*/f32[64,2048]{1,0:T(8,128)}, f32[64,2048]{1,0:T(8,128)}) custom-call(f32[32,8,128]{2,1,0:T(8,128)} %bitcast.106, bf16[256,2048]{1,0:T(8,128)(2,1)} %fusion.7.g_ref, ...), custom_call_target="tpu_custom_call" | custom-call | flops 990000000 | bytes 4500000 | tf_op jit(solution)/shard_map/finish/pallas_call | solution.py:1540
  648.0 1.4 fusion.24
  649.4 1.2 slice.43
  650.6 1.0 copy.47
  651.6 1.0 copy.48
  652.5 0.8 copy.49
  653.3 0.8 copy.50
  654.1 0.8 copy.51
  654.9 0.8 copy.52
  655.7 1.1 copy.53
  656.8 1.1 copy.54
  (54 shorter events, 0.3 us)
Async XLA Ops:
  7.2 208.9 %all-gather.4.cloned.1.call-start = ((), (), s32[]{:S(2)}) async-start(), calls=%async_computation.3 | async-start | bytes 1310720 | tf_op jit(solution)/shard_map/all_gather | solution.py:1612
  105.6 1.8 copy-start.13
  105.6 2.9 copy-start.1
  105.6 156.1 %all-gather.6.cloned.1.call-start = ((), (), s32[]{:S(2)}) async-start(), calls=%async_computation.4 | async-start | bytes 3276800 | tf_op jit(solution)/shard_map/all_gather | solution.py:1612
  106.4 2.4 copy-start.7
  106.4 199.8 %all-gather.8.cloned.1.call-start = ((), (), s32[]{:S(2)}) async-start(), calls=%async_computation.5 | async-start | bytes 6553600 | tf_op jit(solution)/shard_map/all_gather | solution.py:1633
  107.1 281.3 %reduce-scatter.4.cloned.1.call-start = ((), (), s32[]{:S(2)}) async-start(), calls=%async_computation.6 | async-start | bytes 3276800 | tf_op jit(solution)/shard_map/reduce_scatter | solution.py:1628
  108.4 2.1 copy-start.15
  110.5 59.1 %copy-start.17 = (s32[2047]{0:T(1024)S(1)}, s32[2047]{0:T(1024)}, u32[]{:S(2)}) copy-start(s32[2047]{0:T(1024)} %param.17) | copy-start | bytes 24568
  333.4 0.7 copy-start.16
  333.5 151.4 %reduce-scatter.6.cloned.1.call-start = ((), (), s32[]{:S(2)}) async-start(), calls=%async_computation.7 | async-start | bytes 6553600 | tf_op jit(solution)/shard_map/reduce_scatter | solution.py:1639
  388.4 216.6 %reduce-scatter.8.cloned.1.call-start = ((), (), s32[]{:S(2)}) async-start(), calls=%async_computation.8 | async-start | bytes 3932160 | tf_op jit(solution)/shard_map/reduce_scatter | solution.py:1639
  543.6 0.7 copy-start.18
  543.6 1.4 copy-start.8
  546.2 44.6 %copy-start.2 = (bf16[256,2048]{1,0:T(8,128)(2,1)S(1)}, bf16[256,2048]{1,0:T(8,128)(2,1)}, u32[]{:S(2)}) copy-start(bf16[256,2048]{1,0:T(8,128)(2,1)} %get-tuple-element.54) | copy-start | bytes 3145732
  590.8 2.4 copy-start.14
  590.8 5.9 copy-start
  599.9 50.6 %copy-start.5 = (bf16[256,2048]{1,0:T(8,128)(2,1)S(1)}, bf16[256,2048]{1,0:T(8,128)(2,1)}, u32[]{:S(2)}) copy-start(bf16[256,2048]{1,0:T(8,128)(2,1)} %get-tuple-element.78) | copy-start | bytes 3145732
  648.0 3.5 copy-start.6
  650.6 2.0 copy-start.12
  651.6 1.8 copy-start.11
  651.6 2.6 copy-start.10
  652.5 2.4 copy-start.9
  652.5 3.2 copy-start.4
  654.9 1.9 copy-start.3
Sparse Core Ops, SparseCore 0:
  105.7 45.3 all-gather.3
  152.7 53.6 all-gather.5
  208.0 96.3 all-gather.7
  333.6 54.7 reduce-scatter.3
  390.6 94.2 reduce-scatter.5
  543.7 61.2 reduce-scatter.7
